TPU v7x, 768 devices: a whole 4x8x12 slice. The times are simulated.
768 devices in a mesh: rep: 12 (over x, z_lo), shard: 64 (over z_hi, y, core).
Axes of the slice: x: 4, y: 8, z: 12 (z_hi: 4, z_lo: 3; z = z_hi * 3 + z_lo), core: 2. Of those that a mesh axis runs over, the one named last changes fastest.
Arguments:
- pooled: bfloat16 [98304, 1024], P(('rep', 'shard')), may hold values from -6 to 6
- layer_grad: bfloat16 [98304, 512], P(('rep', 'shard')), may hold values from -6 to 6
- dense_weight: bfloat16 [1024, 512], replicated, may hold values from -0.25 to 0.25
- bag_owner: int32 [1572864, 1], P(('rep', 'shard')), may hold values from 0 to 63; in each aligned block of 2048 rows (0 to 2047, 2048 to 4095, ...) at most 64 rows name the same one
- bag_slot: int32 [1572864], P(('rep', 'shard')), may hold values from 0 to 1535
- touched: int32 [98304], P('shard'), may hold values from 0 to 4095, as said below
- codes: bfloat16 [262144, 256], P('shard'), may hold values from 0 to 255, as said below
- row_scale: float32 [262144], P('shard'), may hold values from 0.002 to 0.02
- row_bias: float32 [262144], P('shard'), may hold values from -1 to 1
- accum: float32 [262144], P('shard'), may hold values from 1 to 100
Outputs:
- weight_grad: float32 [1024, 512], replicated
- new_codes: float32 [98304, 256], P('shard')
- new_scale: float32 [98304], P('shard')
- new_bias: float32 [98304], P('shard')
- new_accum: float32 [98304], P('shard')
Inputs may be any that keep to these rules, and one draw needn't show every extreme that they name: `bag_owner`: within the lookups of one device no shard is named more than 64 times. `touched`: each aligned block of 1536 entries lists distinct local rows of one shard, in shard order. `codes`: whole numbers.
All inputs are finite; a program needn't handle non-finite values.
Results may differ from a plain program's by a relative error of at most 0.00047.
Values may be sent and summed in bfloat16 or wider, within the bound.
No kernel may reach another device: no remote copies, remote signals or barrier semaphores. Data moves between devices by JAX's collectives and lax.ppermute only.
A program may use at most 32 MiB of HBM per device.

v0:
```python
import jax
import jax.numpy as jnp
from jax import lax
from jax.sharding import PartitionSpec as P


def update_rows(row_grad, local_rows, codes, row_scale, row_bias, accum):
    weights = (
        codes[local_rows].astype(jnp.float32) * row_scale[local_rows][:, None]
        + row_bias[local_rows][:, None]
    )
    new_accum = accum[local_rows] + jnp.mean(row_grad * row_grad, axis=1)
    updated = weights - 0.1 * row_grad / (jnp.sqrt(new_accum)[:, None] + 1e-06)
    lowest = jnp.min(updated, axis=1)
    highest = jnp.max(updated, axis=1)
    new_scale = (highest - lowest) / 255.0
    new_codes = (updated - lowest[:, None]) / new_scale[:, None]
    return (new_codes, new_scale, lowest, new_accum)


def dense_part(pooled, layer_grad):
    partial_grad = lax.dot_general(
        pooled, layer_grad, (((0,), (0,)), ((), ())), preferred_element_type=jnp.float32
    )
    return lax.psum(partial_grad, ("rep", "shard"))


def shards(
    pooled,
    layer_grad,
    dense_weight,
    bag_owner,
    bag_slot,
    touched,
    codes,
    row_scale,
    row_bias,
    accum,
):
    groups = lax.axis_size("shard")
    width = codes.shape[1]
    touch = touched.shape[0]
    lookups = bag_owner.shape[0]
    capacity = 2 * lookups // groups
    per_bag = lookups // (pooled.shape[0] * (pooled.shape[1] // width))
    pooled_grad = lax.dot_general(
        layer_grad, dense_weight, (((1,), (1,)), ((), ())), preferred_element_type=jnp.float32
    ).astype(jnp.bfloat16)
    lookup_rows = jnp.repeat(pooled_grad.reshape(-1, width), per_bag, axis=0)
    owners = bag_owner[:, 0]
    member = (owners[:, None] == jnp.arange(groups, dtype=jnp.int32)[None, :]).astype(jnp.int32)
    position = jnp.sum(jnp.cumsum(member, axis=0) * member, axis=1) - 1
    target = owners * capacity + position
    send_rows = jnp.zeros((groups * capacity, width), jnp.bfloat16).at[target].set(lookup_rows)
    send_slots = jnp.full((groups * capacity,), touch, jnp.int32).at[target].set(bag_slot)
    got_rows, got_slots = (
        lax.all_to_all(
            send_rows.reshape(groups, capacity, width),
            "shard",
            split_axis=0,
            concat_axis=0,
            tiled=True,
        ),
        lax.all_to_all(
            send_slots.reshape(groups, capacity), "shard", split_axis=0, concat_axis=0, tiled=True
        ),
    )
    selector = (jnp.arange(touch, dtype=jnp.int32)[:, None] == got_slots.reshape(1, -1)).astype(
        jnp.bfloat16
    )
    local_grad = jnp.dot(selector, got_rows.reshape(-1, width), preferred_element_type=jnp.float32)
    row_grad = lax.psum(local_grad, "rep")
    new_codes, new_scale, new_bias, new_accum = update_rows(
        row_grad, touched, codes, row_scale, row_bias, accum
    )
    weight_grad = dense_part(pooled, layer_grad)
    return (weight_grad, new_codes, new_scale, new_bias, new_accum)


def solution(mesh):
    in_specs = (
        P(("rep", "shard"), None),
        P(("rep", "shard"), None),
        P(),
        P(("rep", "shard"), None),
        P(("rep", "shard")),
        P("shard"),
        P("shard", None),
        P("shard"),
        P("shard"),
        P("shard"),
    )
    out_specs = (P(), P("shard", None), P("shard"), P("shard"), P("shard"))
    return jax.shard_map(shards, mesh=mesh, in_specs=in_specs, out_specs=out_specs, check_vma=False)
```

profile of v0, /device:TPU:1, one launch (start us, length us, event | category | flops | bytes accessed | tf_op | source)
XLA Modules:
  0.0 832.9 jit_solution(3734076188329177358)
XLA Ops:
  7.2 0.9 fusion.6
  8.1 18.1 %reduce-window.6 = s32[64,16,128]{2,1,0:T(8,128)S(1)} reduce-window(s32[64,16,128]{2,1,0:T(8,128)S(1)} %fusion.6, s32[]{:T(128)} %constant.13.clone.1), window={size=1x1x128 pad=0_0x0_0x127_0}, to_apply=%region_1.2 | reduce-window | flops 16646144 | bytes 1048580 | tf_op jit(solution)/shard_map/reduce-window
  26.2 0.2 slice.16
  26.4 0.4 copy.17
  27.0 0.2 broadcast_add_fusion
  27.5 8.2 scatter_custom_fusion
  35.7 0.7 all_to_all.9
  36.4 22.0 %all-to-all-start = ((s32[64,1,64]{2,1,0:T(1,128)}), s32[64,1,64]{2,1,0:T(1,128)}, u32[]{:S(2)}, u32[]{:S(2)}) async-start(s32[64,1,64]{2,1,0:T(1,128)} %all_to_all.9), calls=%async_computation | async-start | bytes 65536 | tf_op jit(solution)/shard_map/all_to_all | solution.py:64
  58.5 1.7 convolution_convert_fusion
  60.3 0.3 broadcast_in_dim.11
  60.6 1.1 reshape.121
  61.7 11.2 %scatter_custom_fusion.1 = bf16[4096,256]{1,0:T(8,128)(2,1)} fusion(s32[2048]{0:T(1024)S(1)} %bitcast.37, bf16[2048,256]{1,0:T(8,128)(2,1)} %reshape.121, bf16[]{:T(256)} %constant.7.clone.1), kind=kCustom, calls=%fused_computation.13 | custom fusion | bytes 2097664 | tf_op jit(solution)/shard_map/scatter | solution.py:54
  73.0 15.3 %all-to-all-start.1 = ((bf16[64,64,256]{2,1,0:T(8,128)(2,1)}), bf16[64,64,256]{2,1,0:T(8,128)(2,1)}, u32[]{:S(2)}, u32[]{:S(2)}) async-start(bf16[64,64,256]{2,1,0:T(8,128)(2,1)} %bitcast.29), calls=%async_computation.1 | async-start | bytes 4194304 | tf_op jit(solution)/shard_map/all_to_all | solution.py:57
  88.3 0.2 all-reduce.5.cloned.1.call-start
  88.5 0.5 broadcast.86
  89.0 1.5 reduce.3
  90.6 51.2 %all-to-all-done.1 = bf16[64,64,256]{2,1,0:T(8,128)(2,1)} async-done(((bf16[64,64,256]{2,1,0:T(8,128)(2,1)}), bf16[64,64,256]{2,1,0:T(8,128)(2,1)}, u32[]{:S(2)}, u32[]{:S(2)}) %all-to-all-start.1) | async-done | bytes 2097184 | tf_op jit(solution)/shard_map/all_to_all | solution.py:57
  141.8 7.3 fusion
  149.2 0.9 copy-done.6
  150.1 1.8 fusion.10
  151.9 0.7 copy-done.10
  152.6 8.4 %gather_fusion.3 = f32[1536]{0:T(1024)S(1)} fusion(f32[4096]{0:T(1024)S(1)} %copy-done.1, s32[2048]{0:T(1024)S(1)} %pad_clamp_fusion), kind=kCustom, calls=%fused_computation.3 | custom fusion | bytes 18432 | tf_op jit(solution)/shard_map/gather | solution.py:12
  161.0 8.4 %gather_fusion.2 = f32[1536]{0:T(1024)S(1)} fusion(f32[4096]{0:T(1024)S(1)} %copy-done.2, s32[2048]{0:T(1024)S(1)} %pad_clamp_fusion), kind=kCustom, calls=%fused_computation.2 | custom fusion | bytes 18432 | tf_op jit(solution)/shard_map/gather | solution.py:10
  169.4 8.4 %gather_fusion.1 = f32[1536]{0:T(1024)S(1)} fusion(f32[4096]{0:T(1024)S(1)} %copy-done.3, s32[2048]{0:T(1024)S(1)} %pad_clamp_fusion), kind=kCustom, calls=%fused_computation.1 | custom fusion | bytes 18432 | tf_op jit(solution)/shard_map/gather | solution.py:9
  177.8 4.8 gather_fusion
  182.6 143.2 %all-reduce.5.cloned.1.call-done = f32[1536,256]{1,0:T(8,128)} async-done(((f32[1536,256]{1,0:T(8,128)}), f32[1536,256]{1,0:T(8,128)}) %all-reduce.5.cloned.1.call-update) | async-done | bytes 1572880 | tf_op jit(solution)/shard_map/psum | solution.py:72
  325.8 1.8 multiply_reduce_fusion
  327.6 0.6 sqrt_add_fusion
  328.2 1.5 fusion.9
  329.8 1.6 subtract_divide_fusion
  331.4 491.6 %all-reduce.3.cloned.1.call-done = f32[1024,512]{1,0:T(8,128)} async-done(((f32[1024,512]{1,0:T(8,128)}), f32[1024,512]{1,0:T(8,128)}) %all-reduce.3.cloned.1.call-update) | async-done | bytes 2097168 | tf_op jit(solution)/shard_map/psum | solution.py:25
  823.0 3.1 copy.22
  (33 shorter events, 0.8 us)
Async XLA Ops:
  7.2 170.7 %copy-start = (bf16[4096,256]{1,0:T(8,128)(2,1)S(1)}, bf16[4096,256]{1,0:T(8,128)(2,1)}, u32[]{:S(2)}) copy-start(bf16[4096,256]{1,0:T(8,128)(2,1)} %param.16) | copy-start | bytes 6291460
  26.2 1.1 copy-start.7
  26.2 32.2 %copy-start.5 = (bf16[128,512]{1,0:T(8,128)(2,1)S(1)}, bf16[128,512]{1,0:T(8,128)(2,1)}, u32[]{:S(2)}) copy-start(bf16[128,512]{1,0:T(8,128)(2,1)} %param.11) | copy-start | bytes 393220
  36.4 36.6 %all-to-all-start = ((s32[64,1,64]{2,1,0:T(1,128)}), s32[64,1,64]{2,1,0:T(1,128)}, u32[]{:S(2)}, u32[]{:S(2)}) async-start(s32[64,1,64]{2,1,0:T(1,128)} %all_to_all.9), calls=%async_computation | async-start | bytes 65536 | tf_op jit(solution)/shard_map/all_to_all | solution.py:64
  73.0 68.9 %all-to-all-start.1 = ((bf16[64,64,256]{2,1,0:T(8,128)(2,1)}), bf16[64,64,256]{2,1,0:T(8,128)(2,1)}, u32[]{:S(2)}, u32[]{:S(2)}) async-start(bf16[64,64,256]{2,1,0:T(8,128)(2,1)} %bitcast.29), calls=%async_computation.1 | async-start | bytes 4194304 | tf_op jit(solution)/shard_map/all_to_all | solution.py:57
  88.3 237.5 %all-reduce.5.cloned.1.call-start = ((), (), s32[]{:S(2)}) async-start(), calls=%async_computation.3 | async-start | bytes 3145728 | tf_op jit(solution)/shard_map/psum | solution.py:72
  149.1 0.9 copy-start.6
  149.2 673.9 %all-reduce.3.cloned.1.call-start = ((), (), s32[]{:S(2)}) async-start(), calls=%async_computation.2 | async-start | bytes 4194304 | tf_op jit(solution)/shard_map/psum | solution.py:25
  151.9 0.7 copy-start.10
  151.9 0.7 copy-start.1
  152.6 8.4 %copy-start.2 = (f32[4096]{0:T(1024)S(1)}, f32[4096]{0:T(1024)}, u32[]{:S(2)}) copy-start(f32[4096]{0:T(1024)} %param.18) | copy-start | bytes 49156
  161.0 8.4 %copy-start.3 = (f32[4096]{0:T(1024)S(1)}, f32[4096]{0:T(1024)}, u32[]{:S(2)}) copy-start(f32[4096]{0:T(1024)} %param.17) | copy-start | bytes 49156
  325.8 2.4 copy-start.4
  329.8 1.7 copy-start.8
  329.8 1.6 copy-start.9
Sparse Core Ops, SparseCore 0:
  149.3 176.4 all-reduce.4
  331.8 491.1 all-reduce.2
where the time goes:
time: 835 us; the launch traced here: 833 us
  waiting for transfers between devices  686 us (82%)
  local copies, waits for them, and re-layouts  57.5 us (7%)
  starting transfers between devices  37.6 us (5%)
  other arithmetic  26.7 us (3%)
  between operations  14.3 us (2%)
  matrix products  10.8 us (1%)
    psum x1, waiting for transfers between devices, dense_part(): return lax.psum(partial_grad, ('rep', 'shard'))  492 us
    psum x1, waiting for transfers between devices, shards(): row_grad = lax.psum(local_grad, 'rep')  143 us
    all_to_all x1, waiting for transfers between devices, shards(): lax.all_to_all(send_rows.reshape(groups, capacity, width), 'shard', split...  51.2 us
    all_to_all x1, starting transfers between devices, shards(): lax.all_to_all(send_slots.reshape(groups, capacity), 'shard', split_axis=...  22 us
    another operation x3, other arithmetic  18.5 us
  transfers between devices with their start and end apart: 4, of which 3 were waited for; matrix products, arithmetic and copies ran while one was open for 6% of the time, Pallas kernels for 0%

commit v1 on v0

v1 whole, which is shorter than its diff:
```python
import jax
import jax.numpy as jnp
from jax import lax
from jax.experimental import pallas as pl
from jax.experimental.pallas import tpu as pltpu
from jax.sharding import Mesh, PartitionSpec as P

f32, bf16, i32 = jnp.float32, jnp.bfloat16, jnp.int32
NX, NZL, NZH, NY, NC = 4, 3, 4, 8, 2
AXES = ("x", "zl", "zh", "y", "c")
REP = ("x", "zl")
SHARD = ("zh", "y", "c")
NT = (((1,), (1,)), ((), ()))


def dispatch_kernel(groups, cap, lg_ref, w_ref, owner_ref, slot_ref, rows_ref, slots_ref, g_ref):
    per_bag, bags = owner_ref.shape
    samples = lg_ref.shape[0]
    width = rows_ref.shape[1]
    lg = lg_ref[...]
    for f in range(bags // samples):
        block = lax.dot_general(lg, w_ref[f * width : (f + 1) * width, :], NT, preferred_element_type=f32)
        g_ref[f * samples : (f + 1) * samples, :] = block.astype(bf16)
    owner, slot = owner_ref[...], slot_ref[...] + 1
    group = lax.broadcasted_iota(i32, (groups, bags), 0)
    earlier = lax.broadcasted_iota(i32, (bags, bags), 0) < lax.broadcasted_iota(i32, (bags, bags), 1)
    earlier = jnp.where(earlier, 1.0, 0.0).astype(bf16)
    base = jnp.zeros((groups, 1), f32)
    packed = jnp.zeros((2 * groups, cap), f32)
    targets = []
    for j in range(per_bag):
        own = owner[j : j + 1, :]
        member = jnp.where(own == group, 1.0, 0.0)
        prefix = jnp.dot(member.astype(bf16), earlier, preferred_element_type=f32) + base
        pos = jnp.sum(member * prefix, axis=0, keepdims=True)
        base = base + jnp.sum(member, axis=1, keepdims=True)
        pos = pos.astype(i32)
        targets.append(own * cap + pos)
        place = jnp.where(pos == lax.broadcasted_iota(i32, (cap, bags), 0), 1.0, 0.0).astype(bf16)
        high = (slot[j : j + 1, :] >> 5).astype(f32)
        low = (slot[j : j + 1, :] & 31).astype(f32)
        parts = jnp.concatenate([member * high, member * low], axis=0).astype(bf16)
        packed = packed + lax.dot_general(parts, place, NT, preferred_element_type=f32)
    slots_ref[...] = (packed[:groups] * 32.0 + packed[groups:]).astype(i32) - 1
    chunk = 256
    line = lax.broadcasted_iota(i32, (chunk, bags), 0)

    def step(i, carry):
        start = pl.multiple_of(i * chunk, chunk)
        hit = (targets[0] - start) == line
        for j in range(1, per_bag):
            hit = hit | ((targets[j] - start) == line)
        pick = jnp.where(hit, 1.0, 0.0).astype(bf16)
        out = jnp.dot(pick, g_ref[...], preferred_element_type=f32)
        rows_ref[pl.ds(start, chunk), :] = out.astype(bf16)
        return carry

    lax.fori_loop(0, groups * cap // chunk, step, 0)


def dispatch(layer_grad, dense_weight, bag_owner, bag_slot, width, groups, cap):
    samples = layer_grad.shape[0]
    features = dense_weight.shape[0] // width
    bags = samples * features
    per_bag = bag_slot.shape[0] // bags

    def lay(a):
        return a.reshape(samples, features, per_bag).transpose(2, 1, 0).reshape(per_bag, bags)

    vmem = pl.BlockSpec(memory_space=pltpu.VMEM)
    return pl.pallas_call(
        lambda *refs: dispatch_kernel(groups, cap, *refs),
        out_shape=(
            jax.ShapeDtypeStruct((groups * cap, width), bf16),
            jax.ShapeDtypeStruct((groups, cap), i32),
        ),
        in_specs=[vmem] * 4,
        out_specs=(vmem, vmem),
        scratch_shapes=[pltpu.VMEM((bags, width), bf16)],
        compiler_params=pltpu.CompilerParams(vmem_limit_bytes=32 << 20),
        name="dispatch",
    )(layer_grad, dense_weight, lay(bag_owner), lay(bag_slot))


def shift(a, axis, size, k):
    return lax.ppermute(a, axis, [(i, (i + k) % size) for i in range(size)])


def scatter_sum(a, axis, size):
    me = lax.axis_index(axis)
    n = a.shape[0] // size

    def block(k):
        return lax.dynamic_slice_in_dim(a, lax.rem(me + k, size) * n, n, 0)

    got = [shift(block(k), axis, size, k) for k in range(1, size)]
    total = block(0)
    for g in got:
        total = total + g
    return total


def gather(a, axis, size):
    me = lax.axis_index(axis)
    n = a.shape[0]
    out = jnp.zeros((size * n,) + a.shape[1:], a.dtype)
    for k in range(size):
        piece = a if k == 0 else shift(a, axis, size, k)
        out = lax.dynamic_update_slice_in_dim(out, piece, lax.rem(me - k + size, size) * n, 0)
    return out


def reduce_weight(a):
    rows, columns = a.shape
    a = scatter_sum(a, "c", NC)
    a = scatter_sum(a, "x", NX)
    n = a.shape[0]
    a = a.reshape(NY, n // NY, NZH, columns // NZH).transpose(0, 2, 1, 3).reshape(NY * NZH, n // NY, columns // NZH)
    a = jnp.sum(lax.all_to_all(a, ("zh", "y"), 0, 0, tiled=True), axis=0)
    a = jnp.sum(gather(a[None], "zl", NZL), axis=0)
    a = jnp.broadcast_to(a[None], (NY * NZH,) + a.shape)
    a = lax.all_to_all(a, ("zh", "y"), 0, 0, tiled=True)
    a = a.reshape(NY, NZH, n // NY, columns // NZH).transpose(0, 2, 1, 3).reshape(n, columns)
    a = gather(a, "x", NX)
    return gather(a, "c", NC)


def shards(pooled, layer_grad, dense_weight, bag_owner, bag_slot, touched, codes, row_scale, row_bias, accum):
    groups = NZH * NY * NC
    width = codes.shape[1]
    touch = touched.shape[0]
    cap = 2 * bag_slot.shape[0] // groups
    partial_grad = lax.dot_general(pooled, layer_grad, (((0,), (0,)), ((), ())), preferred_element_type=f32)
    rows, slots = dispatch(layer_grad, dense_weight, bag_owner, bag_slot, width, groups, cap)
    slots = lax.all_to_all(slots, SHARD, 0, 0, tiled=True)
    rows = lax.all_to_all(rows.reshape(groups, cap, width), SHARD, 0, 0, tiled=True)
    weight_grad = reduce_weight(partial_grad)

    part = touch // (NX * NZL)
    mine = lax.axis_index("x") * NZL + lax.axis_index("zl")
    local = lax.dynamic_slice_in_dim(touched, mine * part, part, 0)
    old = codes[local].astype(f32) * row_scale[local][:, None] + row_bias[local][:, None]
    old_accum = accum[local]

    selector = (jnp.arange(touch, dtype=i32)[:, None] == slots.reshape(1, -1)).astype(bf16)
    total = jnp.dot(selector, rows.reshape(-1, width), preferred_element_type=f32)
    total = scatter_sum(total, "x", NX)
    total = scatter_sum(total, "zl", NZL)

    new_accum = old_accum + jnp.mean(total * total, axis=1)
    updated = old - 0.1 * total / (jnp.sqrt(new_accum)[:, None] + 1e-06)
    lowest = jnp.min(updated, axis=1)
    highest = jnp.max(updated, axis=1)
    new_scale = (highest - lowest) / 255.0
    new_codes = (updated - lowest[:, None]) / new_scale[:, None]
    small = jnp.concatenate([new_scale, lowest, new_accum, jnp.zeros((8 * width - 3 * part,), f32)])
    payload = jnp.concatenate([new_codes, small.reshape(8, width)], axis=0)
    payload = gather(gather(payload, "zl", NZL), "x", NX)
    payload = payload.reshape(NX * NZL, part + 8, width)
    new_codes = payload[:, :part].reshape(touch, width)
    small = payload[:, part:].reshape(NX * NZL, 8 * width)
    new_scale, lowest, new_accum = (small[:, i * part : (i + 1) * part].reshape(touch) for i in range(3))
    return (weight_grad, new_codes, new_scale, lowest, new_accum)


def solution(mesh):
    mesh = Mesh(mesh.devices.reshape(NX, NZL, NZH, NY, NC), AXES)
    in_specs = (
        P(AXES, None),
        P(AXES, None),
        P(),
        P(AXES, None),
        P(AXES),
        P(SHARD),
        P(SHARD, None),
        P(SHARD),
        P(SHARD),
        P(SHARD),
    )
    out_specs = (P(), P(SHARD, None), P(SHARD), P(SHARD), P(SHARD))
    return jax.shard_map(shards, mesh=mesh, in_specs=in_specs, out_specs=out_specs, check_vma=False)
```

time: 835 us -> 307 us (0.37)
  the two profiles are of different devices: /device:TPU:1 before, /device:TPU:203 now
where the time goes in v1:
time: 307 us; the launch traced here: 306 us
  starting transfers between devices  125 us (41%)
  waiting for transfers between devices  102 us (33%)
  local copies, waits for them, and re-layouts  29.6 us (10%)
  blocking collectives  23 us (7%)
  other arithmetic  8.52 us (3%)
  matrix products  7.78 us (3%)
  Pallas kernels  7.52 us (2%)
    ppermute x20, starting transfers between devices, shift(): return lax.ppermute(a, axis, [(i, (i + k) % size) for i in range(size)])  79.2 us
    all_to_all x1, waiting for transfers between devices, shards(): lax.all_to_all(rows.reshape(groups, cap, width), SHARD, 0, 0, tiled=True)  64.6 us
    ppermute x20, waiting for transfers between devices, shift(): return lax.ppermute(a, axis, [(i, (i + k) % size) for i in range(size)])  37.8 us
    all_to_all x1, blocking collectives, reduce_weight(): a = lax.all_to_all(a, ('zh', 'y'), 0, 0, tiled=True)  23 us
    all_to_all x1, starting transfers between devices, reduce_weight(): a = jnp.sum(lax.all_to_all(a, ('zh', 'y'), 0, 0, tiled=True), axis=0)  17.1 us
    all_to_all x1, starting transfers between devices, shards(): slots = lax.all_to_all(slots, SHARD, 0, 0, tiled=True)  15.7 us
    all_to_all x1, starting transfers between devices, shards(): lax.all_to_all(rows.reshape(groups, cap, width), SHARD, 0, 0, tiled=True)  13.2 us
    pallas_call x1, Pallas kernels, dispatch(): pl.pallas_call(lambda *refs: dispatch_kernel(groups, cap, *refs), out_sha...  7.52 us
  transfers between devices with their start and end apart: 23, of which 12 were waited for; matrix products, arithmetic and copies ran while one was open for 10% of the time, Pallas kernels for 2%

profile of v1, /device:TPU:203, one launch (start us, length us, event | category | flops | bytes accessed | tf_op | source)
XLA Modules:
  0.0 305.6 jit_solution(15899587979698097028)
XLA Ops:
  3.6 2.6 collective-permute-start
  6.3 2.4 collective-permute-done
  12.2 3.2 %collective-permute-start.1 = (f32[128,512]{1,0:T(8,128)}, f32[128,512]{1,0:T(8,128)S(1)}, u32[]{:S(2)}, u32[]{:S(2)}) collective-permute-start(f32[128,512]{1,0:T(8,128)} %get-tuple-element.19), channel_id=1, source_target_pairs={{0,192},{192,384},{384,576},{576,0},{1,193},{193,385},{385,577},{5... | collective-permute-start | bytes 786440 | tf_op jit(solution)/shard_map/ppermute | solution.py:86
  15.5 2.7 collective-permute-start.2
  18.2 3.8 %collective-permute-start.3 = (f32[128,512]{1,0:T(8,128)}, f32[128,512]{1,0:T(8,128)}, u32[]{:S(2)}, u32[]{:S(2)}) collective-permute-start(f32[128,512]{1,0:T(8,128)} %get-tuple-element.20), channel_id=1, source_target_pairs={{0,576},{192,0},{384,192},{576,384},{1,577},{193,1},{385,193},{577... | collective-permute-start | bytes 786440 | tf_op jit(solution)/shard_map/ppermute | solution.py:86
  22.1 4.4 %collective-permute-done.2 = f32[128,512]{1,0:T(8,128)} collective-permute-done((f32[128,512]{1,0:T(8,128)}, f32[128,512]{1,0:T(8,128)}, u32[]{:S(2)}, u32[]{:S(2)}) %collective-permute-start.2) | collective-permute-done | bytes 262176 | tf_op jit(solution)/shard_map/ppermute | solution.py:86
  26.4 6.6 %collective-permute-done.3 = f32[128,512]{1,0:T(8,128)} collective-permute-done((f32[128,512]{1,0:T(8,128)}, f32[128,512]{1,0:T(8,128)}, u32[]{:S(2)}, u32[]{:S(2)}) %collective-permute-start.3) | collective-permute-done | bytes 262176 | tf_op jit(solution)/shard_map/ppermute | solution.py:86
  36.8 17.1 %all-to-all-start = ((f32[32,16,128]{2,1,0:T(8,128)}), f32[32,16,128]{2,1,0:T(8,128)S(1)}, u32[]{:S(2)}, u32[]{:S(2)}) async-start(f32[32,16,128]{2,1,0:T(8,128)} %bitcast.49), calls=%async_computation | async-start | bytes 524288 | tf_op jit(solution)/shard_map/all_to_all | solution.py:119
  60.1 7.5 %dispatch.1 = (bf16[4096,256]{1,0:T(8,128)(2,1)S(1)}, s32[64,64]{1,0:T(8,128)}) custom-call(bf16[128,512]{1,0:T(8,128)(2,1)S(1)} %copy-done.3, bf16[1024,512]{1,0:T(8,128)(2,1)S(1)} %copy-done.2, s32[4,512]{1,0:T(4,128)S(1)} %get-tuple-element.30.refs_2_, s32[4,512]{1,0:T(4,128)S(1)} %get-tuple-element.29.refs_3_), custom_call_target="tpu_custom_call" | custom-call | tf_op jit(solution)/shard_map/dispatch/pallas_call | solution.py:71
  68.9 15.7 %all-to-all-start.2 = ((s32[64,1,64]{2,1,0:T(1,128)}), s32[64,1,64]{2,1,0:T(1,128)S(1)}, u32[]{:S(2)}, u32[]{:S(2)}) async-start(s32[64,1,64]{2,1,0:T(1,128)} %bitcast.8), calls=%async_computation.2 | async-start | bytes 65536 | tf_op jit(solution)/shard_map/all_to_all | solution.py:135
  84.7 4.3 %collective-permute-start.4 = (f32[1,16,128]{2,1,0:T(8,128)S(1)}, f32[1,16,128]{2,1,0:T(8,128)S(1)}, u32[]{:S(2)}, u32[]{:S(2)}) collective-permute-start(f32[1,16,128]{2,1,0:T(8,128)S(1)} %bitcast.55), channel_id=1, source_target_pairs={{0,64},{64,128},{128,0},{1,65},{65,129},{129,1},{2,66},{66,130},{1... | collective-permute-start | bytes 24584 | tf_op jit(solution)/shard_map/ppermute | solution.py:86
  89.0 3.1 %collective-permute-start.5 = (f32[1,16,128]{2,1,0:T(8,128)S(1)}, f32[1,16,128]{2,1,0:T(8,128)S(1)}, u32[]{:S(2)}, u32[]{:S(2)}) collective-permute-start(f32[1,16,128]{2,1,0:T(8,128)S(1)} %bitcast.56), channel_id=1, source_target_pairs={{0,128},{64,0},{128,64},{1,129},{65,1},{129,65},{2,130},{66,2},{13... | collective-permute-start | bytes 24584 | tf_op jit(solution)/shard_map/ppermute | solution.py:86
  92.1 2.8 collective-permute-done.5
  95.0 23.0 %all_to_all.24 = f32[32,16,128]{2,1,0:T(8,128)S(1)} all-to-all(f32[32,16,128]{2,1,0:T(8,128)S(1)} %broadcast_in_dim.43), channel_id=1, replica_groups=mesh['x'=4,'zl'=3,'zh'=4,'y'=8,'c'=2] {'zh','y'}, dimensions={0} | all-to-all | bytes 524288 | tf_op jit(solution)/shard_map/all_to_all | solution.py:122
  118.0 13.2 %all-to-all-start.3 = ((bf16[64,64,256]{2,1,0:T(8,128)(2,1)}), bf16[64,64,256]{2,1,0:T(8,128)(2,1)}, u32[]{:S(2)}, u32[]{:S(2)}) async-start(bf16[64,64,256]{2,1,0:T(8,128)(2,1)} %bitcast.43), calls=%async_computation.3 | async-start | bytes 4194304 | tf_op jit(solution)/shard_map/all_to_all | solution.py:136
  133.7 2.2 collective-permute-start.6
  135.9 64.6 %all-to-all-done.3 = bf16[64,64,256]{2,1,0:T(8,128)(2,1)} async-done(((bf16[64,64,256]{2,1,0:T(8,128)(2,1)}), bf16[64,64,256]{2,1,0:T(8,128)(2,1)}, u32[]{:S(2)}, u32[]{:S(2)}) %all-to-all-start.3) | async-done | bytes 2097184 | tf_op jit(solution)/shard_map/all_to_all | solution.py:136
  200.5 6.2 %fusion = f32[1536,256]{1,0:T(8,128)S(1)} fusion(bf16[4096,256]{1,0:T(8,128)(2,1)} %bitcast.10, s32[4096]{0:T(1024)S(1)} %eq.16), kind=kOutput, calls=%fused_computation.5 | convolution fusion | flops 3227516928 | bytes 3686400 | tf_op jit(solution)/shard_map/dot_general | solution.py:146
  208.9 2.3 collective-permute-start.10
  211.2 4.4 %collective-permute-start.11 = (f32[384,256]{1,0:T(8,128)}, f32[384,256]{1,0:T(8,128)}, u32[]{:S(2)}, u32[]{:S(2)}) collective-permute-start(f32[384,256]{1,0:T(8,128)} %get-tuple-element.18), channel_id=1, source_target_pairs={{0,384},{192,576},{384,0},{576,192},{1,385},{193,577},{385,1},{577... | collective-permute-start | bytes 1179656 | tf_op jit(solution)/shard_map/ppermute | solution.py:86
  222.2 2.6 collective-permute-start.7
  225.0 4.3 %collective-permute-start.8 = (f32[128,512]{1,0:T(8,128)}, f32[128,512]{1,0:T(8,128)S(1)}, u32[]{:S(2)}, u32[]{:S(2)}) collective-permute-start(f32[128,512]{1,0:T(8,128)} %bitcast.42), channel_id=1, source_target_pairs={{0,576},{192,0},{384,192},{576,384},{1,577},{193,1},{385,193},{577... | collective-permute-start | bytes 786440 | tf_op jit(solution)/shard_map/ppermute | solution.py:86
  231.8 20.9 %collective-permute-start.13 = (f32[128,256]{1,0:T(8,128)S(1)}, f32[128,256]{1,0:T(8,128)S(1)}, u32[]{:S(2)}, u32[]{:S(2)}) collective-permute-start(f32[128,256]{1,0:T(8,128)S(1)} %get-tuple-element.22), channel_id=1, source_target_pairs={{0,64},{64,128},{128,0},{1,65},{65,129},{129,1},{2,66},{66,130},{1... | collective-permute-start | bytes 393224 | tf_op jit(solution)/shard_map/ppermute | solution.py:86
  254.7 2.6 collective-permute-start.9
  257.3 2.8 collective-permute-done.14
  262.2 4.5 %collective-permute-start.15 = (f32[136,256]{1,0:T(8,128)S(1)}, f32[136,256]{1,0:T(8,128)}, u32[]{:S(2)}, u32[]{:S(2)}) collective-permute-start(f32[136,256]{1,0:T(8,128)S(1)} %get-tuple-element.24), channel_id=1, source_target_pairs={{0,64},{64,128},{128,0},{1,65},{65,129},{129,1},{2,66},{66,130},{1... | collective-permute-start | bytes 417800 | tf_op jit(solution)/shard_map/ppermute | solution.py:86
  266.7 2.8 collective-permute-start.16
  271.7 4.0 %collective-permute-done.16 = f32[136,256]{1,0:T(8,128)S(1)} collective-permute-done((f32[136,256]{1,0:T(8,128)S(1)}, f32[136,256]{1,0:T(8,128)S(1)}, u32[]{:S(2)}, u32[]{:S(2)}) %collective-permute-start.16) | collective-permute-done | bytes 139296 | tf_op jit(solution)/shard_map/ppermute | solution.py:86
  276.4 3.0 collective-permute-start.17
  281.7 3.7 %collective-permute-start.19 = (f32[408,256]{1,0:T(8,128)}, f32[408,256]{1,0:T(8,128)S(1)}, u32[]{:S(2)}, u32[]{:S(2)}) collective-permute-start(f32[408,256]{1,0:T(8,128)} %constant_dynamic-update-slice_fusion.4), channel_id=1, source_target_pairs={{0,576},{192,0},{384,192},{576,384},{1,577},{193,1},{385,193},{577... | collective-permute-start | bytes 1253384 | tf_op jit(solution)/shard_map/ppermute | solution.py:86
  290.0 3.1 %collective-permute-done.18 = f32[408,256]{1,0:T(8,128)S(1)} collective-permute-done((f32[408,256]{1,0:T(8,128)}, f32[408,256]{1,0:T(8,128)S(1)}, u32[]{:S(2)}, u32[]{:S(2)}) %collective-permute-start.18) | collective-permute-done | bytes 417824 | tf_op jit(solution)/shard_map/ppermute | solution.py:86
  293.1 10.5 %collective-permute-done.19 = f32[408,256]{1,0:T(8,128)S(1)} collective-permute-done((f32[408,256]{1,0:T(8,128)}, f32[408,256]{1,0:T(8,128)S(1)}, u32[]{:S(2)}, u32[]{:S(2)}) %collective-permute-start.19) | collective-permute-done | bytes 417824 | tf_op jit(solution)/shard_map/ppermute | solution.py:86
  (107 shorter events, 47.1 us)
Async XLA Ops:
  0.6 218.4 %copy-start = (bf16[4096,256]{1,0:T(8,128)(2,1)S(1)}, bf16[4096,256]{1,0:T(8,128)(2,1)}, u32[]{:S(2)}) copy-start(bf16[4096,256]{1,0:T(8,128)(2,1)} %param.16) | copy-start | bytes 6291460
  3.6 5.0 %collective-permute-start = (f32[512,512]{1,0:T(8,128)S(1)}, f32[512,512]{1,0:T(8,128)}, u32[]{:S(2)}, u32[]{:S(2)}) collective-permute-start(f32[512,512]{1,0:T(8,128)S(1)} %constant_dynamic-slice_fusion.8), channel_id=1, source_target_pairs={{0,1},{1,0},{2,3},{3,2},{4,5},{5,4},{6,7},{7,6},{8,9},{9,8},{10,11... | collective-permute-start | bytes 3145736 | tf_op jit(solution)/shard_map/ppermute | solution.py:86
  12.2 45.7 %copy-start.12 = (s32[2048]{0:T(1024)S(1)}, s32[2048]{0:T(1024)}, u32[]{:S(2)}) copy-start(s32[2048]{0:T(1024)} %param.14) | copy-start | bytes 24580
  12.2 47.8 %copy-start.2 = (bf16[1024,512]{1,0:T(8,128)(2,1)S(1)}, bf16[1024,512]{1,0:T(8,128)(2,1)}, u32[]{:S(2)}) copy-start(bf16[1024,512]{1,0:T(8,128)(2,1)} %refs_1_.1) | copy-start | bytes 3145732
  12.2 47.8 %copy-start.3 = (bf16[128,512]{1,0:T(8,128)(2,1)S(1)}, bf16[128,512]{1,0:T(8,128)(2,1)}, u32[]{:S(2)}) copy-start(bf16[128,512]{1,0:T(8,128)(2,1)} %refs_0_.1) | copy-start | bytes 393220
  12.2 9.8 %collective-permute-start.1 = (f32[128,512]{1,0:T(8,128)}, f32[128,512]{1,0:T(8,128)S(1)}, u32[]{:S(2)}, u32[]{:S(2)}) collective-permute-start(f32[128,512]{1,0:T(8,128)} %get-tuple-element.19), channel_id=1, source_target_pairs={{0,192},{192,384},{384,576},{576,0},{1,193},{193,385},{385,577},{5... | collective-permute-start | bytes 786440 | tf_op jit(solution)/shard_map/ppermute | solution.py:86
  15.5 11.0 %collective-permute-start.2 = (f32[128,512]{1,0:T(8,128)}, f32[128,512]{1,0:T(8,128)}, u32[]{:S(2)}, u32[]{:S(2)}) collective-permute-start(f32[128,512]{1,0:T(8,128)} %get-tuple-element.21), channel_id=1, source_target_pairs={{0,384},{192,576},{384,0},{576,192},{1,385},{193,577},{385,1},{577... | collective-permute-start | bytes 786440 | tf_op jit(solution)/shard_map/ppermute | solution.py:86
  18.2 14.8 %collective-permute-start.3 = (f32[128,512]{1,0:T(8,128)}, f32[128,512]{1,0:T(8,128)}, u32[]{:S(2)}, u32[]{:S(2)}) collective-permute-start(f32[128,512]{1,0:T(8,128)} %get-tuple-element.20), channel_id=1, source_target_pairs={{0,576},{192,0},{384,192},{576,384},{1,577},{193,1},{385,193},{577... | collective-permute-start | bytes 786440 | tf_op jit(solution)/shard_map/ppermute | solution.py:86
  22.0 4.4 %copy-start.11 = (f32[128,512]{1,0:T(8,128)}, f32[128,512]{1,0:T(8,128)S(1)}, u32[]{:S(2)}) copy-start(f32[128,512]{1,0:T(8,128)S(1)} %collective-permute-done.1) | copy-start | bytes 786436
  36.8 32.1 %all-to-all-start = ((f32[32,16,128]{2,1,0:T(8,128)}), f32[32,16,128]{2,1,0:T(8,128)S(1)}, u32[]{:S(2)}, u32[]{:S(2)}) async-start(f32[32,16,128]{2,1,0:T(8,128)} %bitcast.49), calls=%async_computation | async-start | bytes 524288 | tf_op jit(solution)/shard_map/all_to_all | solution.py:119
  68.9 26.1 %all-to-all-start.2 = ((s32[64,1,64]{2,1,0:T(1,128)}), s32[64,1,64]{2,1,0:T(1,128)S(1)}, u32[]{:S(2)}, u32[]{:S(2)}) async-start(s32[64,1,64]{2,1,0:T(1,128)} %bitcast.8), calls=%async_computation.2 | async-start | bytes 65536 | tf_op jit(solution)/shard_map/all_to_all | solution.py:135
  84.7 7.4 %collective-permute-start.4 = (f32[1,16,128]{2,1,0:T(8,128)S(1)}, f32[1,16,128]{2,1,0:T(8,128)S(1)}, u32[]{:S(2)}, u32[]{:S(2)}) collective-permute-start(f32[1,16,128]{2,1,0:T(8,128)S(1)} %bitcast.55), channel_id=1, source_target_pairs={{0,64},{64,128},{128,0},{1,65},{65,129},{129,1},{2,66},{66,130},{1... | collective-permute-start | bytes 24584 | tf_op jit(solution)/shard_map/ppermute | solution.py:86
  89.0 5.9 %collective-permute-start.5 = (f32[1,16,128]{2,1,0:T(8,128)S(1)}, f32[1,16,128]{2,1,0:T(8,128)S(1)}, u32[]{:S(2)}, u32[]{:S(2)}) collective-permute-start(f32[1,16,128]{2,1,0:T(8,128)S(1)} %bitcast.56), channel_id=1, source_target_pairs={{0,128},{64,0},{128,64},{1,129},{65,1},{129,65},{2,130},{66,2},{13... | collective-permute-start | bytes 24584 | tf_op jit(solution)/shard_map/ppermute | solution.py:86
  118.0 82.5 %all-to-all-start.3 = ((bf16[64,64,256]{2,1,0:T(8,128)(2,1)}), bf16[64,64,256]{2,1,0:T(8,128)(2,1)}, u32[]{:S(2)}, u32[]{:S(2)}) async-start(bf16[64,64,256]{2,1,0:T(8,128)(2,1)} %bitcast.43), calls=%async_computation.3 | async-start | bytes 4194304 | tf_op jit(solution)/shard_map/all_to_all | solution.py:136
  133.7 91.3 %collective-permute-start.6 = (f32[128,512]{1,0:T(8,128)}, f32[128,512]{1,0:T(8,128)}, u32[]{:S(2)}, u32[]{:S(2)}) collective-permute-start(f32[128,512]{1,0:T(8,128)} %bitcast.42), channel_id=1, source_target_pairs={{0,192},{192,384},{384,576},{576,0},{1,193},{193,385},{385,577},{5... | collective-permute-start | bytes 786440 | tf_op jit(solution)/shard_map/ppermute | solution.py:86
  207.8 10.0 %copy-start.4 = (f32[4096]{0:T(1024)S(1)}, f32[4096]{0:T(1024)}, u32[]{:S(2)}) copy-start(f32[4096]{0:T(1024)} %param.19) | copy-start | bytes 49156
  207.9 12.0 %copy-start.5 = (f32[4096]{0:T(1024)S(1)}, f32[4096]{0:T(1024)}, u32[]{:S(2)}) copy-start(f32[4096]{0:T(1024)} %param.17) | copy-start | bytes 49156
  207.9 13.2 %copy-start.6 = (f32[4096]{0:T(1024)S(1)}, f32[4096]{0:T(1024)}, u32[]{:S(2)}) copy-start(f32[4096]{0:T(1024)} %param.18) | copy-start | bytes 49156
  208.9 21.4 %collective-permute-start.10 = (f32[384,256]{1,0:T(8,128)}, f32[384,256]{1,0:T(8,128)}, u32[]{:S(2)}, u32[]{:S(2)}) collective-permute-start(f32[384,256]{1,0:T(8,128)} %get-tuple-element.16), channel_id=1, source_target_pairs={{0,192},{192,384},{384,576},{576,0},{1,193},{193,385},{385,577},{5... | collective-permute-start | bytes 1179656 | tf_op jit(solution)/shard_map/ppermute | solution.py:86
  211.2 19.0 %collective-permute-start.11 = (f32[384,256]{1,0:T(8,128)}, f32[384,256]{1,0:T(8,128)}, u32[]{:S(2)}, u32[]{:S(2)}) collective-permute-start(f32[384,256]{1,0:T(8,128)} %get-tuple-element.18), channel_id=1, source_target_pairs={{0,384},{192,576},{384,0},{576,192},{1,385},{193,577},{385,1},{577... | collective-permute-start | bytes 1179656 | tf_op jit(solution)/shard_map/ppermute | solution.py:86
  215.7 14.6 %collective-permute-start.12 = (f32[384,256]{1,0:T(8,128)}, f32[384,256]{1,0:T(8,128)}, u32[]{:S(2)}, u32[]{:S(2)}) collective-permute-start(f32[384,256]{1,0:T(8,128)} %get-tuple-element.17), channel_id=1, source_target_pairs={{0,576},{192,0},{384,192},{576,384},{1,577},{193,1},{385,193},{577... | collective-permute-start | bytes 1179656 | tf_op jit(solution)/shard_map/ppermute | solution.py:86
  222.2 32.4 %collective-permute-start.7 = (f32[128,512]{1,0:T(8,128)}, f32[128,512]{1,0:T(8,128)S(1)}, u32[]{:S(2)}, u32[]{:S(2)}) collective-permute-start(f32[128,512]{1,0:T(8,128)} %bitcast.42), channel_id=1, source_target_pairs={{0,384},{192,576},{384,0},{576,192},{1,385},{193,577},{385,1},{577... | collective-permute-start | bytes 786440 | tf_op jit(solution)/shard_map/ppermute | solution.py:86
  225.0 29.7 %collective-permute-start.8 = (f32[128,512]{1,0:T(8,128)}, f32[128,512]{1,0:T(8,128)S(1)}, u32[]{:S(2)}, u32[]{:S(2)}) collective-permute-start(f32[128,512]{1,0:T(8,128)} %bitcast.42), channel_id=1, source_target_pairs={{0,576},{192,0},{384,192},{576,384},{1,577},{193,1},{385,193},{577... | collective-permute-start | bytes 786440 | tf_op jit(solution)/shard_map/ppermute | solution.py:86
  231.8 25.5 %collective-permute-start.13 = (f32[128,256]{1,0:T(8,128)S(1)}, f32[128,256]{1,0:T(8,128)S(1)}, u32[]{:S(2)}, u32[]{:S(2)}) collective-permute-start(f32[128,256]{1,0:T(8,128)S(1)} %get-tuple-element.22), channel_id=1, source_target_pairs={{0,64},{64,128},{128,0},{1,65},{65,129},{129,1},{2,66},{66,130},{1... | collective-permute-start | bytes 393224 | tf_op jit(solution)/shard_map/ppermute | solution.py:86
  252.7 7.5 %collective-permute-start.14 = (f32[128,256]{1,0:T(8,128)S(1)}, f32[128,256]{1,0:T(8,128)S(1)}, u32[]{:S(2)}, u32[]{:S(2)}) collective-permute-start(f32[128,256]{1,0:T(8,128)S(1)} %get-tuple-element.23), channel_id=1, source_target_pairs={{0,128},{64,0},{128,64},{1,129},{65,1},{129,65},{2,130},{66,2},{13... | collective-permute-start | bytes 393224 | tf_op jit(solution)/shard_map/ppermute | solution.py:86
  254.7 30.7 %collective-permute-start.9 = (f32[512,512]{1,0:T(8,128)S(1)}, f32[512,512]{1,0:T(8,128)}, u32[]{:S(2)}, u32[]{:S(2)}) collective-permute-start(f32[512,512]{1,0:T(8,128)S(1)} %constant_dynamic-update-slice_fusion.9), channel_id=1, source_target_pairs={{0,1},{1,0},{2,3},{3,2},{4,5},{5,4},{6,7},{7,6},{8,9},{9,8},{10,11... | collective-permute-start | bytes 3145736 | tf_op jit(solution)/shard_map/ppermute | solution.py:86
  262.2 8.0 %collective-permute-start.15 = (f32[136,256]{1,0:T(8,128)S(1)}, f32[136,256]{1,0:T(8,128)}, u32[]{:S(2)}, u32[]{:S(2)}) collective-permute-start(f32[136,256]{1,0:T(8,128)S(1)} %get-tuple-element.24), channel_id=1, source_target_pairs={{0,64},{64,128},{128,0},{1,65},{65,129},{129,1},{2,66},{66,130},{1... | collective-permute-start | bytes 417800 | tf_op jit(solution)/shard_map/ppermute | solution.py:86
  266.7 9.0 %collective-permute-start.16 = (f32[136,256]{1,0:T(8,128)S(1)}, f32[136,256]{1,0:T(8,128)S(1)}, u32[]{:S(2)}, u32[]{:S(2)}) collective-permute-start(f32[136,256]{1,0:T(8,128)S(1)} %get-tuple-element.24), channel_id=1, source_target_pairs={{0,128},{64,0},{128,64},{1,129},{65,1},{129,65},{2,130},{66,2},{13... | collective-permute-start | bytes 417800 | tf_op jit(solution)/shard_map/ppermute | solution.py:86
  276.4 12.6 %collective-permute-start.17 = (f32[408,256]{1,0:T(8,128)}, f32[408,256]{1,0:T(8,128)}, u32[]{:S(2)}, u32[]{:S(2)}) collective-permute-start(f32[408,256]{1,0:T(8,128)} %constant_dynamic-update-slice_fusion.4), channel_id=1, source_target_pairs={{0,192},{192,384},{384,576},{576,0},{1,193},{193,385},{385,577},{5... | collective-permute-start | bytes 1253384 | tf_op jit(solution)/shard_map/ppermute | solution.py:86
  279.5 13.6 %collective-permute-start.18 = (f32[408,256]{1,0:T(8,128)}, f32[408,256]{1,0:T(8,128)S(1)}, u32[]{:S(2)}, u32[]{:S(2)}) collective-permute-start(f32[408,256]{1,0:T(8,128)} %constant_dynamic-update-slice_fusion.4), channel_id=1, source_target_pairs={{0,384},{192,576},{384,0},{576,192},{1,385},{193,577},{385,1},{577... | collective-permute-start | bytes 1253384 | tf_op jit(solution)/shard_map/ppermute | solution.py:86
  281.7 21.9 %collective-permute-start.19 = (f32[408,256]{1,0:T(8,128)}, f32[408,256]{1,0:T(8,128)S(1)}, u32[]{:S(2)}, u32[]{:S(2)}) collective-permute-start(f32[408,256]{1,0:T(8,128)} %constant_dynamic-update-slice_fusion.4), channel_id=1, source_target_pairs={{0,576},{192,0},{384,192},{576,384},{1,577},{193,1},{385,193},{577... | collective-permute-start | bytes 1253384 | tf_op jit(solution)/shard_map/ppermute | solution.py:86
  286.8 16.9 %copy-start.9 = (f32[1024,512]{1,0:T(8,128)}, f32[1024,512]{1,0:T(8,128)S(1)}, u32[]{:S(2)}) copy-start(f32[1024,512]{1,0:T(8,128)S(1)} %constant_dynamic-update-slice_fusion.7) | copy-start | bytes 6291460
  (4 other events, 4.8 us)

commit v2 on v1

v2 whole, which is shorter than its diff:
```python
import jax
import jax.numpy as jnp
from jax import lax
from jax.experimental import pallas as pl
from jax.experimental.pallas import tpu as pltpu
from jax.sharding import Mesh, PartitionSpec as P

f32, bf16, i32 = jnp.float32, jnp.bfloat16, jnp.int32
NX, NZL, NZH, NY, NC = 4, 3, 4, 8, 2
AXES = ("x", "zl", "zh", "y", "c")
REP = ("x", "zl")
SHARD = ("zh", "y", "c")
KEYS, EXTRA = 16, 16
NT = (((1,), (1,)), ((), ()))


def dispatch_kernel(here, cap, first_ref, own_ref, prev_ref, next_ref, far_ref, w_ref, out_ref, g_ref, slots_ref, aim_ref):
    samples = own_ref.shape[0]
    depth = w_ref.shape[1]
    width = out_ref.shape[2]
    features = w_ref.shape[0] // width
    bags = samples * features
    per_bag = KEYS // features
    sources = (own_ref, prev_ref, next_ref, far_ref)
    group = lax.broadcasted_iota(i32, (here, bags), 0)
    earlier = lax.broadcasted_iota(i32, (bags, bags), 0) < lax.broadcasted_iota(i32, (bags, bags), 1)
    earlier = jnp.where(earlier, 1.0, 0.0).astype(bf16)
    lane = lax.broadcasted_iota(i32, (len(sources) * cap, bags), 0)
    packed = jnp.zeros((2 * here, len(sources) * cap), f32)
    some = 4
    line = lax.broadcasted_iota(i32, (some * cap, bags), 0)
    for q, ref in enumerate(sources):
        lg = ref[:, :depth]
        for f in range(features):
            block = lax.dot_general(lg, w_ref[f * width : (f + 1) * width, :], NT, preferred_element_type=f32)
            g_ref[f * samples : (f + 1) * samples, :] = block.astype(bf16)
        keys = jnp.transpose(ref[:, depth:].astype(f32))

        def pick(kind, j):
            at = [kind * KEYS + f * per_bag + j for f in range(features)]
            return jnp.concatenate([keys[i : i + 1, :] for i in at], axis=1)

        owners = [pick(0, j).astype(i32) - first_ref[0] for j in range(per_bag)]
        members = [jnp.where(own == group, 1.0, 0.0) for own in owners]
        stacked = jnp.concatenate(members, axis=0).astype(bf16)
        prefix = jnp.dot(stacked, earlier, preferred_element_type=f32)
        base = jnp.zeros((here, 1), f32)
        for j in range(per_bag):
            member = members[j]
            pos = jnp.sum(member * (prefix[j * here : (j + 1) * here] + base), axis=0, keepdims=True).astype(i32)
            base = base + jnp.sum(member, axis=1, keepdims=True)
            aim_ref[j : j + 1, :] = owners[j] * cap + pos
            place = jnp.where(pos + q * cap == lane, 1.0, 0.0).astype(bf16)
            parts = jnp.concatenate([member * pick(1, j), member * pick(2, j)], axis=0).astype(bf16)
            packed = packed + lax.dot_general(parts, place, NT, preferred_element_type=f32)

        def step(i, carry):
            start = i * some * cap
            aim = aim_ref[:per_bag, :] - start
            hit = aim[0:1, :] == line
            for j in range(1, per_bag):
                hit = hit | (aim[j : j + 1, :] == line)
            chosen = jnp.where(hit, 1.0, 0.0).astype(bf16)
            out = jnp.dot(chosen, g_ref[...], preferred_element_type=f32).astype(bf16)
            for k in range(some):
                out_ref[i * some + k, q * cap : (q + 1) * cap, :] = out[k * cap : (k + 1) * cap]
            return carry

        for i in range(here // some):
            step(i, 0)
    slots_ref[...] = packed
    row = lax.broadcasted_iota(i32, (EXTRA, width), 0)
    for d in range(here):
        extra = jnp.where(row == 0, slots_ref[d : d + 1, :], 0.0)
        extra = jnp.where(row == 1, slots_ref[here + d : here + d + 1, :], extra)
        out_ref[d, len(sources) * cap :, :] = extra.astype(bf16)


def vmem():
    return pl.BlockSpec(memory_space=pltpu.VMEM)


def limit():
    return pltpu.CompilerParams(vmem_limit_bytes=40 << 20)


def with_keys(layer_grad, bag_owner, bag_slot):
    samples = layer_grad.shape[0]
    slot = bag_slot.reshape(samples, KEYS) + 1
    keys = jnp.concatenate([bag_owner.reshape(samples, KEYS), slot >> 5, slot & 31], axis=1).astype(bf16)
    return jnp.concatenate([layer_grad, jnp.pad(keys, ((0, 0), (0, 128 - 3 * KEYS)))], axis=1)


def gather_near(a):
    half = a.shape[0] // 2
    prev = shift(a, "zh", NZH, 1)
    after = shift(a, "zh", NZH, NZH - 1)
    far = [shift(prev[:half], "zh", NZH, 1), shift(after[half:], "zh", NZH, NZH - 1)]
    return a, prev, after, jnp.concatenate(far, axis=0)


def dispatch(first, sources, dense_weight, width, here, cap):
    samples = sources[0].shape[0]
    features = dense_weight.shape[0] // width
    return pl.pallas_call(
        lambda *refs: dispatch_kernel(here, cap, *refs),
        out_shape=jax.ShapeDtypeStruct((here, len(sources) * cap + EXTRA, width), bf16),
        in_specs=[pl.BlockSpec(memory_space=pltpu.SMEM)] + [vmem()] * 5,
        out_specs=vmem(),
        scratch_shapes=[pltpu.VMEM((samples * features, width), bf16), pltpu.VMEM((2 * here, width), f32), pltpu.VMEM((8, samples * features), i32)],
        compiler_params=limit(),
        name="dispatch",
    )(first, *sources, dense_weight)


def collect(got, touch):
    here, height, width = got.shape
    many = height - EXTRA
    slots = got[:, many].astype(f32) * 32.0 + got[:, many + 1].astype(f32) - 1.0
    slots = jnp.pad(slots.astype(i32), ((0, 0), (0, EXTRA)), constant_values=-1)
    selector = (jnp.arange(touch, dtype=i32)[:, None] == slots.reshape(1, -1)).astype(bf16)
    return jnp.dot(selector, got.reshape(-1, width), preferred_element_type=f32)


def update_kernel(sums_ref, old_ref, accum_ref, out_ref):
    parts, part, width = sums_ref.shape
    total = sums_ref[0]
    for k in range(1, parts):
        total = total + sums_ref[k]
    new_accum = accum_ref[...] + jnp.mean(total * total, axis=1, keepdims=True)
    updated = old_ref[...] - 0.1 * total / (jnp.sqrt(new_accum) + 1e-06)
    lowest = jnp.min(updated, axis=1, keepdims=True)
    highest = jnp.max(updated, axis=1, keepdims=True)
    new_scale = (highest - lowest) / 255.0
    new_codes = (updated - lowest) / new_scale
    diagonal = lax.broadcasted_iota(i32, (part, part), 0) == lax.broadcasted_iota(i32, (part, part), 1)
    row = lax.broadcasted_iota(i32, (8, part), 0)
    small = jnp.zeros((8, part), f32)
    for i, column in enumerate((new_scale, lowest, new_accum)):
        flat = jnp.sum(jnp.where(diagonal, column, 0.0), axis=0, keepdims=True)
        small = jnp.where(row == i, flat, small)
    small = jnp.concatenate([small, jnp.zeros((8, width - part), f32)], axis=1)
    for k in range(parts):
        out_ref[k, :part, :] = new_codes
        out_ref[k, part:, :] = small


def update(sums, old, old_accum):
    parts, part, width = sums.shape
    return pl.pallas_call(
        update_kernel,
        out_shape=jax.ShapeDtypeStruct((parts, part + 8, width), f32),
        in_specs=[vmem()] * 3,
        out_specs=vmem(),
        compiler_params=limit(),
        name="update",
    )(sums, old, old_accum[:, None])


def swap(a, axis, size, bit):
    return lax.ppermute(a, axis, [(i, i ^ bit) for i in range(size)])


def halve(a, axis, size, bit, dim):
    side = (lax.axis_index(axis) & bit) // bit
    n = a.shape[dim] // 2
    keep = lax.dynamic_slice_in_dim(a, side * n, n, dim)
    send = lax.dynamic_slice_in_dim(a, (1 - side) * n, n, dim)
    return keep + swap(send, axis, size, bit)


def double(a, axis, size, bit, dim):
    other = swap(a, axis, size, bit)
    first = (lax.axis_index(axis) & bit) == 0
    return jnp.concatenate([jnp.where(first, a, other), jnp.where(first, other, a)], axis=dim)


def shift(a, axis, size, k):
    return lax.ppermute(a, axis, [(i, (i + k) % size) for i in range(size)])


def tie(*arrays):
    return lax.optimization_barrier(arrays)


def sum_over_three(a):
    me = lax.axis_index("zl")
    got = [a] + [shift(a, "zl", NZL, k) for k in range(1, NZL)]
    total = None
    for source in range(NZL):
        term = got[NZL - 1]
        for k in range(NZL - 1):
            term = jnp.where((me - k) % NZL == source, got[k], term)
        total = term if total is None else total + term
    return total


def shards(pooled, layer_grad, dense_weight, bag_owner, bag_slot, touched, codes, row_scale, row_bias, accum):
    here = NY * NC
    parts = NX * NZL
    width = codes.shape[1]
    touch = touched.shape[0]
    part = touch // parts
    cap = 2 * bag_slot.shape[0] // (NZH * here)
    first = (lax.axis_index("zh") * here).astype(i32).reshape(1)
    sources = gather_near(with_keys(layer_grad, bag_owner, bag_slot))

    w = lax.dot_general(pooled, layer_grad, (((0,), (0,)), ((), ())), preferred_element_type=f32)
    w = halve(w, "c", NC, 1, 0)
    w = halve(w, "x", NX, 1, 0)
    *sources, w = tie(*sources, w)

    rows = dispatch(first, sources, dense_weight, width, here, cap)
    got = lax.all_to_all(rows, ("y", "c"), 0, 0, tiled=True)
    w = halve(w, "x", NX, 2, 0)
    w = halve(w, "y", NY, 1, 0)
    w = halve(w, "y", NY, 2, 0)
    mine = lax.axis_index("x") * NZL + lax.axis_index("zl")
    local = lax.dynamic_slice_in_dim(touched, mine * part, part, 0)
    old = codes[local].astype(f32) * row_scale[local][:, None] + row_bias[local][:, None]
    old_accum = accum[local]
    got, w, old, old_accum = tie(got, w, old, old_accum)

    sums = collect(got, touch).reshape(parts, part, width)
    sums = lax.all_to_all(sums, REP, 0, 0, tiled=True)
    w = w + swap(w, "y", NY, 4)
    w = w + swap(w, "zh", NZH, 1)
    w = w + swap(w, "zh", NZH, 2)
    sums, w = tie(sums, w)

    payload = lax.all_to_all(update(sums, old, old_accum), REP, 0, 0, tiled=True)
    w = sum_over_three(w)
    w = double(w, "y", NY, 2, 0)
    w = double(w, "y", NY, 1, 0)
    w = double(w, "x", NX, 2, 0)
    w = double(w, "x", NX, 1, 0)
    weight_grad = double(w, "c", NC, 1, 0)
    new_codes = payload[:, :part].reshape(touch, width)
    new_scale, lowest, new_accum = (payload[:, part + i, :part].reshape(touch) for i in range(3))
    return (weight_grad, new_codes, new_scale, lowest, new_accum)


def solution(mesh):
    mesh = Mesh(mesh.devices.reshape(NX, NZL, NZH, NY, NC), AXES)
    in_specs = (
        P(AXES, None),
        P(AXES, None),
        P(),
        P(AXES, None),
        P(AXES),
        P(SHARD),
        P(SHARD, None),
        P(SHARD),
        P(SHARD),
        P(SHARD),
    )
    out_specs = (P(), P(SHARD, None), P(SHARD), P(SHARD), P(SHARD))
    return jax.shard_map(shards, mesh=mesh, in_specs=in_specs, out_specs=out_specs, check_vma=False)
```

time: 307 us -> 284 us (0.925)
  the two profiles are of different devices: /device:TPU:203 before, /device:TPU:1 now
where the time goes in v2:
time: 284 us; the launch traced here: 283 us
  waiting for transfers between devices  129 us (45%)
  starting transfers between devices  107 us (38%)
  local copies, waits for them, and re-layouts  17.4 us (6%)
  other arithmetic  12.2 us (4%)
  matrix products  8.35 us (3%)
  Pallas kernels  8.15 us (3%)
    ppermute x13, waiting for transfers between devices, swap(): return lax.ppermute(a, axis, [(i, i ^ bit) for i in range(size)])  94.9 us
    ppermute x13, starting transfers between devices, swap(): return lax.ppermute(a, axis, [(i, i ^ bit) for i in range(size)])  54.2 us
    ppermute x6, waiting for transfers between devices, shift(): return lax.ppermute(a, axis, [(i, (i + k) % size) for i in range(size)])  33.9 us
    ppermute x6, starting transfers between devices, shift(): return lax.ppermute(a, axis, [(i, (i + k) % size) for i in range(size)])  21.6 us
    all_to_all x1, starting transfers between devices, shards(): got = lax.all_to_all(rows, ('y', 'c'), 0, 0, tiled=True)  14.6 us
    all_to_all x1, starting transfers between devices, shards(): lax.all_to_all(update(sums, old, old_accum), REP, 0, 0, tiled=True)  9.21 us
    all_to_all x1, starting transfers between devices, shards(): sums = lax.all_to_all(sums, REP, 0, 0, tiled=True)  7.16 us
    dot_general x1, matrix products, collect(): return jnp.dot(selector, got.reshape(-1, width), preferred_element_type=f32)  6.78 us
  transfers between devices with their start and end apart: 22, of which 16 were waited for; matrix products, arithmetic and copies ran while one was open for 5% of the time, Pallas kernels for 0%

profile of v2, /device:TPU:1, one launch (start us, length us, event | category | flops | bytes accessed | tf_op | source)
XLA Modules:
  0.0 283.0 jit_solution(8548800263486764447)
XLA Ops:
  3.6 12.4 %collective-permute-start.4 = (f32[512,512]{1,0:T(8,128)S(1)}, f32[512,512]{1,0:T(8,128)}, u32[]{:S(2)}, u32[]{:S(2)}) collective-permute-start(f32[512,512]{1,0:T(8,128)S(1)} %constant_dynamic-slice_fusion.4), channel_id=1, source_target_pairs={{0,1},{1,0},{2,3},{3,2},{4,5},{5,4},{6,7},{7,6},{8,9},{9,8},{10,11... | collective-permute-start | bytes 3145736 | tf_op jit(solution)/shard_map/ppermute | solution.py:161
  23.3 6.5 %collective-permute-start.1 = (bf16[128,640]{1,0:T(8,128)(2,1)S(1)}, bf16[128,640]{1,0:T(8,128)(2,1)S(1)}, u32[]{:S(2)}, u32[]{:S(2)}) collective-permute-start(bf16[128,640]{1,0:T(8,128)(2,1)S(1)} %pad_maximum_fusion.4.refs_1_), channel_id=1, source_target_pairs={{0,48},{16,0},{32,16},{48,32},{1,49},{17,1},{33,17},{49,33},{2,50}... | collective-permute-start | bytes 491528 | tf_op jit(solution)/shard_map/ppermute | solution.py:179
  31.7 6.1 %collective-permute-done.1.refs_3_ = bf16[128,640]{1,0:T(8,128)(2,1)S(1)} collective-permute-done((bf16[128,640]{1,0:T(8,128)(2,1)S(1)}, bf16[128,640]{1,0:T(8,128)(2,1)S(1)}, u32[]{:S(2)}, u32[]{:S(2)}) %collective-permute-start.1) | collective-permute-done | bytes 163872 | tf_op jit(solution)/shard_map/ppermute | solution.py:179
  38.5 4.7 %collective-permute-start.3 = (bf16[64,640]{1,0:T(8,128)(2,1)}, bf16[64,640]{1,0:T(8,128)(2,1)S(1)}, u32[]{:S(2)}, u32[]{:S(2)}) collective-permute-start(bf16[64,640]{1,0:T(8,128)(2,1)} %slice.41), channel_id=1, source_target_pairs={{0,48},{16,0},{32,16},{48,32},{1,49},{17,1},{33,17},{49,33},{2,50}... | collective-permute-start | bytes 245768 | tf_op jit(solution)/shard_map/ppermute | solution.py:179
  44.5 2.3 collective-permute-start.2
  46.9 6.2 %collective-permute-done.2 = bf16[64,640]{1,0:T(8,128)(2,1)} collective-permute-done((bf16[64,640]{1,0:T(8,128)(2,1)}, bf16[64,640]{1,0:T(8,128)(2,1)}, u32[]{:S(2)}, u32[]{:S(2)}) %collective-permute-start.2) | collective-permute-done | bytes 81952 | tf_op jit(solution)/shard_map/ppermute | solution.py:179
  56.9 6.3 %dispatch.1 = bf16[16,272,256]{2,1,0:T(8,128)(2,1)S(1)} custom-call(s32[1]{0:T(128)} %bitcast.refs_0_, bf16[128,640]{1,0:T(8,128)(2,1)S(1)} %pad_maximum_fusion.4.refs_1_, bf16[128,640]{1,0:T(8,128)(2,1)S(1)} %copy-done.5, bf16[128,640]{1,0:T(8,128)(2,1)S(1)} %collective-permute-done.1.refs_3_, bf16[128,640]{1,0:T(8,128)(2,1)S(1)} %pad_maximum_fusion.5.refs_4_, ...), custom_call_target="tpu_custom_call" | custom-call | tf_op jit(solution)/shard_map/dispatch/pallas_call | solution.py:105
  64.6 14.6 %all-to-all-start = ((bf16[16,272,256]{2,1,0:T(8,128)(2,1)}), bf16[16,272,256]{2,1,0:T(8,128)(2,1)}, u32[]{:S(2)}, u32[]{:S(2)}) async-start(bf16[16,272,256]{2,1,0:T(8,128)(2,1)} %copy-done.1), calls=%async_computation | async-start | bytes 4456448 | tf_op jit(solution)/shard_map/all_to_all | solution.py:214
  79.3 4.4 %collective-permute-start.6 = (f32[128,512]{1,0:T(8,128)S(1)}, f32[128,512]{1,0:T(8,128)S(1)}, u32[]{:S(2)}, u32[]{:S(2)}) collective-permute-start(f32[128,512]{1,0:T(8,128)S(1)} %constant_dynamic-slice_fusion.2), channel_id=1, source_target_pairs={{0,384},{192,576},{384,0},{576,192},{1,385},{193,577},{385,1},{577... | collective-permute-start | bytes 786440 | tf_op jit(solution)/shard_map/ppermute | solution.py:161
  90.5 3.2 %collective-permute-start.7 = (f32[64,512]{1,0:T(8,128)S(1)}, f32[64,512]{1,0:T(8,128)S(1)}, u32[]{:S(2)}, u32[]{:S(2)}) collective-permute-start(f32[64,512]{1,0:T(8,128)S(1)} %constant_dynamic-slice_fusion.1), channel_id=1, source_target_pairs={{0,2},{2,0},{4,6},{6,4},{8,10},{10,8},{12,14},{14,12},{1,3},{3,1},... | collective-permute-start | bytes 393224 | tf_op jit(solution)/shard_map/ppermute | solution.py:161
  93.8 38.5 %collective-permute-done.7 = f32[64,512]{1,0:T(8,128)S(1)} collective-permute-done((f32[64,512]{1,0:T(8,128)S(1)}, f32[64,512]{1,0:T(8,128)S(1)}, u32[]{:S(2)}, u32[]{:S(2)}) %collective-permute-start.7) | collective-permute-done | bytes 131104 | tf_op jit(solution)/shard_map/ppermute | solution.py:161
  132.4 4.3 %collective-permute-start.8 = (f32[32,512]{1,0:T(8,128)S(1)}, f32[32,512]{1,0:T(8,128)S(1)}, u32[]{:S(2)}, u32[]{:S(2)}) collective-permute-start(f32[32,512]{1,0:T(8,128)S(1)} %constant_dynamic-slice_fusion), channel_id=1, source_target_pairs={{0,4},{2,6},{4,0},{6,2},{8,12},{10,14},{12,8},{14,10},{1,5},{3,7},... | collective-permute-start | bytes 196616 | tf_op jit(solution)/shard_map/ppermute | solution.py:161
  136.7 3.5 %collective-permute-done.8 = f32[32,512]{1,0:T(8,128)S(1)} collective-permute-done((f32[32,512]{1,0:T(8,128)S(1)}, f32[32,512]{1,0:T(8,128)S(1)}, u32[]{:S(2)}, u32[]{:S(2)}) %collective-permute-start.8) | collective-permute-done | bytes 65568 | tf_op jit(solution)/shard_map/ppermute | solution.py:161
  141.3 6.8 %fusion = f32[12,128,256]{2,1,0:T(8,128)} fusion(bf16[4352,256,1]{1,0,2:T(8,128)(2,1)} %bitcast.2, s32[4352]{0:T(1024)S(1)} %eq.76, s32[12,128]{1,0:T(8,128)S(1)} %multiply_add_fusion.1), kind=kOutput, calls=%fused_computation.4 | convolution fusion | flops 3429236736 | bytes 3824640 | tf_op jit(solution)/shard_map/dot_general | solution.py:122
  148.1 7.2 %all-to-all-start.1 = ((f32[12,128,256]{2,1,0:T(8,128)}), f32[12,128,256]{2,1,0:T(8,128)}, u32[]{:S(2)}, u32[]{:S(2)}) async-start(f32[12,128,256]{2,1,0:T(8,128)} %fusion), calls=%async_computation.1 | async-start | bytes 3145728 | tf_op jit(solution)/shard_map/all_to_all | solution.py:225
  155.3 4.2 %collective-permute-start.9 = (f32[32,512]{1,0:T(8,128)S(1)}, f32[32,512]{1,0:T(8,128)S(1)}, u32[]{:S(2)}, u32[]{:S(2)}) collective-permute-start(f32[32,512]{1,0:T(8,128)S(1)} %dynamic-slice_add_fusion.4), channel_id=1, source_target_pairs={{0,8},{2,10},{4,12},{6,14},{8,0},{10,2},{12,4},{14,6},{1,9},{3,11}... | collective-permute-start | bytes 196616 | tf_op jit(solution)/shard_map/ppermute | solution.py:161
  159.4 5.5 %collective-permute-done.9 = f32[32,512]{1,0:T(8,128)S(1)} collective-permute-done((f32[32,512]{1,0:T(8,128)S(1)}, f32[32,512]{1,0:T(8,128)S(1)}, u32[]{:S(2)}, u32[]{:S(2)}) %collective-permute-start.9) | collective-permute-done | bytes 65568 | tf_op jit(solution)/shard_map/ppermute | solution.py:161
  166.9 11.5 %collective-permute-done.10 = f32[32,512]{1,0:T(8,128)S(1)} collective-permute-done((f32[32,512]{1,0:T(8,128)S(1)}, f32[32,512]{1,0:T(8,128)S(1)}, u32[]{:S(2)}, u32[]{:S(2)}) %collective-permute-start.10) | collective-permute-done | bytes 65568 | tf_op jit(solution)/shard_map/ppermute | solution.py:161
  180.5 9.3 %collective-permute-done.11 = f32[32,512]{1,0:T(8,128)S(1)} collective-permute-done((f32[32,512]{1,0:T(8,128)S(1)}, f32[32,512]{1,0:T(8,128)S(1)}, u32[]{:S(2)}, u32[]{:S(2)}) %collective-permute-start.11) | collective-permute-done | bytes 65568 | tf_op jit(solution)/shard_map/ppermute | solution.py:161
  192.8 9.2 %all-to-all-start.2 = ((f32[12,136,256]{2,1,0:T(8,128)}), f32[12,136,256]{2,1,0:T(8,128)}, u32[]{:S(2)}, u32[]{:S(2)}) async-start(f32[12,136,256]{2,1,0:T(8,128)} %copy-done.2), calls=%async_computation.2 | async-start | bytes 3342336 | tf_op jit(solution)/shard_map/all_to_all | solution.py:231
  202.0 4.2 %collective-permute-start.13 = (f32[32,512]{1,0:T(8,128)S(1)}, f32[32,512]{1,0:T(8,128)S(1)}, u32[]{:S(2)}, u32[]{:S(2)}) collective-permute-start(f32[32,512]{1,0:T(8,128)S(1)} %add.144), channel_id=1, source_target_pairs={{0,128},{64,0},{128,64},{1,129},{65,1},{129,65},{2,130},{66,2},{13... | collective-permute-start | bytes 196616 | tf_op jit(solution)/shard_map/ppermute | solution.py:179
  208.2 18.7 %collective-permute-done.13 = f32[32,512]{1,0:T(8,128)S(1)} collective-permute-done((f32[32,512]{1,0:T(8,128)S(1)}, f32[32,512]{1,0:T(8,128)S(1)}, u32[]{:S(2)}, u32[]{:S(2)}) %collective-permute-start.13) | collective-permute-done | bytes 65568 | tf_op jit(solution)/shard_map/ppermute | solution.py:179
  226.9 2.9 %collective-permute-done.12 = f32[32,512]{1,0:T(8,128)S(1)} collective-permute-done((f32[32,512]{1,0:T(8,128)S(1)}, f32[32,512]{1,0:T(8,128)S(1)}, u32[]{:S(2)}, u32[]{:S(2)}) %collective-permute-start.12) | collective-permute-done | bytes 65568 | tf_op jit(solution)/shard_map/ppermute | solution.py:179
  231.8 4.0 %collective-permute-done.14 = f32[32,512]{1,0:T(8,128)S(1)} collective-permute-done((f32[32,512]{1,0:T(8,128)S(1)}, f32[32,512]{1,0:T(8,128)S(1)}, u32[]{:S(2)}, u32[]{:S(2)}) %collective-permute-start.14) | collective-permute-done | bytes 65568 | tf_op jit(solution)/shard_map/ppermute | solution.py:161
  237.7 3.8 %collective-permute-done.15 = f32[64,512]{1,0:T(8,128)S(1)} collective-permute-done((f32[64,512]{1,0:T(8,128)S(1)}, f32[64,512]{1,0:T(8,128)S(1)}, u32[]{:S(2)}, u32[]{:S(2)}) %collective-permute-start.15) | collective-permute-done | bytes 131104 | tf_op jit(solution)/shard_map/ppermute | solution.py:161
  241.6 4.2 %collective-permute-start.16 = (f32[128,512]{1,0:T(8,128)S(1)}, f32[128,512]{1,0:T(8,128)S(1)}, u32[]{:S(2)}, u32[]{:S(2)}) collective-permute-start(f32[128,512]{1,0:T(8,128)S(1)} %pad_maximum_fusion.3), channel_id=1, source_target_pairs={{0,384},{192,576},{384,0},{576,192},{1,385},{193,577},{385,1},{577... | collective-permute-start | bytes 786440 | tf_op jit(solution)/shard_map/ppermute | solution.py:161
  245.8 4.4 %collective-permute-done.16 = f32[128,512]{1,0:T(8,128)S(1)} collective-permute-done((f32[128,512]{1,0:T(8,128)S(1)}, f32[128,512]{1,0:T(8,128)S(1)}, u32[]{:S(2)}, u32[]{:S(2)}) %collective-permute-start.16) | collective-permute-done | bytes 262176 | tf_op jit(solution)/shard_map/ppermute | solution.py:161
  251.0 2.8 %collective-permute-start.17 = (f32[256,512]{1,0:T(8,128)S(1)}, f32[256,512]{1,0:T(8,128)}, u32[]{:S(2)}, u32[]{:S(2)}) collective-permute-start(f32[256,512]{1,0:T(8,128)S(1)} %pad_maximum_fusion.2), channel_id=1, source_target_pairs={{0,192},{192,0},{384,576},{576,384},{1,193},{193,1},{385,577},{577... | collective-permute-start | bytes 1572872 | tf_op jit(solution)/shard_map/ppermute | solution.py:161
  253.8 8.2 %collective-permute-done.17 = f32[256,512]{1,0:T(8,128)} collective-permute-done((f32[256,512]{1,0:T(8,128)S(1)}, f32[256,512]{1,0:T(8,128)}, u32[]{:S(2)}, u32[]{:S(2)}) %collective-permute-start.17) | collective-permute-done | bytes 524320 | tf_op jit(solution)/shard_map/ppermute | solution.py:161
  264.3 9.0 %collective-permute-start.18 = (f32[512,512]{1,0:T(8,128)}, f32[512,512]{1,0:T(8,128)}, u32[]{:S(2)}, u32[]{:S(2)}) collective-permute-start(f32[512,512]{1,0:T(8,128)} %pad_maximum_fusion.1), channel_id=1, source_target_pairs={{0,1},{1,0},{2,3},{3,2},{4,5},{5,4},{6,7},{7,6},{8,9},{9,8},{10,11... | collective-permute-start | bytes 3145736 | tf_op jit(solution)/shard_map/ppermute | solution.py:161
  273.2 2.6 collective-permute-done.18
  280.4 2.7 slice.42
  (97 shorter events, 47.5 us)
Async XLA Ops:
  0.6 87.4 %copy-start = (bf16[4096,256]{1,0:T(8,128)(2,1)S(1)}, bf16[4096,256]{1,0:T(8,128)(2,1)}, u32[]{:S(2)}) copy-start(bf16[4096,256]{1,0:T(8,128)(2,1)} %param.16) | copy-start | bytes 6291460
  0.7 15.4 %copy-start.15 = (s32[2048]{0:T(1024)S(1)}, s32[2048]{0:T(1024)}, u32[]{:S(2)}) copy-start(s32[2048]{0:T(1024)} %param.14) | copy-start | bytes 24580
  0.7 15.5 %copy-start.14 = (s32[2048,1]{0,1:T(1,128)S(1)}, s32[2048,1]{0,1:T(1,128)}, u32[]{:S(2)}) copy-start(s32[2048,1]{0,1:T(1,128)} %param.13) | copy-start | bytes 24580
  3.6 14.8 %collective-permute-start.4 = (f32[512,512]{1,0:T(8,128)S(1)}, f32[512,512]{1,0:T(8,128)}, u32[]{:S(2)}, u32[]{:S(2)}) collective-permute-start(f32[512,512]{1,0:T(8,128)S(1)} %constant_dynamic-slice_fusion.4), channel_id=1, source_target_pairs={{0,1},{1,0},{2,3},{3,2},{4,5},{5,4},{6,7},{7,6},{8,9},{9,8},{10,11... | collective-permute-start | bytes 3145736 | tf_op jit(solution)/shard_map/ppermute | solution.py:161
  16.4 6.8 %copy-start.13 = (bf16[128,512]{1,0:T(8,128)(2,1)S(1)}, bf16[128,512]{1,0:T(8,128)(2,1)}, u32[]{:S(2)}) copy-start(bf16[128,512]{1,0:T(8,128)(2,1)} %param.11) | copy-start | bytes 393220
  20.2 23.6 %copy-start.10 = (f32[512,512]{1,0:T(8,128)}, f32[512,512]{1,0:T(8,128)S(1)}, u32[]{:S(2)}) copy-start(f32[512,512]{1,0:T(8,128)S(1)} %dynamic-slice_add_fusion) | copy-start | bytes 3145732
  20.2 35.8 %copy-start.3 = (bf16[1024,512]{1,0:T(8,128)(2,1)S(1)}, bf16[1024,512]{1,0:T(8,128)(2,1)}, u32[]{:S(2)}) copy-start(bf16[1024,512]{1,0:T(8,128)(2,1)} %refs_5_.1) | copy-start | bytes 3145732
  21.1 32.8 %collective-permute-start.5 = (f32[256,512]{1,0:T(8,128)}, f32[256,512]{1,0:T(8,128)}, u32[]{:S(2)}, u32[]{:S(2)}) collective-permute-start(f32[256,512]{1,0:T(8,128)} %constant_dynamic-slice_fusion.3), channel_id=1, source_target_pairs={{0,192},{192,0},{384,576},{576,384},{1,193},{193,1},{385,577},{577... | collective-permute-start | bytes 1572872 | tf_op jit(solution)/shard_map/ppermute | solution.py:161
  23.3 14.6 %collective-permute-start.1 = (bf16[128,640]{1,0:T(8,128)(2,1)S(1)}, bf16[128,640]{1,0:T(8,128)(2,1)S(1)}, u32[]{:S(2)}, u32[]{:S(2)}) collective-permute-start(bf16[128,640]{1,0:T(8,128)(2,1)S(1)} %pad_maximum_fusion.4.refs_1_), channel_id=1, source_target_pairs={{0,48},{16,0},{32,16},{48,32},{1,49},{17,1},{33,17},{49,33},{2,50}... | collective-permute-start | bytes 491528 | tf_op jit(solution)/shard_map/ppermute | solution.py:179
  29.8 13.5 %collective-permute-start = (bf16[128,640]{1,0:T(8,128)(2,1)S(1)}, bf16[128,640]{1,0:T(8,128)(2,1)S(1)}, u32[]{:S(2)}, u32[]{:S(2)}) collective-permute-start(bf16[128,640]{1,0:T(8,128)(2,1)S(1)} %pad_maximum_fusion.4.refs_1_), channel_id=1, source_target_pairs={{0,16},{16,32},{32,48},{48,0},{1,17},{17,33},{33,49},{49,1},{2,18}... | collective-permute-start | bytes 491528 | tf_op jit(solution)/shard_map/ppermute | solution.py:179
  38.5 8.4 %collective-permute-start.3 = (bf16[64,640]{1,0:T(8,128)(2,1)}, bf16[64,640]{1,0:T(8,128)(2,1)S(1)}, u32[]{:S(2)}, u32[]{:S(2)}) collective-permute-start(bf16[64,640]{1,0:T(8,128)(2,1)} %slice.41), channel_id=1, source_target_pairs={{0,48},{16,0},{32,16},{48,32},{1,49},{17,1},{33,17},{49,33},{2,50}... | collective-permute-start | bytes 245768 | tf_op jit(solution)/shard_map/ppermute | solution.py:179
  44.5 8.5 %collective-permute-start.2 = (bf16[64,640]{1,0:T(8,128)(2,1)}, bf16[64,640]{1,0:T(8,128)(2,1)}, u32[]{:S(2)}, u32[]{:S(2)}) collective-permute-start(bf16[64,640]{1,0:T(8,128)(2,1)} %slice.40), channel_id=1, source_target_pairs={{0,16},{16,32},{32,48},{48,0},{1,17},{17,33},{33,49},{49,1},{2,18}... | collective-permute-start | bytes 245768 | tf_op jit(solution)/shard_map/ppermute | solution.py:179
  64.6 14.6 %copy-start.12 = (f32[256,512]{1,0:T(8,128)S(1)}, f32[256,512]{1,0:T(8,128)}, u32[]{:S(2)}) copy-start(f32[256,512]{1,0:T(8,128)} %dynamic-slice_add_fusion.1) | copy-start | bytes 1572868
  64.6 19.9 %copy-start.6 = (f32[4096]{0:T(1024)S(1)}, f32[4096]{0:T(1024)}, u32[]{:S(2)}) copy-start(f32[4096]{0:T(1024)} %param.19) | copy-start | bytes 49156
  64.6 21.0 %copy-start.7 = (f32[4096]{0:T(1024)S(1)}, f32[4096]{0:T(1024)}, u32[]{:S(2)}) copy-start(f32[4096]{0:T(1024)} %param.18) | copy-start | bytes 49156
  64.6 22.2 %copy-start.8 = (f32[4096]{0:T(1024)S(1)}, f32[4096]{0:T(1024)}, u32[]{:S(2)}) copy-start(f32[4096]{0:T(1024)} %param.17) | copy-start | bytes 49156
  64.6 75.6 %all-to-all-start = ((bf16[16,272,256]{2,1,0:T(8,128)(2,1)}), bf16[16,272,256]{2,1,0:T(8,128)(2,1)}, u32[]{:S(2)}, u32[]{:S(2)}) async-start(bf16[16,272,256]{2,1,0:T(8,128)(2,1)} %copy-done.1), calls=%async_computation | async-start | bytes 4456448 | tf_op jit(solution)/shard_map/all_to_all | solution.py:214
  79.3 11.2 %collective-permute-start.6 = (f32[128,512]{1,0:T(8,128)S(1)}, f32[128,512]{1,0:T(8,128)S(1)}, u32[]{:S(2)}, u32[]{:S(2)}) collective-permute-start(f32[128,512]{1,0:T(8,128)S(1)} %constant_dynamic-slice_fusion.2), channel_id=1, source_target_pairs={{0,384},{192,576},{384,0},{576,192},{1,385},{193,577},{385,1},{577... | collective-permute-start | bytes 786440 | tf_op jit(solution)/shard_map/ppermute | solution.py:161
  90.5 41.8 %collective-permute-start.7 = (f32[64,512]{1,0:T(8,128)S(1)}, f32[64,512]{1,0:T(8,128)S(1)}, u32[]{:S(2)}, u32[]{:S(2)}) collective-permute-start(f32[64,512]{1,0:T(8,128)S(1)} %constant_dynamic-slice_fusion.1), channel_id=1, source_target_pairs={{0,2},{2,0},{4,6},{6,4},{8,10},{10,8},{12,14},{14,12},{1,3},{3,1},... | collective-permute-start | bytes 393224 | tf_op jit(solution)/shard_map/ppermute | solution.py:161
  132.4 7.8 %collective-permute-start.8 = (f32[32,512]{1,0:T(8,128)S(1)}, f32[32,512]{1,0:T(8,128)S(1)}, u32[]{:S(2)}, u32[]{:S(2)}) collective-permute-start(f32[32,512]{1,0:T(8,128)S(1)} %constant_dynamic-slice_fusion), channel_id=1, source_target_pairs={{0,4},{2,6},{4,0},{6,2},{8,12},{10,14},{12,8},{14,10},{1,5},{3,7},... | collective-permute-start | bytes 196616 | tf_op jit(solution)/shard_map/ppermute | solution.py:161
  148.1 41.7 %all-to-all-start.1 = ((f32[12,128,256]{2,1,0:T(8,128)}), f32[12,128,256]{2,1,0:T(8,128)}, u32[]{:S(2)}, u32[]{:S(2)}) async-start(f32[12,128,256]{2,1,0:T(8,128)} %fusion), calls=%async_computation.1 | async-start | bytes 3145728 | tf_op jit(solution)/shard_map/all_to_all | solution.py:225
  155.3 9.7 %collective-permute-start.9 = (f32[32,512]{1,0:T(8,128)S(1)}, f32[32,512]{1,0:T(8,128)S(1)}, u32[]{:S(2)}, u32[]{:S(2)}) collective-permute-start(f32[32,512]{1,0:T(8,128)S(1)} %dynamic-slice_add_fusion.4), channel_id=1, source_target_pairs={{0,8},{2,10},{4,12},{6,14},{8,0},{10,2},{12,4},{14,6},{1,9},{3,11}... | collective-permute-start | bytes 196616 | tf_op jit(solution)/shard_map/ppermute | solution.py:161
  165.0 13.4 %collective-permute-start.10 = (f32[32,512]{1,0:T(8,128)S(1)}, f32[32,512]{1,0:T(8,128)S(1)}, u32[]{:S(2)}, u32[]{:S(2)}) collective-permute-start(f32[32,512]{1,0:T(8,128)S(1)} %add.142), channel_id=1, source_target_pairs={{0,16},{16,0},{32,48},{48,32},{1,17},{17,1},{33,49},{49,33},{2,18}... | collective-permute-start | bytes 196616 | tf_op jit(solution)/shard_map/ppermute | solution.py:161
  178.4 11.3 %collective-permute-start.11 = (f32[32,512]{1,0:T(8,128)S(1)}, f32[32,512]{1,0:T(8,128)S(1)}, u32[]{:S(2)}, u32[]{:S(2)}) collective-permute-start(f32[32,512]{1,0:T(8,128)S(1)} %add.143), channel_id=1, source_target_pairs={{0,32},{16,48},{32,0},{48,16},{1,33},{17,49},{33,1},{49,17},{2,34}... | collective-permute-start | bytes 196616 | tf_op jit(solution)/shard_map/ppermute | solution.py:161
  192.8 86.0 %all-to-all-start.2 = ((f32[12,136,256]{2,1,0:T(8,128)}), f32[12,136,256]{2,1,0:T(8,128)}, u32[]{:S(2)}, u32[]{:S(2)}) async-start(f32[12,136,256]{2,1,0:T(8,128)} %copy-done.2), calls=%async_computation.2 | async-start | bytes 3342336 | tf_op jit(solution)/shard_map/all_to_all | solution.py:231
  202.0 24.9 %collective-permute-start.13 = (f32[32,512]{1,0:T(8,128)S(1)}, f32[32,512]{1,0:T(8,128)S(1)}, u32[]{:S(2)}, u32[]{:S(2)}) collective-permute-start(f32[32,512]{1,0:T(8,128)S(1)} %add.144), channel_id=1, source_target_pairs={{0,128},{64,0},{128,64},{1,129},{65,1},{129,65},{2,130},{66,2},{13... | collective-permute-start | bytes 196616 | tf_op jit(solution)/shard_map/ppermute | solution.py:179
  206.3 23.6 %collective-permute-start.12 = (f32[32,512]{1,0:T(8,128)S(1)}, f32[32,512]{1,0:T(8,128)S(1)}, u32[]{:S(2)}, u32[]{:S(2)}) collective-permute-start(f32[32,512]{1,0:T(8,128)S(1)} %add.144), channel_id=1, source_target_pairs={{0,64},{64,128},{128,0},{1,65},{65,129},{129,1},{2,66},{66,130},{1... | collective-permute-start | bytes 196616 | tf_op jit(solution)/shard_map/ppermute | solution.py:179
  229.8 5.9 %collective-permute-start.14 = (f32[32,512]{1,0:T(8,128)S(1)}, f32[32,512]{1,0:T(8,128)S(1)}, u32[]{:S(2)}, u32[]{:S(2)}) collective-permute-start(f32[32,512]{1,0:T(8,128)S(1)} %select_add_fusion), channel_id=1, source_target_pairs={{0,4},{2,6},{4,0},{6,2},{8,12},{10,14},{12,8},{14,10},{1,5},{3,7},... | collective-permute-start | bytes 196616 | tf_op jit(solution)/shard_map/ppermute | solution.py:161
  235.8 5.7 %collective-permute-start.15 = (f32[64,512]{1,0:T(8,128)S(1)}, f32[64,512]{1,0:T(8,128)S(1)}, u32[]{:S(2)}, u32[]{:S(2)}) collective-permute-start(f32[64,512]{1,0:T(8,128)S(1)} %pad_maximum_fusion.6), channel_id=1, source_target_pairs={{0,2},{2,0},{4,6},{6,4},{8,10},{10,8},{12,14},{14,12},{1,3},{3,1},... | collective-permute-start | bytes 393224 | tf_op jit(solution)/shard_map/ppermute | solution.py:161
  241.6 8.6 %collective-permute-start.16 = (f32[128,512]{1,0:T(8,128)S(1)}, f32[128,512]{1,0:T(8,128)S(1)}, u32[]{:S(2)}, u32[]{:S(2)}) collective-permute-start(f32[128,512]{1,0:T(8,128)S(1)} %pad_maximum_fusion.3), channel_id=1, source_target_pairs={{0,384},{192,576},{384,0},{576,192},{1,385},{193,577},{385,1},{577... | collective-permute-start | bytes 786440 | tf_op jit(solution)/shard_map/ppermute | solution.py:161
  251.0 11.1 %collective-permute-start.17 = (f32[256,512]{1,0:T(8,128)S(1)}, f32[256,512]{1,0:T(8,128)}, u32[]{:S(2)}, u32[]{:S(2)}) collective-permute-start(f32[256,512]{1,0:T(8,128)S(1)} %pad_maximum_fusion.2), channel_id=1, source_target_pairs={{0,192},{192,0},{384,576},{576,384},{1,193},{193,1},{385,577},{577... | collective-permute-start | bytes 1572872 | tf_op jit(solution)/shard_map/ppermute | solution.py:161
  264.3 11.6 %collective-permute-start.18 = (f32[512,512]{1,0:T(8,128)}, f32[512,512]{1,0:T(8,128)}, u32[]{:S(2)}, u32[]{:S(2)}) collective-permute-start(f32[512,512]{1,0:T(8,128)} %pad_maximum_fusion.1), channel_id=1, source_target_pairs={{0,1},{1,0},{2,3},{3,2},{4,5},{5,4},{6,7},{7,6},{8,9},{9,8},{10,11... | collective-permute-start | bytes 3145736 | tf_op jit(solution)/shard_map/ppermute | solution.py:161
  (6 other events, 6.2 us)

commit v3 on v2

--- a/solution.py
+++ b/solution.py
@@ -14,27 +14,26 @@
 NT = (((1,), (1,)), ((), ()))
 
 
-def dispatch_kernel(here, cap, first_ref, own_ref, prev_ref, next_ref, far_ref, w_ref, out_ref, g_ref, slots_ref, aim_ref):
-    samples = own_ref.shape[0]
+def dispatch_kernel(here, cap, first_ref, near_ref, w_ref, out_ref, g_ref, slots_ref, aim_ref):
+    count, samples = near_ref.shape[0], near_ref.shape[1]
     depth = w_ref.shape[1]
     width = out_ref.shape[2]
     features = w_ref.shape[0] // width
     bags = samples * features
     per_bag = KEYS // features
-    sources = (own_ref, prev_ref, next_ref, far_ref)
     group = lax.broadcasted_iota(i32, (here, bags), 0)
     earlier = lax.broadcasted_iota(i32, (bags, bags), 0) < lax.broadcasted_iota(i32, (bags, bags), 1)
     earlier = jnp.where(earlier, 1.0, 0.0).astype(bf16)
-    lane = lax.broadcasted_iota(i32, (len(sources) * cap, bags), 0)
-    packed = jnp.zeros((2 * here, len(sources) * cap), f32)
+    lane = lax.broadcasted_iota(i32, (count * cap, bags), 0)
+    packed = jnp.zeros((2 * here, count * cap), f32)
     some = 4
     line = lax.broadcasted_iota(i32, (some * cap, bags), 0)
-    for q, ref in enumerate(sources):
-        lg = ref[:, :depth]
+    for q in range(count):
+        lg = near_ref[q, :, :depth]
         for f in range(features):
             block = lax.dot_general(lg, w_ref[f * width : (f + 1) * width, :], NT, preferred_element_type=f32)
             g_ref[f * samples : (f + 1) * samples, :] = block.astype(bf16)
-        keys = jnp.transpose(ref[:, depth:].astype(f32))
+        keys = jnp.transpose(near_ref[q, :, depth:].astype(f32))
 
         def pick(kind, j):
             at = [kind * KEYS + f * per_bag + j for f in range(features)]
@@ -73,7 +72,7 @@
     for d in range(here):
         extra = jnp.where(row == 0, slots_ref[d : d + 1, :], 0.0)
         extra = jnp.where(row == 1, slots_ref[here + d : here + d + 1, :], extra)
-        out_ref[d, len(sources) * cap :, :] = extra.astype(bf16)
+        out_ref[d, count * cap :, :] = extra.astype(bf16)
 
 
 def vmem():
@@ -91,26 +90,18 @@
     return jnp.concatenate([layer_grad, jnp.pad(keys, ((0, 0), (0, 128 - 3 * KEYS)))], axis=1)
 
 
-def gather_near(a):
-    half = a.shape[0] // 2
-    prev = shift(a, "zh", NZH, 1)
-    after = shift(a, "zh", NZH, NZH - 1)
-    far = [shift(prev[:half], "zh", NZH, 1), shift(after[half:], "zh", NZH, NZH - 1)]
-    return a, prev, after, jnp.concatenate(far, axis=0)
-
-
-def dispatch(first, sources, dense_weight, width, here, cap):
-    samples = sources[0].shape[0]
+def dispatch(first, near, dense_weight, width, here, cap):
+    count, samples = near.shape[0], near.shape[1]
     features = dense_weight.shape[0] // width
     return pl.pallas_call(
         lambda *refs: dispatch_kernel(here, cap, *refs),
-        out_shape=jax.ShapeDtypeStruct((here, len(sources) * cap + EXTRA, width), bf16),
-        in_specs=[pl.BlockSpec(memory_space=pltpu.SMEM)] + [vmem()] * 5,
+        out_shape=jax.ShapeDtypeStruct((here, count * cap + EXTRA, width), bf16),
+        in_specs=[pl.BlockSpec(memory_space=pltpu.SMEM)] + [vmem()] * 2,
         out_specs=vmem(),
         scratch_shapes=[pltpu.VMEM((samples * features, width), bf16), pltpu.VMEM((2 * here, width), f32), pltpu.VMEM((8, samples * features), i32)],
         compiler_params=limit(),
         name="dispatch",
-    )(first, *sources, dense_weight)
+    )(first, near, dense_weight)
 
 
 def collect(got, touch):
@@ -203,18 +194,18 @@
     part = touch // parts
     cap = 2 * bag_slot.shape[0] // (NZH * here)
     first = (lax.axis_index("zh") * here).astype(i32).reshape(1)
-    sources = gather_near(with_keys(layer_grad, bag_owner, bag_slot))
-
+    near = with_keys(layer_grad, bag_owner, bag_slot)
+    near = lax.all_gather(near, "zh", axis=0, tiled=False)
+    rows = dispatch(first, near, dense_weight, width, here, cap)
+    rows, pooled = tie(rows, pooled)
+    got = lax.all_to_all(rows, ("y", "c"), 0, 0, tiled=True)
     w = lax.dot_general(pooled, layer_grad, (((0,), (0,)), ((), ())), preferred_element_type=f32)
     w = halve(w, "c", NC, 1, 0)
     w = halve(w, "x", NX, 1, 0)
-    *sources, w = tie(*sources, w)
-
-    rows = dispatch(first, sources, dense_weight, width, here, cap)
-    got = lax.all_to_all(rows, ("y", "c"), 0, 0, tiled=True)
     w = halve(w, "x", NX, 2, 0)
-    w = halve(w, "y", NY, 1, 0)
-    w = halve(w, "y", NY, 2, 0)
+    w = halve(w, "zh", NZH, 1, 0)
+    w = halve(w, "zh", NZH, 2, 0)
+    w = sum_over_three(w)
     mine = lax.axis_index("x") * NZL + lax.axis_index("zl")
     local = lax.dynamic_slice_in_dim(touched, mine * part, part, 0)
     old = codes[local].astype(f32) * row_scale[local][:, None] + row_bias[local][:, None]
@@ -223,15 +214,13 @@
 
     sums = collect(got, touch).reshape(parts, part, width)
     sums = lax.all_to_all(sums, REP, 0, 0, tiled=True)
-    w = w + swap(w, "y", NY, 4)
-    w = w + swap(w, "zh", NZH, 1)
-    w = w + swap(w, "zh", NZH, 2)
+    for bit in (1, 2, 4):
+        w = w + swap(w, "y", NY, bit)
+    w = double(w, "zh", NZH, 2, 0)
     sums, w = tie(sums, w)
 
     payload = lax.all_to_all(update(sums, old, old_accum), REP, 0, 0, tiled=True)
-    w = sum_over_three(w)
-    w = double(w, "y", NY, 2, 0)
-    w = double(w, "y", NY, 1, 0)
+    w = double(w, "zh", NZH, 1, 0)
     w = double(w, "x", NX, 2, 0)
     w = double(w, "x", NX, 1, 0)
     weight_grad = double(w, "c", NC, 1, 0)

time: 284 us -> 259 us (0.912)
  the two profiles are of different devices: /device:TPU:1 before, /device:TPU:69 now
where the time goes in v3:
time: 259 us; the launch traced here: 257 us
  starting transfers between devices  93.2 us (36%)
  waiting for transfers between devices  82.8 us (32%)
  blocking collectives  32.9 us (13%)
  local copies, waits for them, and re-layouts  16.8 us (6%)
  other arithmetic  13.6 us (5%)
  matrix products  8.55 us (3%)
  Pallas kernels  8.14 us (3%)
    ppermute x13, waiting for transfers between devices, swap(): return lax.ppermute(a, axis, [(i, i ^ bit) for i in range(size)])  79.7 us
    ppermute x13, starting transfers between devices, swap(): return lax.ppermute(a, axis, [(i, i ^ bit) for i in range(size)])  64.5 us
    all_gather x1, blocking collectives, shards(): near = lax.all_gather(near, 'zh', axis=0, tiled=False)  32.9 us
    ppermute x2, starting transfers between devices, shift(): return lax.ppermute(a, axis, [(i, (i + k) % size) for i in range(size)])  8.8 us
    all_to_all x1, starting transfers between devices, shards(): got = lax.all_to_all(rows, ('y', 'c'), 0, 0, tiled=True)  7.24 us
    dot_general x1, matrix products, collect(): return jnp.dot(selector, got.reshape(-1, width), preferred_element_type=f32)  6.77 us
    all_to_all x1, starting transfers between devices, shards(): lax.all_to_all(update(sums, old, old_accum), REP, 0, 0, tiled=True)  6.67 us
    pallas_call x1, Pallas kernels, dispatch(): pl.pallas_call(lambda *refs: dispatch_kernel(here, cap, *refs), out_shape...  6.3 us
  transfers between devices with their start and end apart: 18, of which 13 were waited for; matrix products, arithmetic and copies ran while one was open for 6% of the time, Pallas kernels for 0%

profile of v3, /device:TPU:69, one launch (start us, length us, event | category | flops | bytes accessed | tf_op | source)
XLA Modules:
  0.0 257.3 jit_solution(8408699595788797133)
XLA Ops:
  3.9 32.9 %all-gather = bf16[512,640]{1,0:T(8,128)(2,1)S(1)} all-gather(bf16[128,640]{1,0:T(8,128)(2,1)S(1)} %fusion.5), channel_id=2, replica_groups=mesh['x'=4,'zl'=3,'zh'=4,'y'=8,'c'=2] {'zh'}, dimensions={0}, use_global_device_ids=true | all-gather | bytes 819200 | tf_op jit(solution)/shard_map/all_gather | solution.py:198
  38.0 6.3 %dispatch.1 = bf16[16,272,256]{2,1,0:T(8,128)(2,1)S(1)} custom-call(s32[1]{0:T(128)} %bitcast.refs_0_, bf16[4,128,640]{2,1,0:T(8,128)(2,1)S(1)} %bitcast.16, bf16[1024,512]{1,0:T(8,128)(2,1)S(1)} %copy-done.3), custom_call_target="tpu_custom_call" | custom-call | tf_op jit(solution)/shard_map/dispatch/pallas_call | solution.py:96
  48.8 2.4 collective-permute-start
  51.1 7.2 %all-to-all-start = ((bf16[16,272,256]{2,1,0:T(8,128)(2,1)}), bf16[16,272,256]{2,1,0:T(8,128)(2,1)}, u32[]{:S(2)}, u32[]{:S(2)}) async-start(bf16[16,272,256]{2,1,0:T(8,128)(2,1)} %copy-done.1), calls=%async_computation | async-start | bytes 4456448 | tf_op jit(solution)/shard_map/all_to_all | solution.py:201
  61.0 2.9 %collective-permute-start.1 = (f32[256,512]{1,0:T(8,128)}, f32[256,512]{1,0:T(8,128)}, u32[]{:S(2)}, u32[]{:S(2)}) collective-permute-start(f32[256,512]{1,0:T(8,128)} %constant_dynamic-slice_fusion.3), channel_id=1, source_target_pairs={{0,192},{192,0},{384,576},{576,384},{1,193},{193,1},{385,577},{577... | collective-permute-start | bytes 1572872 | tf_op jit(solution)/shard_map/ppermute | solution.py:152
  64.0 12.7 %collective-permute-done.1 = f32[256,512]{1,0:T(8,128)} collective-permute-done((f32[256,512]{1,0:T(8,128)}, f32[256,512]{1,0:T(8,128)}, u32[]{:S(2)}, u32[]{:S(2)}) %collective-permute-start.1) | collective-permute-done | bytes 524320 | tf_op jit(solution)/shard_map/ppermute | solution.py:152
  78.6 2.1 collective-permute-start.2
  80.8 8.2 %collective-permute-done.2 = f32[128,512]{1,0:T(8,128)S(1)} collective-permute-done((f32[128,512]{1,0:T(8,128)S(1)}, f32[128,512]{1,0:T(8,128)S(1)}, u32[]{:S(2)}, u32[]{:S(2)}) %collective-permute-start.2) | collective-permute-done | bytes 262176 | tf_op jit(solution)/shard_map/ppermute | solution.py:152
  90.0 3.6 %collective-permute-start.3 = (f32[64,512]{1,0:T(8,128)S(1)}, f32[64,512]{1,0:T(8,128)S(1)}, u32[]{:S(2)}, u32[]{:S(2)}) collective-permute-start(f32[64,512]{1,0:T(8,128)S(1)} %constant_dynamic-slice_fusion.1), channel_id=1, source_target_pairs={{0,16},{16,0},{32,48},{48,32},{1,17},{17,1},{33,49},{49,33},{2,18}... | collective-permute-start | bytes 393224 | tf_op jit(solution)/shard_map/ppermute | solution.py:152
  99.2 6.4 %collective-permute-start.4 = (f32[32,512]{1,0:T(8,128)S(1)}, f32[32,512]{1,0:T(8,128)S(1)}, u32[]{:S(2)}, u32[]{:S(2)}) collective-permute-start(f32[32,512]{1,0:T(8,128)S(1)} %constant_dynamic-slice_fusion), channel_id=1, source_target_pairs={{0,32},{16,48},{32,0},{48,16},{1,33},{17,49},{33,1},{49,17},{2,34}... | collective-permute-start | bytes 196616 | tf_op jit(solution)/shard_map/ppermute | solution.py:152
  106.8 3.6 %collective-permute-done.4 = f32[32,512]{1,0:T(8,128)S(1)} collective-permute-done((f32[32,512]{1,0:T(8,128)S(1)}, f32[32,512]{1,0:T(8,128)S(1)}, u32[]{:S(2)}, u32[]{:S(2)}) %collective-permute-start.4) | collective-permute-done | bytes 65568 | tf_op jit(solution)/shard_map/ppermute | solution.py:152
  110.5 6.7 %collective-permute-start.5 = (f32[32,512]{1,0:T(8,128)S(1)}, f32[32,512]{1,0:T(8,128)S(1)}, u32[]{:S(2)}, u32[]{:S(2)}) collective-permute-start(f32[32,512]{1,0:T(8,128)S(1)} %dynamic-slice_add_fusion.4), channel_id=1, source_target_pairs={{0,64},{64,128},{128,0},{1,65},{65,129},{129,1},{2,66},{66,130},{1... | collective-permute-start | bytes 196616 | tf_op jit(solution)/shard_map/ppermute | solution.py:170
  117.2 2.1 collective-permute-start.6
  119.3 3.2 %collective-permute-done.6 = f32[32,512]{1,0:T(8,128)S(1)} collective-permute-done((f32[32,512]{1,0:T(8,128)S(1)}, f32[32,512]{1,0:T(8,128)S(1)}, u32[]{:S(2)}, u32[]{:S(2)}) %collective-permute-start.6) | collective-permute-done | bytes 65568 | tf_op jit(solution)/shard_map/ppermute | solution.py:170
  123.6 6.8 %fusion = f32[12,128,256]{2,1,0:T(8,128)} fusion(bf16[4352,256,1]{1,0,2:T(8,128)(2,1)} %bitcast.3, s32[4352]{0:T(1024)S(1)} %eq.80, s32[12,128]{1,0:T(8,128)S(1)} %multiply_add_fusion.1), kind=kOutput, calls=%fused_computation.4 | convolution fusion | flops 3429236736 | bytes 3824640 | tf_op jit(solution)/shard_map/dot_general | solution.py:113
  130.4 5.9 %all-to-all-start.1 = ((f32[12,128,256]{2,1,0:T(8,128)}), f32[12,128,256]{2,1,0:T(8,128)}, u32[]{:S(2)}, u32[]{:S(2)}) async-start(f32[12,128,256]{2,1,0:T(8,128)} %fusion), calls=%async_computation.1 | async-start | bytes 3145728 | tf_op jit(solution)/shard_map/all_to_all | solution.py:216
  136.3 2.4 collective-permute-start.7
  138.7 2.6 %collective-permute-done.7 = f32[32,512]{1,0:T(8,128)S(1)} collective-permute-done((f32[32,512]{1,0:T(8,128)S(1)}, f32[32,512]{1,0:T(8,128)S(1)}, u32[]{:S(2)}, u32[]{:S(2)}) %collective-permute-start.7) | collective-permute-done | bytes 65568 | tf_op jit(solution)/shard_map/ppermute | solution.py:152
  141.3 3.2 %collective-permute-start.8 = (f32[32,512]{1,0:T(8,128)S(1)}, f32[32,512]{1,0:T(8,128)S(1)}, u32[]{:S(2)}, u32[]{:S(2)}) collective-permute-start(f32[32,512]{1,0:T(8,128)S(1)} %add.145), channel_id=1, source_target_pairs={{0,4},{2,6},{4,0},{6,2},{8,12},{10,14},{12,8},{14,10},{1,5},{3,7},... | collective-permute-start | bytes 196616 | tf_op jit(solution)/shard_map/ppermute | solution.py:152
  144.5 3.8 %collective-permute-done.8 = f32[32,512]{1,0:T(8,128)S(1)} collective-permute-done((f32[32,512]{1,0:T(8,128)S(1)}, f32[32,512]{1,0:T(8,128)S(1)}, u32[]{:S(2)}, u32[]{:S(2)}) %collective-permute-start.8) | collective-permute-done | bytes 65568 | tf_op jit(solution)/shard_map/ppermute | solution.py:152
  148.3 6.2 %collective-permute-start.9 = (f32[32,512]{1,0:T(8,128)S(1)}, f32[32,512]{1,0:T(8,128)S(1)}, u32[]{:S(2)}, u32[]{:S(2)}) collective-permute-start(f32[32,512]{1,0:T(8,128)S(1)} %add.146), channel_id=1, source_target_pairs={{0,8},{2,10},{4,12},{6,14},{8,0},{10,2},{12,4},{14,6},{1,9},{3,11}... | collective-permute-start | bytes 196616 | tf_op jit(solution)/shard_map/ppermute | solution.py:152
  154.5 2.7 %collective-permute-done.9 = f32[32,512]{1,0:T(8,128)S(1)} collective-permute-done((f32[32,512]{1,0:T(8,128)S(1)}, f32[32,512]{1,0:T(8,128)S(1)}, u32[]{:S(2)}, u32[]{:S(2)}) %collective-permute-start.9) | collective-permute-done | bytes 65568 | tf_op jit(solution)/shard_map/ppermute | solution.py:152
  157.3 8.8 %collective-permute-start.10 = (f32[32,512]{1,0:T(8,128)S(1)}, f32[32,512]{1,0:T(8,128)S(1)}, u32[]{:S(2)}, u32[]{:S(2)}) collective-permute-start(f32[32,512]{1,0:T(8,128)S(1)} %add.147), channel_id=1, source_target_pairs={{0,32},{16,48},{32,0},{48,16},{1,33},{17,49},{33,1},{49,17},{2,34}... | collective-permute-start | bytes 196616 | tf_op jit(solution)/shard_map/ppermute | solution.py:152
  166.2 2.5 collective-permute-done.10
  171.8 6.7 %all-to-all-start.2 = ((f32[12,136,256]{2,1,0:T(8,128)}), f32[12,136,256]{2,1,0:T(8,128)}, u32[]{:S(2)}, u32[]{:S(2)}) async-start(f32[12,136,256]{2,1,0:T(8,128)} %copy-done.2), calls=%async_computation.2 | async-start | bytes 3342336 | tf_op jit(solution)/shard_map/all_to_all | solution.py:222
  178.4 10.6 %collective-permute-start.11 = (f32[64,512]{1,0:T(8,128)S(1)}, f32[64,512]{1,0:T(8,128)S(1)}, u32[]{:S(2)}, u32[]{:S(2)}) collective-permute-start(f32[64,512]{1,0:T(8,128)S(1)} %pad_maximum_fusion.4), channel_id=1, source_target_pairs={{0,16},{16,0},{32,48},{48,32},{1,17},{17,1},{33,49},{49,33},{2,18}... | collective-permute-start | bytes 393224 | tf_op jit(solution)/shard_map/ppermute | solution.py:152
  189.0 24.5 %collective-permute-done.11 = f32[64,512]{1,0:T(8,128)S(1)} collective-permute-done((f32[64,512]{1,0:T(8,128)S(1)}, f32[64,512]{1,0:T(8,128)S(1)}, u32[]{:S(2)}, u32[]{:S(2)}) %collective-permute-start.11) | collective-permute-done | bytes 131104 | tf_op jit(solution)/shard_map/ppermute | solution.py:152
  215.5 6.7 %collective-permute-done.12 = f32[128,512]{1,0:T(8,128)S(1)} collective-permute-done((f32[128,512]{1,0:T(8,128)S(1)}, f32[128,512]{1,0:T(8,128)S(1)}, u32[]{:S(2)}, u32[]{:S(2)}) %collective-permute-start.12) | collective-permute-done | bytes 262176 | tf_op jit(solution)/shard_map/ppermute | solution.py:152
  224.9 8.1 %collective-permute-done.13 = f32[256,512]{1,0:T(8,128)} collective-permute-done((f32[256,512]{1,0:T(8,128)S(1)}, f32[256,512]{1,0:T(8,128)}, u32[]{:S(2)}, u32[]{:S(2)}) %collective-permute-start.13) | collective-permute-done | bytes 524320 | tf_op jit(solution)/shard_map/ppermute | solution.py:152
  235.2 12.2 %collective-permute-start.14 = (f32[512,512]{1,0:T(8,128)}, f32[512,512]{1,0:T(8,128)}, u32[]{:S(2)}, u32[]{:S(2)}) collective-permute-start(f32[512,512]{1,0:T(8,128)} %pad_maximum_fusion.1), channel_id=1, source_target_pairs={{0,1},{1,0},{2,3},{3,2},{4,5},{5,4},{6,7},{7,6},{8,9},{9,8},{10,11... | collective-permute-start | bytes 3145736 | tf_op jit(solution)/shard_map/ppermute | solution.py:152
  247.5 2.6 %collective-permute-done.14 = f32[512,512]{1,0:T(8,128)} collective-permute-done((f32[512,512]{1,0:T(8,128)}, f32[512,512]{1,0:T(8,128)}, u32[]{:S(2)}, u32[]{:S(2)}) %collective-permute-start.14) | collective-permute-done | bytes 1048608 | tf_op jit(solution)/shard_map/ppermute | solution.py:152
  253.1 2.7 %slice.32 = f32[12,128,256]{2,1,0:T(8,128)} slice(f32[12,136,256]{2,1,0:T(8,128)} %all-to-all-done.2), slice={[0:12], [0:128], [0:256]} | slice | bytes 3145728 | tf_op jit(solution)/shard_map/slice | solution.py:227
  (81 shorter events, 36.8 us)
Async XLA Ops:
  0.6 93.7 %copy-start = (bf16[4096,256]{1,0:T(8,128)(2,1)S(1)}, bf16[4096,256]{1,0:T(8,128)(2,1)}, u32[]{:S(2)}) copy-start(bf16[4096,256]{1,0:T(8,128)(2,1)} %param.16) | copy-start | bytes 6291460
  3.8 41.9 %copy-start.9 = (bf16[128,512]{1,0:T(8,128)(2,1)S(1)}, bf16[128,512]{1,0:T(8,128)(2,1)}, u32[]{:S(2)}) copy-start(bf16[128,512]{1,0:T(8,128)(2,1)} %param.11) | copy-start | bytes 393220
  3.8 41.9 %copy-start.10 = (bf16[128,1024]{1,0:T(8,128)(2,1)S(1)}, bf16[128,1024]{1,0:T(8,128)(2,1)}, u32[]{:S(2)}) copy-start(bf16[128,1024]{1,0:T(8,128)(2,1)} %param.10) | copy-start | bytes 786436
  36.8 1.2 copy-start.3
  44.3 1.4 copy-start.1
  48.8 9.6 %collective-permute-start = (f32[512,512]{1,0:T(8,128)S(1)}, f32[512,512]{1,0:T(8,128)}, u32[]{:S(2)}, u32[]{:S(2)}) collective-permute-start(f32[512,512]{1,0:T(8,128)S(1)} %constant_dynamic-slice_fusion.4), channel_id=1, source_target_pairs={{0,1},{1,0},{2,3},{3,2},{4,5},{5,4},{6,7},{7,6},{8,9},{9,8},{10,11... | collective-permute-start | bytes 3145736 | tf_op jit(solution)/shard_map/ppermute | solution.py:152
  51.1 71.4 %all-to-all-start = ((bf16[16,272,256]{2,1,0:T(8,128)(2,1)}), bf16[16,272,256]{2,1,0:T(8,128)(2,1)}, u32[]{:S(2)}, u32[]{:S(2)}) async-start(bf16[16,272,256]{2,1,0:T(8,128)(2,1)} %copy-done.1), calls=%async_computation | async-start | bytes 4456448 | tf_op jit(solution)/shard_map/all_to_all | solution.py:201
  61.0 34.3 %copy-start.4 = (f32[4096]{0:T(1024)S(1)}, f32[4096]{0:T(1024)}, u32[]{:S(2)}) copy-start(f32[4096]{0:T(1024)} %param.18) | copy-start | bytes 49156
  61.0 15.7 %collective-permute-start.1 = (f32[256,512]{1,0:T(8,128)}, f32[256,512]{1,0:T(8,128)}, u32[]{:S(2)}, u32[]{:S(2)}) collective-permute-start(f32[256,512]{1,0:T(8,128)} %constant_dynamic-slice_fusion.3), channel_id=1, source_target_pairs={{0,192},{192,0},{384,576},{576,384},{1,193},{193,1},{385,577},{577... | collective-permute-start | bytes 1572872 | tf_op jit(solution)/shard_map/ppermute | solution.py:152
  63.9 32.5 %copy-start.5 = (f32[4096]{0:T(1024)S(1)}, f32[4096]{0:T(1024)}, u32[]{:S(2)}) copy-start(f32[4096]{0:T(1024)} %param.17) | copy-start | bytes 49156
  77.8 0.8 copy-start.8
  78.6 27.1 %copy-start.6 = (f32[4096]{0:T(1024)S(1)}, f32[4096]{0:T(1024)}, u32[]{:S(2)}) copy-start(f32[4096]{0:T(1024)} %param.19) | copy-start | bytes 49156
  78.6 10.3 %collective-permute-start.2 = (f32[128,512]{1,0:T(8,128)S(1)}, f32[128,512]{1,0:T(8,128)S(1)}, u32[]{:S(2)}, u32[]{:S(2)}) collective-permute-start(f32[128,512]{1,0:T(8,128)S(1)} %constant_dynamic-slice_fusion.2), channel_id=1, source_target_pairs={{0,384},{192,576},{384,0},{576,192},{1,385},{193,577},{385,1},{577... | collective-permute-start | bytes 786440 | tf_op jit(solution)/shard_map/ppermute | solution.py:152
  90.0 9.1 %collective-permute-start.3 = (f32[64,512]{1,0:T(8,128)S(1)}, f32[64,512]{1,0:T(8,128)S(1)}, u32[]{:S(2)}, u32[]{:S(2)}) collective-permute-start(f32[64,512]{1,0:T(8,128)S(1)} %constant_dynamic-slice_fusion.1), channel_id=1, source_target_pairs={{0,16},{16,0},{32,48},{48,32},{1,17},{17,1},{33,49},{49,33},{2,18}... | collective-permute-start | bytes 393224 | tf_op jit(solution)/shard_map/ppermute | solution.py:152
  99.2 11.3 %collective-permute-start.4 = (f32[32,512]{1,0:T(8,128)S(1)}, f32[32,512]{1,0:T(8,128)S(1)}, u32[]{:S(2)}, u32[]{:S(2)}) collective-permute-start(f32[32,512]{1,0:T(8,128)S(1)} %constant_dynamic-slice_fusion), channel_id=1, source_target_pairs={{0,32},{16,48},{32,0},{48,16},{1,33},{17,49},{33,1},{49,17},{2,34}... | collective-permute-start | bytes 196616 | tf_op jit(solution)/shard_map/ppermute | solution.py:152
  110.5 8.8 %collective-permute-start.5 = (f32[32,512]{1,0:T(8,128)S(1)}, f32[32,512]{1,0:T(8,128)S(1)}, u32[]{:S(2)}, u32[]{:S(2)}) collective-permute-start(f32[32,512]{1,0:T(8,128)S(1)} %dynamic-slice_add_fusion.4), channel_id=1, source_target_pairs={{0,64},{64,128},{128,0},{1,65},{65,129},{129,1},{2,66},{66,130},{1... | collective-permute-start | bytes 196616 | tf_op jit(solution)/shard_map/ppermute | solution.py:170
  117.2 5.3 %collective-permute-start.6 = (f32[32,512]{1,0:T(8,128)S(1)}, f32[32,512]{1,0:T(8,128)S(1)}, u32[]{:S(2)}, u32[]{:S(2)}) collective-permute-start(f32[32,512]{1,0:T(8,128)S(1)} %dynamic-slice_add_fusion.4), channel_id=1, source_target_pairs={{0,128},{64,0},{128,64},{1,129},{65,1},{129,65},{2,130},{66,2},{13... | collective-permute-start | bytes 196616 | tf_op jit(solution)/shard_map/ppermute | solution.py:170
  130.4 38.3 %all-to-all-start.1 = ((f32[12,128,256]{2,1,0:T(8,128)}), f32[12,128,256]{2,1,0:T(8,128)}, u32[]{:S(2)}, u32[]{:S(2)}) async-start(f32[12,128,256]{2,1,0:T(8,128)} %fusion), calls=%async_computation.1 | async-start | bytes 3145728 | tf_op jit(solution)/shard_map/all_to_all | solution.py:216
  136.3 5.0 %collective-permute-start.7 = (f32[32,512]{1,0:T(8,128)S(1)}, f32[32,512]{1,0:T(8,128)S(1)}, u32[]{:S(2)}, u32[]{:S(2)}) collective-permute-start(f32[32,512]{1,0:T(8,128)S(1)} %select_add_fusion), channel_id=1, source_target_pairs={{0,2},{2,0},{4,6},{6,4},{8,10},{10,8},{12,14},{14,12},{1,3},{3,1},... | collective-permute-start | bytes 196616 | tf_op jit(solution)/shard_map/ppermute | solution.py:152
  141.3 7.0 %collective-permute-start.8 = (f32[32,512]{1,0:T(8,128)S(1)}, f32[32,512]{1,0:T(8,128)S(1)}, u32[]{:S(2)}, u32[]{:S(2)}) collective-permute-start(f32[32,512]{1,0:T(8,128)S(1)} %add.145), channel_id=1, source_target_pairs={{0,4},{2,6},{4,0},{6,2},{8,12},{10,14},{12,8},{14,10},{1,5},{3,7},... | collective-permute-start | bytes 196616 | tf_op jit(solution)/shard_map/ppermute | solution.py:152
  148.3 8.9 %collective-permute-start.9 = (f32[32,512]{1,0:T(8,128)S(1)}, f32[32,512]{1,0:T(8,128)S(1)}, u32[]{:S(2)}, u32[]{:S(2)}) collective-permute-start(f32[32,512]{1,0:T(8,128)S(1)} %add.146), channel_id=1, source_target_pairs={{0,8},{2,10},{4,12},{6,14},{8,0},{10,2},{12,4},{14,6},{1,9},{3,11}... | collective-permute-start | bytes 196616 | tf_op jit(solution)/shard_map/ppermute | solution.py:152
  157.3 11.4 %collective-permute-start.10 = (f32[32,512]{1,0:T(8,128)S(1)}, f32[32,512]{1,0:T(8,128)S(1)}, u32[]{:S(2)}, u32[]{:S(2)}) collective-permute-start(f32[32,512]{1,0:T(8,128)S(1)} %add.147), channel_id=1, source_target_pairs={{0,32},{16,48},{32,0},{48,16},{1,33},{17,49},{33,1},{49,17},{2,34}... | collective-permute-start | bytes 196616 | tf_op jit(solution)/shard_map/ppermute | solution.py:152
  170.6 1.2 copy-start.2
  171.8 81.3 %all-to-all-start.2 = ((f32[12,136,256]{2,1,0:T(8,128)}), f32[12,136,256]{2,1,0:T(8,128)}, u32[]{:S(2)}, u32[]{:S(2)}) async-start(f32[12,136,256]{2,1,0:T(8,128)} %copy-done.2), calls=%async_computation.2 | async-start | bytes 3342336 | tf_op jit(solution)/shard_map/all_to_all | solution.py:222
  178.4 35.1 %collective-permute-start.11 = (f32[64,512]{1,0:T(8,128)S(1)}, f32[64,512]{1,0:T(8,128)S(1)}, u32[]{:S(2)}, u32[]{:S(2)}) collective-permute-start(f32[64,512]{1,0:T(8,128)S(1)} %pad_maximum_fusion.4), channel_id=1, source_target_pairs={{0,16},{16,0},{32,48},{48,32},{1,17},{17,1},{33,49},{49,33},{2,18}... | collective-permute-start | bytes 393224 | tf_op jit(solution)/shard_map/ppermute | solution.py:152
  213.6 8.6 %collective-permute-start.12 = (f32[128,512]{1,0:T(8,128)S(1)}, f32[128,512]{1,0:T(8,128)S(1)}, u32[]{:S(2)}, u32[]{:S(2)}) collective-permute-start(f32[128,512]{1,0:T(8,128)S(1)} %pad_maximum_fusion.3), channel_id=1, source_target_pairs={{0,384},{192,576},{384,0},{576,192},{1,385},{193,577},{385,1},{577... | collective-permute-start | bytes 786440 | tf_op jit(solution)/shard_map/ppermute | solution.py:152
  222.2 0.7 copy-start.7
  223.0 10.0 %collective-permute-start.13 = (f32[256,512]{1,0:T(8,128)S(1)}, f32[256,512]{1,0:T(8,128)}, u32[]{:S(2)}, u32[]{:S(2)}) collective-permute-start(f32[256,512]{1,0:T(8,128)S(1)} %pad_maximum_fusion.2), channel_id=1, source_target_pairs={{0,192},{192,0},{384,576},{576,384},{1,193},{193,1},{385,577},{577... | collective-permute-start | bytes 1572872 | tf_op jit(solution)/shard_map/ppermute | solution.py:152
  235.2 14.9 %collective-permute-start.14 = (f32[512,512]{1,0:T(8,128)}, f32[512,512]{1,0:T(8,128)}, u32[]{:S(2)}, u32[]{:S(2)}) collective-permute-start(f32[512,512]{1,0:T(8,128)} %pad_maximum_fusion.1), channel_id=1, source_target_pairs={{0,1},{1,0},{2,3},{3,2},{4,5},{5,4},{6,7},{7,6},{8,9},{9,8},{10,11... | collective-permute-start | bytes 3145736 | tf_op jit(solution)/shard_map/ppermute | solution.py:152

commit v4 on v3

--- a/solution.py
+++ b/solution.py
@@ -160,10 +160,28 @@
     return keep + swap(send, axis, size, bit)
 
 
-def double(a, axis, size, bit, dim):
-    other = swap(a, axis, size, bit)
-    first = (lax.axis_index(axis) & bit) == 0
-    return jnp.concatenate([jnp.where(first, a, other), jnp.where(first, other, a)], axis=dim)
+def scatter_sum(a, axis, size):
+    me = lax.axis_index(axis)
+    n = a.shape[0] // size
+
+    def block(k):
+        return lax.dynamic_slice_in_dim(a, lax.rem(me + k, size) * n, n, 0)
+
+    got = [shift(block(k), axis, size, k) for k in range(1, size)]
+    total = block(0)
+    for g in got:
+        total = total + g
+    return total
+
+
+def gather(a, axis, size):
+    me = lax.axis_index(axis)
+    n = a.shape[0]
+    got = [shift(a, axis, size, k) for k in range(1, size)]
+    out = jnp.concatenate([a] * size, axis=0)
+    for k, piece in enumerate(got, 1):
+        out = lax.dynamic_update_slice_in_dim(out, piece, lax.rem(me - k + size, size) * n, 0)
+    return out
 
 
 def shift(a, axis, size, k):
@@ -201,10 +219,8 @@
     got = lax.all_to_all(rows, ("y", "c"), 0, 0, tiled=True)
     w = lax.dot_general(pooled, layer_grad, (((0,), (0,)), ((), ())), preferred_element_type=f32)
     w = halve(w, "c", NC, 1, 0)
-    w = halve(w, "x", NX, 1, 0)
-    w = halve(w, "x", NX, 2, 0)
-    w = halve(w, "zh", NZH, 1, 0)
-    w = halve(w, "zh", NZH, 2, 0)
+    w = scatter_sum(w, "x", NX)
+    w = scatter_sum(w, "zh", NZH)
     w = sum_over_three(w)
     mine = lax.axis_index("x") * NZL + lax.axis_index("zl")
     local = lax.dynamic_slice_in_dim(touched, mine * part, part, 0)
@@ -216,14 +232,12 @@
     sums = lax.all_to_all(sums, REP, 0, 0, tiled=True)
     for bit in (1, 2, 4):
         w = w + swap(w, "y", NY, bit)
-    w = double(w, "zh", NZH, 2, 0)
     sums, w = tie(sums, w)
 
     payload = lax.all_to_all(update(sums, old, old_accum), REP, 0, 0, tiled=True)
-    w = double(w, "zh", NZH, 1, 0)
-    w = double(w, "x", NX, 2, 0)
-    w = double(w, "x", NX, 1, 0)
-    weight_grad = double(w, "c", NC, 1, 0)
+    w = gather(w, "zh", NZH)
+    w = gather(w, "x", NX)
+    weight_grad = gather(w, "c", NC)
     new_codes = payload[:, :part].reshape(touch, width)
     new_scale, lowest, new_accum = (payload[:, part + i, :part].reshape(touch) for i in range(3))
     return (weight_grad, new_codes, new_scale, lowest, new_accum)

time: 259 us -> 226 us (0.87)
  the two profiles are of different devices: /device:TPU:69 before, /device:TPU:1 now
where the time goes in v4:
time: 226 us; the launch traced here: 222 us
  starting transfers between devices  111 us (49%)
  blocking collectives  33.5 us (15%)
  waiting for transfers between devices  32.8 us (15%)
  local copies, waits for them, and re-layouts  18.6 us (8%)
  other arithmetic  9.08 us (4%)
  Pallas kernels  8.14 us (4%)
  matrix products  7.23 us (3%)
    ppermute x15, starting transfers between devices, shift(): return lax.ppermute(a, axis, [(i, (i + k) % size) for i in range(size)])  77.1 us
    all_gather x1, blocking collectives, shards(): near = lax.all_gather(near, 'zh', axis=0, tiled=False)  33.5 us
    ppermute x15, waiting for transfers between devices, shift(): return lax.ppermute(a, axis, [(i, (i + k) % size) for i in range(size)])  23 us
    ppermute x4, starting transfers between devices, swap(): return lax.ppermute(a, axis, [(i, i ^ bit) for i in range(size)])  17 us
    ppermute x4, waiting for transfers between devices, swap(): return lax.ppermute(a, axis, [(i, i ^ bit) for i in range(size)])  8.85 us
    all_to_all x1, starting transfers between devices, shards(): got = lax.all_to_all(rows, ('y', 'c'), 0, 0, tiled=True)  7.61 us
    dot_general x1, matrix products, collect(): return jnp.dot(selector, got.reshape(-1, width), preferred_element_type=f32)  6.77 us
    pallas_call x1, Pallas kernels, dispatch(): pl.pallas_call(lambda *refs: dispatch_kernel(here, cap, *refs), out_shape...  6.3 us
  transfers between devices with their start and end apart: 22, of which 12 were waited for; matrix products, arithmetic and copies ran while one was open for 6% of the time, Pallas kernels for 0%

profile of v4, /device:TPU:1, one launch (start us, length us, event | category | flops | bytes accessed | tf_op | source)
XLA Modules:
  0.0 221.9 jit_solution(3628914065591828806)
XLA Ops:
  3.8 33.5 %all-gather = bf16[512,640]{1,0:T(8,128)(2,1)S(1)} all-gather(bf16[128,640]{1,0:T(8,128)(2,1)S(1)} %fusion.5), channel_id=2, replica_groups=mesh['x'=4,'zl'=3,'zh'=4,'y'=8,'c'=2] {'zh'}, dimensions={0}, use_global_device_ids=true | all-gather | bytes 819200 | tf_op jit(solution)/shard_map/all_gather | solution.py:216
  38.5 6.3 %dispatch.1 = bf16[16,272,256]{2,1,0:T(8,128)(2,1)S(1)} custom-call(s32[1]{0:T(128)} %bitcast.refs_0_, bf16[4,128,640]{2,1,0:T(8,128)(2,1)S(1)} %bitcast.16, bf16[1024,512]{1,0:T(8,128)(2,1)S(1)} %copy-done.3), custom_call_target="tpu_custom_call" | custom-call | tf_op jit(solution)/shard_map/dispatch/pallas_call | solution.py:96
  46.2 7.6 %all-to-all-start = ((bf16[16,272,256]{2,1,0:T(8,128)(2,1)}), bf16[16,272,256]{2,1,0:T(8,128)(2,1)}, u32[]{:S(2)}, u32[]{:S(2)}) async-start(bf16[16,272,256]{2,1,0:T(8,128)(2,1)} %copy-done.1), calls=%async_computation | async-start | bytes 4456448 | tf_op jit(solution)/shard_map/all_to_all | solution.py:219
  57.8 2.6 %collective-permute-done = f32[512,512]{1,0:T(8,128)} collective-permute-done((f32[512,512]{1,0:T(8,128)S(1)}, f32[512,512]{1,0:T(8,128)}, u32[]{:S(2)}, u32[]{:S(2)}) %collective-permute-start) | collective-permute-done | bytes 1048608 | tf_op jit(solution)/shard_map/ppermute | solution.py:152
  63.1 3.2 %collective-permute-start.1 = (f32[128,512]{1,0:T(8,128)}, f32[128,512]{1,0:T(8,128)S(1)}, u32[]{:S(2)}, u32[]{:S(2)}) collective-permute-start(f32[128,512]{1,0:T(8,128)} %get-tuple-element.24), channel_id=1, source_target_pairs={{0,192},{192,384},{384,576},{576,0},{1,193},{193,385},{385,577},{5... | collective-permute-start | bytes 786440 | tf_op jit(solution)/shard_map/ppermute | solution.py:188
  66.3 3.4 %collective-permute-start.3 = (f32[128,512]{1,0:T(8,128)}, f32[128,512]{1,0:T(8,128)}, u32[]{:S(2)}, u32[]{:S(2)}) collective-permute-start(f32[128,512]{1,0:T(8,128)} %get-tuple-element.25), channel_id=1, source_target_pairs={{0,576},{192,0},{384,192},{576,384},{1,577},{193,1},{385,193},{577... | collective-permute-start | bytes 786440 | tf_op jit(solution)/shard_map/ppermute | solution.py:188
  69.7 3.4 %collective-permute-start.2 = (f32[128,512]{1,0:T(8,128)}, f32[128,512]{1,0:T(8,128)}, u32[]{:S(2)}, u32[]{:S(2)}) collective-permute-start(f32[128,512]{1,0:T(8,128)} %get-tuple-element.26), channel_id=1, source_target_pairs={{0,384},{192,576},{384,0},{576,192},{1,385},{193,577},{385,1},{577... | collective-permute-start | bytes 786440 | tf_op jit(solution)/shard_map/ppermute | solution.py:188
  77.9 2.6 %collective-permute-done.2 = f32[128,512]{1,0:T(8,128)} collective-permute-done((f32[128,512]{1,0:T(8,128)}, f32[128,512]{1,0:T(8,128)}, u32[]{:S(2)}, u32[]{:S(2)}) %collective-permute-start.2) | collective-permute-done | bytes 262176 | tf_op jit(solution)/shard_map/ppermute | solution.py:188
  81.8 4.0 %collective-permute-start.4 = (f32[32,512]{1,0:T(8,128)S(1)}, f32[32,512]{1,0:T(8,128)S(1)}, u32[]{:S(2)}, u32[]{:S(2)}) collective-permute-start(f32[32,512]{1,0:T(8,128)S(1)} %get-tuple-element.27), channel_id=1, source_target_pairs={{0,16},{16,32},{32,48},{48,0},{1,17},{17,33},{33,49},{49,1},{2,18}... | collective-permute-start | bytes 196616 | tf_op jit(solution)/shard_map/ppermute | solution.py:188
  85.8 4.3 %collective-permute-start.6 = (f32[32,512]{1,0:T(8,128)S(1)}, f32[32,512]{1,0:T(8,128)S(1)}, u32[]{:S(2)}, u32[]{:S(2)}) collective-permute-start(f32[32,512]{1,0:T(8,128)S(1)} %get-tuple-element.28), channel_id=1, source_target_pairs={{0,48},{16,0},{32,16},{48,32},{1,49},{17,1},{33,17},{49,33},{2,50}... | collective-permute-start | bytes 196616 | tf_op jit(solution)/shard_map/ppermute | solution.py:188
  90.1 5.8 %collective-permute-start.5 = (f32[32,512]{1,0:T(8,128)S(1)}, f32[32,512]{1,0:T(8,128)S(1)}, u32[]{:S(2)}, u32[]{:S(2)}) collective-permute-start(f32[32,512]{1,0:T(8,128)S(1)} %get-tuple-element.29), channel_id=1, source_target_pairs={{0,32},{16,48},{32,0},{48,16},{1,33},{17,49},{33,1},{49,17},{2,34}... | collective-permute-start | bytes 196616 | tf_op jit(solution)/shard_map/ppermute | solution.py:188
  97.2 4.2 %collective-permute-done.5 = f32[32,512]{1,0:T(8,128)S(1)} collective-permute-done((f32[32,512]{1,0:T(8,128)S(1)}, f32[32,512]{1,0:T(8,128)S(1)}, u32[]{:S(2)}, u32[]{:S(2)}) %collective-permute-start.5) | collective-permute-done | bytes 65568 | tf_op jit(solution)/shard_map/ppermute | solution.py:188
  101.4 5.6 %collective-permute-start.8 = (f32[32,512]{1,0:T(8,128)S(1)}, f32[32,512]{1,0:T(8,128)S(1)}, u32[]{:S(2)}, u32[]{:S(2)}) collective-permute-start(f32[32,512]{1,0:T(8,128)S(1)} %add_add_fusion.1), channel_id=1, source_target_pairs={{0,128},{64,0},{128,64},{1,129},{65,1},{129,65},{2,130},{66,2},{13... | collective-permute-start | bytes 196616 | tf_op jit(solution)/shard_map/ppermute | solution.py:188
  109.2 3.8 %collective-permute-done.7 = f32[32,512]{1,0:T(8,128)S(1)} collective-permute-done((f32[32,512]{1,0:T(8,128)S(1)}, f32[32,512]{1,0:T(8,128)S(1)}, u32[]{:S(2)}, u32[]{:S(2)}) %collective-permute-start.7) | collective-permute-done | bytes 65568 | tf_op jit(solution)/shard_map/ppermute | solution.py:188
  114.1 6.8 %fusion = f32[12,128,256]{2,1,0:T(8,128)} fusion(bf16[4352,256,1]{1,0,2:T(8,128)(2,1)} %bitcast.3, s32[4352]{0:T(1024)S(1)} %eq.61, s32[12,128]{1,0:T(8,128)S(1)} %multiply_add_fusion.1), kind=kOutput, calls=%fused_computation.4 | convolution fusion | flops 3429236736 | bytes 3824640 | tf_op jit(solution)/shard_map/dot_general | solution.py:113
  120.8 4.8 %all-to-all-start.1 = ((f32[12,128,256]{2,1,0:T(8,128)}), f32[12,128,256]{2,1,0:T(8,128)}, u32[]{:S(2)}, u32[]{:S(2)}) async-start(f32[12,128,256]{2,1,0:T(8,128)} %fusion), calls=%async_computation.1 | async-start | bytes 3145728 | tf_op jit(solution)/shard_map/all_to_all | solution.py:232
  125.7 3.2 %collective-permute-start.9 = (f32[32,512]{1,0:T(8,128)S(1)}, f32[32,512]{1,0:T(8,128)S(1)}, u32[]{:S(2)}, u32[]{:S(2)}) collective-permute-start(f32[32,512]{1,0:T(8,128)S(1)} %select_add_fusion), channel_id=1, source_target_pairs={{0,2},{2,0},{4,6},{6,4},{8,10},{10,8},{12,14},{14,12},{1,3},{3,1},... | collective-permute-start | bytes 196616 | tf_op jit(solution)/shard_map/ppermute | solution.py:152
  130.7 4.1 %collective-permute-start.10 = (f32[32,512]{1,0:T(8,128)S(1)}, f32[32,512]{1,0:T(8,128)S(1)}, u32[]{:S(2)}, u32[]{:S(2)}) collective-permute-start(f32[32,512]{1,0:T(8,128)S(1)} %add.212), channel_id=1, source_target_pairs={{0,4},{2,6},{4,0},{6,2},{8,12},{10,14},{12,8},{14,10},{1,5},{3,7},... | collective-permute-start | bytes 196616 | tf_op jit(solution)/shard_map/ppermute | solution.py:152
  134.8 2.2 %collective-permute-done.10 = f32[32,512]{1,0:T(8,128)S(1)} collective-permute-done((f32[32,512]{1,0:T(8,128)S(1)}, f32[32,512]{1,0:T(8,128)S(1)}, u32[]{:S(2)}, u32[]{:S(2)}) %collective-permute-start.10) | collective-permute-done | bytes 65568 | tf_op jit(solution)/shard_map/ppermute | solution.py:152
  137.0 7.8 %collective-permute-start.11 = (f32[32,512]{1,0:T(8,128)S(1)}, f32[32,512]{1,0:T(8,128)S(1)}, u32[]{:S(2)}, u32[]{:S(2)}) collective-permute-start(f32[32,512]{1,0:T(8,128)S(1)} %add.213), channel_id=1, source_target_pairs={{0,8},{2,10},{4,12},{6,14},{8,0},{10,2},{12,4},{14,6},{1,9},{3,11}... | collective-permute-start | bytes 196616 | tf_op jit(solution)/shard_map/ppermute | solution.py:152
  144.9 2.2 collective-permute-done.11
  151.1 4.6 %all-to-all-start.2 = ((f32[12,136,256]{2,1,0:T(8,128)}), f32[12,136,256]{2,1,0:T(8,128)}, u32[]{:S(2)}, u32[]{:S(2)}) async-start(f32[12,136,256]{2,1,0:T(8,128)} %copy-done.2), calls=%async_computation.2 | async-start | bytes 3342336 | tf_op jit(solution)/shard_map/all_to_all | solution.py:237
  155.7 4.0 %collective-permute-start.14 = (f32[32,512]{1,0:T(8,128)S(1)}, f32[32,512]{1,0:T(8,128)S(1)}, u32[]{:S(2)}, u32[]{:S(2)}) collective-permute-start(f32[32,512]{1,0:T(8,128)S(1)} %add.214), channel_id=1, source_target_pairs={{0,48},{16,0},{32,16},{48,32},{1,49},{17,1},{33,17},{49,33},{2,50}... | collective-permute-start | bytes 196616 | tf_op jit(solution)/shard_map/ppermute | solution.py:188
  159.7 13.3 %collective-permute-start.13 = (f32[32,512]{1,0:T(8,128)S(1)}, f32[32,512]{1,0:T(8,128)S(1)}, u32[]{:S(2)}, u32[]{:S(2)}) collective-permute-start(f32[32,512]{1,0:T(8,128)S(1)} %add.214), channel_id=1, source_target_pairs={{0,32},{16,48},{32,0},{48,16},{1,33},{17,49},{33,1},{49,17},{2,34}... | collective-permute-start | bytes 196616 | tf_op jit(solution)/shard_map/ppermute | solution.py:188
  175.0 7.9 %collective-permute-done.12 = f32[32,512]{1,0:T(8,128)S(1)} collective-permute-done((f32[32,512]{1,0:T(8,128)S(1)}, f32[32,512]{1,0:T(8,128)S(1)}, u32[]{:S(2)}, u32[]{:S(2)}) %collective-permute-start.12) | collective-permute-done | bytes 65568 | tf_op jit(solution)/shard_map/ppermute | solution.py:188
  182.9 3.5 %collective-permute-start.15 = (f32[128,512]{1,0:T(8,128)S(1)}, f32[128,512]{1,0:T(8,128)S(1)}, u32[]{:S(2)}, u32[]{:S(2)}) collective-permute-start(f32[128,512]{1,0:T(8,128)S(1)} %constant_dynamic-update-slice_fusion.4), channel_id=1, source_target_pairs={{0,192},{192,384},{384,576},{576,0},{1,193},{193,385},{385,577},{5... | collective-permute-start | bytes 786440 | tf_op jit(solution)/shard_map/ppermute | solution.py:188
  186.5 4.3 %collective-permute-start.16 = (f32[128,512]{1,0:T(8,128)S(1)}, f32[128,512]{1,0:T(8,128)S(1)}, u32[]{:S(2)}, u32[]{:S(2)}) collective-permute-start(f32[128,512]{1,0:T(8,128)S(1)} %constant_dynamic-update-slice_fusion.4), channel_id=1, source_target_pairs={{0,384},{192,576},{384,0},{576,192},{1,385},{193,577},{385,1},{577... | collective-permute-start | bytes 786440 | tf_op jit(solution)/shard_map/ppermute | solution.py:188
  190.8 3.2 %collective-permute-start.17 = (f32[128,512]{1,0:T(8,128)S(1)}, f32[128,512]{1,0:T(8,128)S(1)}, u32[]{:S(2)}, u32[]{:S(2)}) collective-permute-start(f32[128,512]{1,0:T(8,128)S(1)} %constant_dynamic-update-slice_fusion.4), channel_id=1, source_target_pairs={{0,576},{192,0},{384,192},{576,384},{1,577},{193,1},{385,193},{577... | collective-permute-start | bytes 786440 | tf_op jit(solution)/shard_map/ppermute | solution.py:188
  195.5 2.5 %collective-permute-done.17 = f32[128,512]{1,0:T(8,128)S(1)} collective-permute-done((f32[128,512]{1,0:T(8,128)S(1)}, f32[128,512]{1,0:T(8,128)S(1)}, u32[]{:S(2)}, u32[]{:S(2)}) %collective-permute-start.17) | collective-permute-done | bytes 262176 | tf_op jit(solution)/shard_map/ppermute | solution.py:188
  197.9 15.0 %collective-permute-start.18 = (f32[512,512]{1,0:T(8,128)S(1)}, f32[512,512]{1,0:T(8,128)}, u32[]{:S(2)}, u32[]{:S(2)}) collective-permute-start(f32[512,512]{1,0:T(8,128)S(1)} %constant_dynamic-update-slice_fusion.1), channel_id=1, source_target_pairs={{0,1},{1,0},{2,3},{3,2},{4,5},{5,4},{6,7},{7,6},{8,9},{9,8},{10,11... | collective-permute-start | bytes 3145736 | tf_op jit(solution)/shard_map/ppermute | solution.py:188
  215.3 2.3 %constant_dynamic-update-slice_fusion = f32[1024,512]{1,0:T(8,128)} fusion(f32[1024,512]{1,0:T(8,128)} %pad_maximum_fusion, f32[512,512]{1,0:T(8,128)} %collective-permute-done.18, s32[]{:T(128)S(6)} %select_n.133), kind=kLoop, calls=%fused_computation.29 | loop fusion | bytes 2097156 | tf_op jit(solution)/shard_map/dynamic_update_slice | solution.py:183
  219.2 2.7 %slice.32 = f32[12,128,256]{2,1,0:T(8,128)} slice(f32[12,136,256]{2,1,0:T(8,128)} %all-to-all-done.2), slice={[0:12], [0:128], [0:256]} | slice | bytes 3145728 | tf_op jit(solution)/shard_map/slice | solution.py:241
  (85 shorter events, 36.0 us)
Async XLA Ops:
  0.6 75.7 %copy-start = (bf16[4096,256]{1,0:T(8,128)(2,1)S(1)}, bf16[4096,256]{1,0:T(8,128)(2,1)}, u32[]{:S(2)}) copy-start(bf16[4096,256]{1,0:T(8,128)(2,1)} %param.16) | copy-start | bytes 6291460
  37.3 1.2 copy-start.3
  44.9 1.4 copy-start.1
  46.2 7.6 %copy-start.8 = (bf16[128,512]{1,0:T(8,128)(2,1)S(1)}, bf16[128,512]{1,0:T(8,128)(2,1)}, u32[]{:S(2)}) copy-start(bf16[128,512]{1,0:T(8,128)(2,1)} %param.11) | copy-start | bytes 393220
  46.2 7.6 %copy-start.9 = (bf16[128,1024]{1,0:T(8,128)(2,1)S(1)}, bf16[128,1024]{1,0:T(8,128)(2,1)}, u32[]{:S(2)}) copy-start(bf16[128,1024]{1,0:T(8,128)(2,1)} %param.10) | copy-start | bytes 786436
  46.2 66.7 %all-to-all-start = ((bf16[16,272,256]{2,1,0:T(8,128)(2,1)}), bf16[16,272,256]{2,1,0:T(8,128)(2,1)}, u32[]{:S(2)}, u32[]{:S(2)}) async-start(bf16[16,272,256]{2,1,0:T(8,128)(2,1)} %copy-done.1), calls=%async_computation | async-start | bytes 4456448 | tf_op jit(solution)/shard_map/all_to_all | solution.py:219
  54.3 1.3 copy-start.7
  55.7 4.7 %collective-permute-start = (f32[512,512]{1,0:T(8,128)S(1)}, f32[512,512]{1,0:T(8,128)}, u32[]{:S(2)}, u32[]{:S(2)}) collective-permute-start(f32[512,512]{1,0:T(8,128)S(1)} %constant_dynamic-slice_fusion.6), channel_id=1, source_target_pairs={{0,1},{1,0},{2,3},{3,2},{4,5},{5,4},{6,7},{7,6},{8,9},{9,8},{10,11... | collective-permute-start | bytes 3145736 | tf_op jit(solution)/shard_map/ppermute | solution.py:152
  57.8 16.2 %copy-start.4 = (f32[4096]{0:T(1024)S(1)}, f32[4096]{0:T(1024)}, u32[]{:S(2)}) copy-start(f32[4096]{0:T(1024)} %param.18) | copy-start | bytes 49156
  57.8 17.3 %copy-start.5 = (f32[4096]{0:T(1024)S(1)}, f32[4096]{0:T(1024)}, u32[]{:S(2)}) copy-start(f32[4096]{0:T(1024)} %param.17) | copy-start | bytes 49156
  63.1 33.0 %copy-start.6 = (f32[4096]{0:T(1024)S(1)}, f32[4096]{0:T(1024)}, u32[]{:S(2)}) copy-start(f32[4096]{0:T(1024)} %param.19) | copy-start | bytes 49156
  63.1 14.1 %collective-permute-start.1 = (f32[128,512]{1,0:T(8,128)}, f32[128,512]{1,0:T(8,128)S(1)}, u32[]{:S(2)}, u32[]{:S(2)}) collective-permute-start(f32[128,512]{1,0:T(8,128)} %get-tuple-element.24), channel_id=1, source_target_pairs={{0,192},{192,384},{384,576},{576,0},{1,193},{193,385},{385,577},{5... | collective-permute-start | bytes 786440 | tf_op jit(solution)/shard_map/ppermute | solution.py:188
  66.3 10.9 %collective-permute-start.3 = (f32[128,512]{1,0:T(8,128)}, f32[128,512]{1,0:T(8,128)}, u32[]{:S(2)}, u32[]{:S(2)}) collective-permute-start(f32[128,512]{1,0:T(8,128)} %get-tuple-element.25), channel_id=1, source_target_pairs={{0,576},{192,0},{384,192},{576,384},{1,577},{193,1},{385,193},{577... | collective-permute-start | bytes 786440 | tf_op jit(solution)/shard_map/ppermute | solution.py:188
  69.7 10.8 %collective-permute-start.2 = (f32[128,512]{1,0:T(8,128)}, f32[128,512]{1,0:T(8,128)}, u32[]{:S(2)}, u32[]{:S(2)}) collective-permute-start(f32[128,512]{1,0:T(8,128)} %get-tuple-element.26), channel_id=1, source_target_pairs={{0,384},{192,576},{384,0},{576,192},{1,385},{193,577},{385,1},{577... | collective-permute-start | bytes 786440 | tf_op jit(solution)/shard_map/ppermute | solution.py:188
  81.8 15.4 %collective-permute-start.4 = (f32[32,512]{1,0:T(8,128)S(1)}, f32[32,512]{1,0:T(8,128)S(1)}, u32[]{:S(2)}, u32[]{:S(2)}) collective-permute-start(f32[32,512]{1,0:T(8,128)S(1)} %get-tuple-element.27), channel_id=1, source_target_pairs={{0,16},{16,32},{32,48},{48,0},{1,17},{17,33},{33,49},{49,1},{2,18}... | collective-permute-start | bytes 196616 | tf_op jit(solution)/shard_map/ppermute | solution.py:188
  85.8 11.4 %collective-permute-start.6 = (f32[32,512]{1,0:T(8,128)S(1)}, f32[32,512]{1,0:T(8,128)S(1)}, u32[]{:S(2)}, u32[]{:S(2)}) collective-permute-start(f32[32,512]{1,0:T(8,128)S(1)} %get-tuple-element.28), channel_id=1, source_target_pairs={{0,48},{16,0},{32,16},{48,32},{1,49},{17,1},{33,17},{49,33},{2,50}... | collective-permute-start | bytes 196616 | tf_op jit(solution)/shard_map/ppermute | solution.py:188
  90.1 11.3 %collective-permute-start.5 = (f32[32,512]{1,0:T(8,128)S(1)}, f32[32,512]{1,0:T(8,128)S(1)}, u32[]{:S(2)}, u32[]{:S(2)}) collective-permute-start(f32[32,512]{1,0:T(8,128)S(1)} %get-tuple-element.29), channel_id=1, source_target_pairs={{0,32},{16,48},{32,0},{48,16},{1,33},{17,49},{33,1},{49,17},{2,34}... | collective-permute-start | bytes 196616 | tf_op jit(solution)/shard_map/ppermute | solution.py:188
  101.4 7.7 %collective-permute-start.8 = (f32[32,512]{1,0:T(8,128)S(1)}, f32[32,512]{1,0:T(8,128)S(1)}, u32[]{:S(2)}, u32[]{:S(2)}) collective-permute-start(f32[32,512]{1,0:T(8,128)S(1)} %add_add_fusion.1), channel_id=1, source_target_pairs={{0,128},{64,0},{128,64},{1,129},{65,1},{129,65},{2,130},{66,2},{13... | collective-permute-start | bytes 196616 | tf_op jit(solution)/shard_map/ppermute | solution.py:188
  107.0 5.9 %collective-permute-start.7 = (f32[32,512]{1,0:T(8,128)S(1)}, f32[32,512]{1,0:T(8,128)S(1)}, u32[]{:S(2)}, u32[]{:S(2)}) collective-permute-start(f32[32,512]{1,0:T(8,128)S(1)} %add_add_fusion.1), channel_id=1, source_target_pairs={{0,64},{64,128},{128,0},{1,65},{65,129},{129,1},{2,66},{66,130},{1... | collective-permute-start | bytes 196616 | tf_op jit(solution)/shard_map/ppermute | solution.py:188
  120.8 27.2 %all-to-all-start.1 = ((f32[12,128,256]{2,1,0:T(8,128)}), f32[12,128,256]{2,1,0:T(8,128)}, u32[]{:S(2)}, u32[]{:S(2)}) async-start(f32[12,128,256]{2,1,0:T(8,128)} %fusion), calls=%async_computation.1 | async-start | bytes 3145728 | tf_op jit(solution)/shard_map/all_to_all | solution.py:232
  125.7 5.0 %collective-permute-start.9 = (f32[32,512]{1,0:T(8,128)S(1)}, f32[32,512]{1,0:T(8,128)S(1)}, u32[]{:S(2)}, u32[]{:S(2)}) collective-permute-start(f32[32,512]{1,0:T(8,128)S(1)} %select_add_fusion), channel_id=1, source_target_pairs={{0,2},{2,0},{4,6},{6,4},{8,10},{10,8},{12,14},{14,12},{1,3},{3,1},... | collective-permute-start | bytes 196616 | tf_op jit(solution)/shard_map/ppermute | solution.py:152
  130.7 6.3 %collective-permute-start.10 = (f32[32,512]{1,0:T(8,128)S(1)}, f32[32,512]{1,0:T(8,128)S(1)}, u32[]{:S(2)}, u32[]{:S(2)}) collective-permute-start(f32[32,512]{1,0:T(8,128)S(1)} %add.212), channel_id=1, source_target_pairs={{0,4},{2,6},{4,0},{6,2},{8,12},{10,14},{12,8},{14,10},{1,5},{3,7},... | collective-permute-start | bytes 196616 | tf_op jit(solution)/shard_map/ppermute | solution.py:152
  137.0 10.1 %collective-permute-start.11 = (f32[32,512]{1,0:T(8,128)S(1)}, f32[32,512]{1,0:T(8,128)S(1)}, u32[]{:S(2)}, u32[]{:S(2)}) collective-permute-start(f32[32,512]{1,0:T(8,128)S(1)} %add.213), channel_id=1, source_target_pairs={{0,8},{2,10},{4,12},{6,14},{8,0},{10,2},{12,4},{14,6},{1,9},{3,11}... | collective-permute-start | bytes 196616 | tf_op jit(solution)/shard_map/ppermute | solution.py:152
  149.9 1.2 copy-start.2
  151.1 66.5 %all-to-all-start.2 = ((f32[12,136,256]{2,1,0:T(8,128)}), f32[12,136,256]{2,1,0:T(8,128)}, u32[]{:S(2)}, u32[]{:S(2)}) async-start(f32[12,136,256]{2,1,0:T(8,128)} %copy-done.2), calls=%async_computation.2 | async-start | bytes 3342336 | tf_op jit(solution)/shard_map/all_to_all | solution.py:237
  155.7 27.1 %collective-permute-start.14 = (f32[32,512]{1,0:T(8,128)S(1)}, f32[32,512]{1,0:T(8,128)S(1)}, u32[]{:S(2)}, u32[]{:S(2)}) collective-permute-start(f32[32,512]{1,0:T(8,128)S(1)} %add.214), channel_id=1, source_target_pairs={{0,48},{16,0},{32,16},{48,32},{1,49},{17,1},{33,17},{49,33},{2,50}... | collective-permute-start | bytes 196616 | tf_op jit(solution)/shard_map/ppermute | solution.py:188
  159.7 23.1 %collective-permute-start.13 = (f32[32,512]{1,0:T(8,128)S(1)}, f32[32,512]{1,0:T(8,128)S(1)}, u32[]{:S(2)}, u32[]{:S(2)}) collective-permute-start(f32[32,512]{1,0:T(8,128)S(1)} %add.214), channel_id=1, source_target_pairs={{0,32},{16,48},{32,0},{48,16},{1,33},{17,49},{33,1},{49,17},{2,34}... | collective-permute-start | bytes 196616 | tf_op jit(solution)/shard_map/ppermute | solution.py:188
  173.0 9.8 %collective-permute-start.12 = (f32[32,512]{1,0:T(8,128)S(1)}, f32[32,512]{1,0:T(8,128)S(1)}, u32[]{:S(2)}, u32[]{:S(2)}) collective-permute-start(f32[32,512]{1,0:T(8,128)S(1)} %add.214), channel_id=1, source_target_pairs={{0,16},{16,32},{32,48},{48,0},{1,17},{17,33},{33,49},{49,1},{2,18}... | collective-permute-start | bytes 196616 | tf_op jit(solution)/shard_map/ppermute | solution.py:188
  182.9 11.2 %collective-permute-start.15 = (f32[128,512]{1,0:T(8,128)S(1)}, f32[128,512]{1,0:T(8,128)S(1)}, u32[]{:S(2)}, u32[]{:S(2)}) collective-permute-start(f32[128,512]{1,0:T(8,128)S(1)} %constant_dynamic-update-slice_fusion.4), channel_id=1, source_target_pairs={{0,192},{192,384},{384,576},{576,0},{1,193},{193,385},{385,577},{5... | collective-permute-start | bytes 786440 | tf_op jit(solution)/shard_map/ppermute | solution.py:188
  186.5 9.0 %collective-permute-start.16 = (f32[128,512]{1,0:T(8,128)S(1)}, f32[128,512]{1,0:T(8,128)S(1)}, u32[]{:S(2)}, u32[]{:S(2)}) collective-permute-start(f32[128,512]{1,0:T(8,128)S(1)} %constant_dynamic-update-slice_fusion.4), channel_id=1, source_target_pairs={{0,384},{192,576},{384,0},{576,192},{1,385},{193,577},{385,1},{577... | collective-permute-start | bytes 786440 | tf_op jit(solution)/shard_map/ppermute | solution.py:188
  190.8 7.1 %collective-permute-start.17 = (f32[128,512]{1,0:T(8,128)S(1)}, f32[128,512]{1,0:T(8,128)S(1)}, u32[]{:S(2)}, u32[]{:S(2)}) collective-permute-start(f32[128,512]{1,0:T(8,128)S(1)} %constant_dynamic-update-slice_fusion.4), channel_id=1, source_target_pairs={{0,576},{192,0},{384,192},{576,384},{1,577},{193,1},{385,193},{577... | collective-permute-start | bytes 786440 | tf_op jit(solution)/shard_map/ppermute | solution.py:188
  197.9 17.4 %collective-permute-start.18 = (f32[512,512]{1,0:T(8,128)S(1)}, f32[512,512]{1,0:T(8,128)}, u32[]{:S(2)}, u32[]{:S(2)}) collective-permute-start(f32[512,512]{1,0:T(8,128)S(1)} %constant_dynamic-update-slice_fusion.1), channel_id=1, source_target_pairs={{0,1},{1,0},{2,3},{3,2},{4,5},{5,4},{6,7},{7,6},{8,9},{9,8},{10,11... | collective-permute-start | bytes 3145736 | tf_op jit(solution)/shard_map/ppermute | solution.py:188
  (1 other events, 0.7 us)

commit v5 on v4

--- a/solution.py
+++ b/solution.py
@@ -174,13 +174,13 @@
     return total
 
 
-def gather(a, axis, size):
+def gather(a, axis, size, dim=0):
     me = lax.axis_index(axis)
-    n = a.shape[0]
+    n = a.shape[dim]
     got = [shift(a, axis, size, k) for k in range(1, size)]
-    out = jnp.concatenate([a] * size, axis=0)
+    out = jnp.concatenate([a] * size, axis=dim)
     for k, piece in enumerate(got, 1):
-        out = lax.dynamic_update_slice_in_dim(out, piece, lax.rem(me - k + size, size) * n, 0)
+        out = lax.dynamic_update_slice_in_dim(out, piece, lax.rem(me - k + size, size) * n, dim)
     return out
 
 
@@ -190,6 +190,23 @@
 
 def tie(*arrays):
     return lax.optimization_barrier(arrays)
+
+
+def double(a, axis, size, bit, dim):
+    other = swap(a, axis, size, bit)
+    first = (lax.axis_index(axis) & bit) == 0
+    return jnp.concatenate([jnp.where(first, a, other), jnp.where(first, other, a)], axis=dim)
+
+
+def exchange_columns(a, axis, size):
+    me = lax.axis_index(axis)
+    n = a.shape[1] // size
+
+    def block(k):
+        return lax.dynamic_slice_in_dim(a, lax.rem(me + k, size) * n, n, 1)
+
+    got = [shift(block(k), axis, size, k) for k in range(1, size)]
+    return [block(0)] + got
 
 
 def sum_over_three(a):
@@ -213,15 +230,19 @@
     cap = 2 * bag_slot.shape[0] // (NZH * here)
     first = (lax.axis_index("zh") * here).astype(i32).reshape(1)
     near = with_keys(layer_grad, bag_owner, bag_slot)
+    columns = exchange_columns(pooled, "zh", NZH)
     near = lax.all_gather(near, "zh", axis=0, tiled=False)
+    near, *columns = tie(near, *columns)
     rows = dispatch(first, near, dense_weight, width, here, cap)
-    rows, pooled = tie(rows, pooled)
+    rows, near, *columns = tie(rows, near, *columns)
     got = lax.all_to_all(rows, ("y", "c"), 0, 0, tiled=True)
-    w = lax.dot_general(pooled, layer_grad, (((0,), (0,)), ((), ())), preferred_element_type=f32)
+    level = lax.axis_index("zh")
+    lower = [lax.rem(level - k + NZH, NZH) for k in range(NZH)]
+    lg = [lax.dynamic_index_in_dim(near, at, 0, keepdims=False)[:, : layer_grad.shape[1]] for at in lower]
+    w = lax.dot_general(jnp.concatenate(columns, axis=0), jnp.concatenate(lg, axis=0), (((0,), (0,)), ((), ())), preferred_element_type=f32)
     w = halve(w, "c", NC, 1, 0)
     w = scatter_sum(w, "x", NX)
-    w = scatter_sum(w, "zh", NZH)
-    w = sum_over_three(w)
+    w = gather(sum_over_three(w)[None], "zh", NZH)
     mine = lax.axis_index("x") * NZL + lax.axis_index("zl")
     local = lax.dynamic_slice_in_dim(touched, mine * part, part, 0)
     old = codes[local].astype(f32) * row_scale[local][:, None] + row_bias[local][:, None]
@@ -230,16 +251,19 @@
 
     sums = collect(got, touch).reshape(parts, part, width)
     sums = lax.all_to_all(sums, REP, 0, 0, tiled=True)
-    for bit in (1, 2, 4):
-        w = w + swap(w, "y", NY, bit)
+    w = halve(w, "y", NY, 1, 0)
+    w = halve(w, "y", NY, 2, 0)
+    w = w + swap(w, "y", NY, 4)
     sums, w = tie(sums, w)
 
     payload = lax.all_to_all(update(sums, old, old_accum), REP, 0, 0, tiled=True)
-    w = gather(w, "zh", NZH)
-    w = gather(w, "x", NX)
-    weight_grad = gather(w, "c", NC)
+    w = double(w, "y", NY, 2, 0)
+    w = double(w, "y", NY, 1, 0)
+    w = gather(w, "x", NX, 1)
     new_codes = payload[:, :part].reshape(touch, width)
     new_scale, lowest, new_accum = (payload[:, part + i, :part].reshape(touch) for i in range(3))
+    w, new_codes, new_scale, lowest, new_accum = tie(w, new_codes, new_scale, lowest, new_accum)
+    weight_grad = gather(w, "c", NC, 1).reshape(pooled.shape[1], layer_grad.shape[1])
     return (weight_grad, new_codes, new_scale, lowest, new_accum)
 
 

time: 226 us -> 223 us (0.987); the launches traced: 222 us -> 222 us
  waiting for transfers between devices: 32.8 us -> 50.6 us
  blocking collectives: 33.5 us -> 22.4 us
  other arithmetic: 9.08 us -> 4.75 us
    all_gather x1, blocking collectives: 33.5 us -> 22.4 us  [shards(): near = lax.all_gather(near, 'zh', axis=0, tiled=False)]
    ppermute x4 -> x6, waiting for transfers between devices: 8.85 us -> 16.9 us  [swap(): return lax.ppermute(a, axis, [(i, i ^ bit) for i in range(size)])]
    ppermute x15, starting transfers between devices: 77.1 us -> 70.6 us  [shift(): return lax.ppermute(a, axis, [(i, (i + k) % size) for i in range(size)])]
    all_to_all x1, waiting for transfers between devices: 0.97 us -> 4.84 us  [shards(): sums = lax.all_to_all(sums, REP, 0, 0, tiled=True)]
    all_to_all x1, waiting for transfers between devices: 0.01 us -> 3.58 us  [shards(): got = lax.all_to_all(rows, ('y', 'c'), 0, 0, tiled=True)]
    ppermute x4 -> x6, starting transfers between devices: 17 us -> 19.1 us  [swap(): return lax.ppermute(a, axis, [(i, i ^ bit) for i in range(size)])]
    unnamed x24 -> x18, local copies, waits for them, and re-layouts: 5.93 us -> 5.25 us
  transfers between devices with their start and end apart: 22 -> 24, of which waited for: 12 -> 14; matrix products, arithmetic and copies ran while one was open for 6% -> 4% of each run, Pallas kernels for 0% -> 0%
where the time goes in v5:
time: 223 us; the launch traced here: 222 us
  starting transfers between devices  110 us (49%)
  waiting for transfers between devices  50.6 us (23%)
  blocking collectives  22.4 us (10%)
  local copies, waits for them, and re-layouts  17.2 us (8%)
  Pallas kernels  8.14 us (4%)
  matrix products  7.09 us (3%)
  other arithmetic  4.75 us (2%)
    ppermute x15, starting transfers between devices, shift(): return lax.ppermute(a, axis, [(i, (i + k) % size) for i in range(size)])  70.6 us
    ppermute x15, waiting for transfers between devices, shift(): return lax.ppermute(a, axis, [(i, (i + k) % size) for i in range(size)])  25.2 us
    all_gather x1, blocking collectives, shards(): near = lax.all_gather(near, 'zh', axis=0, tiled=False)  22.4 us
    ppermute x6, starting transfers between devices, swap(): return lax.ppermute(a, axis, [(i, i ^ bit) for i in range(size)])  19.1 us
    ppermute x6, waiting for transfers between devices, swap(): return lax.ppermute(a, axis, [(i, i ^ bit) for i in range(size)])  16.9 us
    all_to_all x1, starting transfers between devices, shards(): got = lax.all_to_all(rows, ('y', 'c'), 0, 0, tiled=True)  9.17 us
    dot_general x1, matrix products, collect(): return jnp.dot(selector, got.reshape(-1, width), preferred_element_type=f32)  6.78 us
    all_to_all x1, starting transfers between devices, shards(): sums = lax.all_to_all(sums, REP, 0, 0, tiled=True)  6.55 us
  transfers between devices with their start and end apart: 24, of which 14 were waited for; matrix products, arithmetic and copies ran while one was open for 4% of the time, Pallas kernels for 0%

profile of v5, /device:TPU:1, one launch (start us, length us, event | category | flops | bytes accessed | tf_op | source)
XLA Modules:
  0.0 221.5 jit_solution(15932406527927054170)
XLA Ops:
  1.8 15.1 %collective-permute-start.2 = (bf16[128,256]{1,0:T(8,128)(2,1)S(1)}, bf16[128,256]{1,0:T(8,128)(2,1)S(1)}, u32[]{:S(2)}, u32[]{:S(2)}) collective-permute-start(bf16[128,256]{1,0:T(8,128)(2,1)S(1)} %get-tuple-element.61), channel_id=1, source_target_pairs={{0,48},{16,0},{32,16},{48,32},{1,49},{17,1},{33,17},{49,33},{2,50}... | collective-permute-start | bytes 196616 | tf_op jit(solution)/shard_map/ppermute | solution.py:188
  18.8 6.9 %collective-permute-start.1 = (bf16[128,256]{1,0:T(8,128)(2,1)S(1)}, bf16[128,256]{1,0:T(8,128)(2,1)S(1)}, u32[]{:S(2)}, u32[]{:S(2)}) collective-permute-start(bf16[128,256]{1,0:T(8,128)(2,1)S(1)} %get-tuple-element.64), channel_id=1, source_target_pairs={{0,32},{16,48},{32,0},{48,16},{1,33},{17,49},{33,1},{49,17},{2,34}... | collective-permute-start | bytes 196616 | tf_op jit(solution)/shard_map/ppermute | solution.py:188
  28.8 22.4 %all-gather = bf16[512,640]{1,0:T(8,128)(2,1)S(1)} all-gather(bf16[128,640]{1,0:T(8,128)(2,1)S(1)} %fusion.20), channel_id=2, replica_groups=mesh['x'=4,'zl'=3,'zh'=4,'y'=8,'c'=2] {'zh'}, dimensions={0}, use_global_device_ids=true | all-gather | bytes 819200 | tf_op jit(solution)/shard_map/all_gather | solution.py:234
  52.5 6.3 %dispatch.1 = bf16[16,272,256]{2,1,0:T(8,128)(2,1)S(1)} custom-call(s32[1]{0:T(128)} %bitcast.refs_0_, bf16[4,128,640]{2,1,0:T(8,128)(2,1)S(1)} %bitcast.24, bf16[1024,512]{1,0:T(8,128)(2,1)S(1)} %copy-done.3), custom_call_target="tpu_custom_call" | custom-call | tf_op jit(solution)/shard_map/dispatch/pallas_call | solution.py:96
  60.2 9.2 %all-to-all-start = ((bf16[16,272,256]{2,1,0:T(8,128)(2,1)}), bf16[16,272,256]{2,1,0:T(8,128)(2,1)}, u32[]{:S(2)}, u32[]{:S(2)}) async-start(bf16[16,272,256]{2,1,0:T(8,128)(2,1)} %copy-done.1), calls=%async_computation | async-start | bytes 4456448 | tf_op jit(solution)/shard_map/all_to_all | solution.py:238
  73.4 3.1 %collective-permute-start.4 = (f32[32,512]{1,0:T(8,128)S(1)}, f32[32,512]{1,0:T(8,128)S(1)}, u32[]{:S(2)}, u32[]{:S(2)}) collective-permute-start(f32[32,512]{1,0:T(8,128)S(1)} %get-tuple-element.58), channel_id=1, source_target_pairs={{0,192},{192,384},{384,576},{576,0},{1,193},{193,385},{385,577},{5... | collective-permute-start | bytes 196616 | tf_op jit(solution)/shard_map/ppermute | solution.py:188
  76.5 3.4 %collective-permute-start.6 = (f32[32,512]{1,0:T(8,128)S(1)}, f32[32,512]{1,0:T(8,128)S(1)}, u32[]{:S(2)}, u32[]{:S(2)}) collective-permute-start(f32[32,512]{1,0:T(8,128)S(1)} %get-tuple-element.59), channel_id=1, source_target_pairs={{0,576},{192,0},{384,192},{576,384},{1,577},{193,1},{385,193},{577... | collective-permute-start | bytes 196616 | tf_op jit(solution)/shard_map/ppermute | solution.py:188
  79.9 3.4 %collective-permute-start.5 = (f32[32,512]{1,0:T(8,128)S(1)}, f32[32,512]{1,0:T(8,128)S(1)}, u32[]{:S(2)}, u32[]{:S(2)}) collective-permute-start(f32[32,512]{1,0:T(8,128)S(1)} %get-tuple-element.60), channel_id=1, source_target_pairs={{0,384},{192,576},{384,0},{576,192},{1,385},{193,577},{385,1},{577... | collective-permute-start | bytes 196616 | tf_op jit(solution)/shard_map/ppermute | solution.py:188
  86.8 4.9 %collective-permute-start.8 = (f32[32,512]{1,0:T(8,128)S(1)}, f32[32,512]{1,0:T(8,128)S(1)}, u32[]{:S(2)}, u32[]{:S(2)}) collective-permute-start(f32[32,512]{1,0:T(8,128)S(1)} %add_add_fusion), channel_id=1, source_target_pairs={{0,128},{64,0},{128,64},{1,129},{65,1},{129,65},{2,130},{66,2},{13... | collective-permute-start | bytes 196616 | tf_op jit(solution)/shard_map/ppermute | solution.py:188
  95.0 3.1 %collective-permute-done.7 = f32[32,512]{1,0:T(8,128)S(1)} collective-permute-done((f32[32,512]{1,0:T(8,128)S(1)}, f32[32,512]{1,0:T(8,128)S(1)}, u32[]{:S(2)}, u32[]{:S(2)}) %collective-permute-start.7) | collective-permute-done | bytes 65568 | tf_op jit(solution)/shard_map/ppermute | solution.py:188
  98.0 5.9 %collective-permute-start.9 = (f32[1,32,512]{2,1,0:T(8,128)S(1)}, f32[1,32,512]{2,1,0:T(8,128)S(1)}, u32[]{:S(2)}, u32[]{:S(2)}) collective-permute-start(f32[1,32,512]{2,1,0:T(8,128)S(1)} %bitcast.28), channel_id=1, source_target_pairs={{0,16},{16,32},{32,48},{48,0},{1,17},{17,33},{33,49},{49,1},{2,18}... | collective-permute-start | bytes 196616 | tf_op jit(solution)/shard_map/ppermute | solution.py:188
  106.4 8.0 %collective-permute-start.10 = (f32[1,32,512]{2,1,0:T(8,128)S(1)}, f32[1,32,512]{2,1,0:T(8,128)S(1)}, u32[]{:S(2)}, u32[]{:S(2)}) collective-permute-start(f32[1,32,512]{2,1,0:T(8,128)S(1)} %bitcast.30), channel_id=1, source_target_pairs={{0,32},{16,48},{32,0},{48,16},{1,33},{17,49},{33,1},{49,17},{2,34}... | collective-permute-start | bytes 196616 | tf_op jit(solution)/shard_map/ppermute | solution.py:188
  114.4 3.2 %collective-permute-done.10 = f32[1,32,512]{2,1,0:T(8,128)S(1)} collective-permute-done((f32[1,32,512]{2,1,0:T(8,128)S(1)}, f32[1,32,512]{2,1,0:T(8,128)S(1)}, u32[]{:S(2)}, u32[]{:S(2)}) %collective-permute-start.10) | collective-permute-done | bytes 65568 | tf_op jit(solution)/shard_map/ppermute | solution.py:188
  117.7 3.6 %all-to-all-done = bf16[16,272,256]{2,1,0:T(8,128)(2,1)} async-done(((bf16[16,272,256]{2,1,0:T(8,128)(2,1)}), bf16[16,272,256]{2,1,0:T(8,128)(2,1)}, u32[]{:S(2)}, u32[]{:S(2)}) %all-to-all-start) | async-done | bytes 2228256 | tf_op jit(solution)/shard_map/all_to_all | solution.py:238
  122.4 6.8 %fusion = f32[12,128,256]{2,1,0:T(8,128)} fusion(bf16[4352,256,1]{1,0,2:T(8,128)(2,1)} %bitcast.8, s32[4352]{0:T(1024)S(1)} %eq.69, s32[12,128]{1,0:T(8,128)S(1)} %multiply_add_fusion.1), kind=kOutput, calls=%fused_computation.4 | convolution fusion | flops 3429236736 | bytes 3824640 | tf_op jit(solution)/shard_map/dot_general | solution.py:113
  129.2 6.5 %all-to-all-start.1 = ((f32[12,128,256]{2,1,0:T(8,128)}), f32[12,128,256]{2,1,0:T(8,128)}, u32[]{:S(2)}, u32[]{:S(2)}) async-start(f32[12,128,256]{2,1,0:T(8,128)} %fusion), calls=%async_computation.1 | async-start | bytes 3145728 | tf_op jit(solution)/shard_map/all_to_all | solution.py:253
  137.7 4.3 %collective-permute-done.12 = f32[2,32,512]{2,1,0:T(8,128)S(1)} collective-permute-done((f32[2,32,512]{2,1,0:T(8,128)S(1)}, f32[2,32,512]{2,1,0:T(8,128)S(1)}, u32[]{:S(2)}, u32[]{:S(2)}) %collective-permute-start.12) | collective-permute-done | bytes 131104 | tf_op jit(solution)/shard_map/ppermute | solution.py:152
  142.1 4.1 %collective-permute-start.13 = (f32[1,32,512]{2,1,0:T(8,128)S(1)}, f32[1,32,512]{2,1,0:T(8,128)S(1)}, u32[]{:S(2)}, u32[]{:S(2)}) collective-permute-start(f32[1,32,512]{2,1,0:T(8,128)S(1)} %constant_dynamic-slice_fusion), channel_id=1, source_target_pairs={{0,4},{2,6},{4,0},{6,2},{8,12},{10,14},{12,8},{14,10},{1,5},{3,7},... | collective-permute-start | bytes 196616 | tf_op jit(solution)/shard_map/ppermute | solution.py:152
  148.4 4.5 %collective-permute-start.14 = (f32[1,32,512]{2,1,0:T(8,128)S(1)}, f32[1,32,512]{2,1,0:T(8,128)S(1)}, u32[]{:S(2)}, u32[]{:S(2)}) collective-permute-start(f32[1,32,512]{2,1,0:T(8,128)S(1)} %dynamic-slice_add_fusion.2), channel_id=1, source_target_pairs={{0,8},{2,10},{4,12},{6,14},{8,0},{10,2},{12,4},{14,6},{1,9},{3,11}... | collective-permute-start | bytes 196616 | tf_op jit(solution)/shard_map/ppermute | solution.py:152
  153.0 4.4 %collective-permute-done.14 = f32[1,32,512]{2,1,0:T(8,128)S(1)} collective-permute-done((f32[1,32,512]{2,1,0:T(8,128)S(1)}, f32[1,32,512]{2,1,0:T(8,128)S(1)}, u32[]{:S(2)}, u32[]{:S(2)}) %collective-permute-start.14) | collective-permute-done | bytes 65568 | tf_op jit(solution)/shard_map/ppermute | solution.py:152
  157.4 4.8 %all-to-all-done.1.sums_ref = f32[12,128,256]{2,1,0:T(8,128)} async-done(((f32[12,128,256]{2,1,0:T(8,128)}), f32[12,128,256]{2,1,0:T(8,128)}, u32[]{:S(2)}, u32[]{:S(2)}) %all-to-all-start.1) | async-done | bytes 1572896 | tf_op jit(solution)/shard_map/all_to_all | solution.py:253
  165.3 4.4 %all-to-all-start.2 = ((f32[12,136,256]{2,1,0:T(8,128)}), f32[12,136,256]{2,1,0:T(8,128)}, u32[]{:S(2)}, u32[]{:S(2)}) async-start(f32[12,136,256]{2,1,0:T(8,128)} %copy-done.2), calls=%async_computation.2 | async-start | bytes 3342336 | tf_op jit(solution)/shard_map/all_to_all | solution.py:259
  169.7 3.1 %collective-permute-start.15 = (f32[1,32,512]{2,1,0:T(8,128)S(1)}, f32[1,32,512]{2,1,0:T(8,128)S(1)}, u32[]{:S(2)}, u32[]{:S(2)}) collective-permute-start(f32[1,32,512]{2,1,0:T(8,128)S(1)} %add.245), channel_id=1, source_target_pairs={{0,4},{2,6},{4,0},{6,2},{8,12},{10,14},{12,8},{14,10},{1,5},{3,7},... | collective-permute-start | bytes 196616 | tf_op jit(solution)/shard_map/ppermute | solution.py:152
  172.8 2.8 %collective-permute-done.15 = f32[1,32,512]{2,1,0:T(8,128)S(1)} collective-permute-done((f32[1,32,512]{2,1,0:T(8,128)S(1)}, f32[1,32,512]{2,1,0:T(8,128)S(1)}, u32[]{:S(2)}, u32[]{:S(2)}) %collective-permute-start.15) | collective-permute-done | bytes 65568 | tf_op jit(solution)/shard_map/ppermute | solution.py:152
  175.7 3.4 %collective-permute-start.16 = (f32[2,32,512]{2,1,0:T(8,128)S(1)}, f32[2,32,512]{2,1,0:T(8,128)S(1)}, u32[]{:S(2)}, u32[]{:S(2)}) collective-permute-start(f32[2,32,512]{2,1,0:T(8,128)S(1)} %pad_maximum_fusion.2), channel_id=1, source_target_pairs={{0,2},{2,0},{4,6},{6,4},{8,10},{10,8},{12,14},{14,12},{1,3},{3,1},... | collective-permute-start | bytes 393224 | tf_op jit(solution)/shard_map/ppermute | solution.py:152
  179.0 2.7 %collective-permute-done.16 = f32[2,32,512]{2,1,0:T(8,128)S(1)} collective-permute-done((f32[2,32,512]{2,1,0:T(8,128)S(1)}, f32[2,32,512]{2,1,0:T(8,128)S(1)}, u32[]{:S(2)}, u32[]{:S(2)}) %collective-permute-start.16) | collective-permute-done | bytes 131104 | tf_op jit(solution)/shard_map/ppermute | solution.py:152
  181.8 3.6 %collective-permute-start.17 = (f32[4,32,512]{2,1,0:T(8,128)S(1)}, f32[4,32,512]{2,1,0:T(8,128)S(1)}, u32[]{:S(2)}, u32[]{:S(2)}) collective-permute-start(f32[4,32,512]{2,1,0:T(8,128)S(1)} %pad_maximum_fusion.1), channel_id=1, source_target_pairs={{0,192},{192,384},{384,576},{576,0},{1,193},{193,385},{385,577},{5... | collective-permute-start | bytes 786440 | tf_op jit(solution)/shard_map/ppermute | solution.py:188
  185.4 4.3 %collective-permute-start.18 = (f32[4,32,512]{2,1,0:T(8,128)S(1)}, f32[4,32,512]{2,1,0:T(8,128)S(1)}, u32[]{:S(2)}, u32[]{:S(2)}) collective-permute-start(f32[4,32,512]{2,1,0:T(8,128)S(1)} %pad_maximum_fusion.1), channel_id=1, source_target_pairs={{0,384},{192,576},{384,0},{576,192},{1,385},{193,577},{385,1},{577... | collective-permute-start | bytes 786440 | tf_op jit(solution)/shard_map/ppermute | solution.py:188
  189.8 3.1 %collective-permute-start.19 = (f32[4,32,512]{2,1,0:T(8,128)S(1)}, f32[4,32,512]{2,1,0:T(8,128)S(1)}, u32[]{:S(2)}, u32[]{:S(2)}) collective-permute-start(f32[4,32,512]{2,1,0:T(8,128)S(1)} %pad_maximum_fusion.1), channel_id=1, source_target_pairs={{0,576},{192,0},{384,192},{576,384},{1,577},{193,1},{385,193},{577... | collective-permute-start | bytes 786440 | tf_op jit(solution)/shard_map/ppermute | solution.py:188
  193.0 9.9 %collective-permute-done.17 = f32[4,32,512]{2,1,0:T(8,128)S(1)} collective-permute-done((f32[4,32,512]{2,1,0:T(8,128)S(1)}, f32[4,32,512]{2,1,0:T(8,128)S(1)}, u32[]{:S(2)}, u32[]{:S(2)}) %collective-permute-start.17) | collective-permute-done | bytes 262176 | tf_op jit(solution)/shard_map/ppermute | solution.py:188
  202.9 6.7 %collective-permute-done.18 = f32[4,32,512]{2,1,0:T(8,128)S(1)} collective-permute-done((f32[4,32,512]{2,1,0:T(8,128)S(1)}, f32[4,32,512]{2,1,0:T(8,128)S(1)}, u32[]{:S(2)}, u32[]{:S(2)}) %collective-permute-start.18) | collective-permute-done | bytes 262176 | tf_op jit(solution)/shard_map/ppermute | solution.py:188
  211.3 2.7 %slice.52 = f32[12,128,256]{2,1,0:T(8,128)} slice(f32[12,136,256]{2,1,0:T(8,128)} %all-to-all-done.2), slice={[0:12], [0:128], [0:256]} | slice | bytes 3145728 | tf_op jit(solution)/shard_map/slice | solution.py:263
  (93 shorter events, 39.3 us)
Async XLA Ops:
  0.6 85.1 %copy-start = (bf16[4096,256]{1,0:T(8,128)(2,1)S(1)}, bf16[4096,256]{1,0:T(8,128)(2,1)}, u32[]{:S(2)}) copy-start(bf16[4096,256]{1,0:T(8,128)(2,1)} %param.16) | copy-start | bytes 6291460
  1.8 49.5 %collective-permute-start.2 = (bf16[128,256]{1,0:T(8,128)(2,1)S(1)}, bf16[128,256]{1,0:T(8,128)(2,1)S(1)}, u32[]{:S(2)}, u32[]{:S(2)}) collective-permute-start(bf16[128,256]{1,0:T(8,128)(2,1)S(1)} %get-tuple-element.61), channel_id=1, source_target_pairs={{0,48},{16,0},{32,16},{48,32},{1,49},{17,1},{33,17},{49,33},{2,50}... | collective-permute-start | bytes 196616 | tf_op jit(solution)/shard_map/ppermute | solution.py:188
  16.9 34.4 %collective-permute-start = (bf16[128,256]{1,0:T(8,128)(2,1)S(1)}, bf16[128,256]{1,0:T(8,128)(2,1)S(1)}, u32[]{:S(2)}, u32[]{:S(2)}) collective-permute-start(bf16[128,256]{1,0:T(8,128)(2,1)S(1)} %get-tuple-element.62), channel_id=1, source_target_pairs={{0,16},{16,32},{32,48},{48,0},{1,17},{17,33},{33,49},{49,1},{2,18}... | collective-permute-start | bytes 196616 | tf_op jit(solution)/shard_map/ppermute | solution.py:188
  18.8 32.4 %collective-permute-start.1 = (bf16[128,256]{1,0:T(8,128)(2,1)S(1)}, bf16[128,256]{1,0:T(8,128)(2,1)S(1)}, u32[]{:S(2)}, u32[]{:S(2)}) collective-permute-start(bf16[128,256]{1,0:T(8,128)(2,1)S(1)} %get-tuple-element.64), channel_id=1, source_target_pairs={{0,32},{16,48},{32,0},{48,16},{1,33},{17,49},{33,1},{49,17},{2,34}... | collective-permute-start | bytes 196616 | tf_op jit(solution)/shard_map/ppermute | solution.py:188
  51.3 1.2 copy-start.3
  58.8 1.4 copy-start.1
  60.2 61.1 %all-to-all-start = ((bf16[16,272,256]{2,1,0:T(8,128)(2,1)}), bf16[16,272,256]{2,1,0:T(8,128)(2,1)}, u32[]{:S(2)}, u32[]{:S(2)}) async-start(bf16[16,272,256]{2,1,0:T(8,128)(2,1)} %copy-done.1), calls=%async_computation | async-start | bytes 4456448 | tf_op jit(solution)/shard_map/all_to_all | solution.py:238
  69.5 13.9 %copy-start.4 = (f32[4096]{0:T(1024)S(1)}, f32[4096]{0:T(1024)}, u32[]{:S(2)}) copy-start(f32[4096]{0:T(1024)} %param.18) | copy-start | bytes 49156
  69.5 15.0 %copy-start.5 = (f32[4096]{0:T(1024)S(1)}, f32[4096]{0:T(1024)}, u32[]{:S(2)}) copy-start(f32[4096]{0:T(1024)} %param.17) | copy-start | bytes 49156
  69.8 23.9 %copy-start.6 = (f32[4096]{0:T(1024)S(1)}, f32[4096]{0:T(1024)}, u32[]{:S(2)}) copy-start(f32[4096]{0:T(1024)} %param.19) | copy-start | bytes 49156
  69.9 3.4 %collective-permute-start.3 = (f32[128,512]{1,0:T(8,128)S(1)}, f32[128,512]{1,0:T(8,128)S(1)}, u32[]{:S(2)}, u32[]{:S(2)}) collective-permute-start(f32[128,512]{1,0:T(8,128)S(1)} %constant_dynamic-slice_fusion.5), channel_id=1, source_target_pairs={{0,1},{1,0},{2,3},{3,2},{4,5},{5,4},{6,7},{7,6},{8,9},{9,8},{10,11... | collective-permute-start | bytes 786440 | tf_op jit(solution)/shard_map/ppermute | solution.py:152
  73.4 13.2 %collective-permute-start.4 = (f32[32,512]{1,0:T(8,128)S(1)}, f32[32,512]{1,0:T(8,128)S(1)}, u32[]{:S(2)}, u32[]{:S(2)}) collective-permute-start(f32[32,512]{1,0:T(8,128)S(1)} %get-tuple-element.58), channel_id=1, source_target_pairs={{0,192},{192,384},{384,576},{576,0},{1,193},{193,385},{385,577},{5... | collective-permute-start | bytes 196616 | tf_op jit(solution)/shard_map/ppermute | solution.py:188
  76.5 10.1 %collective-permute-start.6 = (f32[32,512]{1,0:T(8,128)S(1)}, f32[32,512]{1,0:T(8,128)S(1)}, u32[]{:S(2)}, u32[]{:S(2)}) collective-permute-start(f32[32,512]{1,0:T(8,128)S(1)} %get-tuple-element.59), channel_id=1, source_target_pairs={{0,576},{192,0},{384,192},{576,384},{1,577},{193,1},{385,193},{577... | collective-permute-start | bytes 196616 | tf_op jit(solution)/shard_map/ppermute | solution.py:188
  79.9 6.9 %collective-permute-start.5 = (f32[32,512]{1,0:T(8,128)S(1)}, f32[32,512]{1,0:T(8,128)S(1)}, u32[]{:S(2)}, u32[]{:S(2)}) collective-permute-start(f32[32,512]{1,0:T(8,128)S(1)} %get-tuple-element.60), channel_id=1, source_target_pairs={{0,384},{192,576},{384,0},{576,192},{1,385},{193,577},{385,1},{577... | collective-permute-start | bytes 196616 | tf_op jit(solution)/shard_map/ppermute | solution.py:188
  86.8 8.1 %collective-permute-start.8 = (f32[32,512]{1,0:T(8,128)S(1)}, f32[32,512]{1,0:T(8,128)S(1)}, u32[]{:S(2)}, u32[]{:S(2)}) collective-permute-start(f32[32,512]{1,0:T(8,128)S(1)} %add_add_fusion), channel_id=1, source_target_pairs={{0,128},{64,0},{128,64},{1,129},{65,1},{129,65},{2,130},{66,2},{13... | collective-permute-start | bytes 196616 | tf_op jit(solution)/shard_map/ppermute | solution.py:188
  91.7 6.3 %collective-permute-start.7 = (f32[32,512]{1,0:T(8,128)S(1)}, f32[32,512]{1,0:T(8,128)S(1)}, u32[]{:S(2)}, u32[]{:S(2)}) collective-permute-start(f32[32,512]{1,0:T(8,128)S(1)} %add_add_fusion), channel_id=1, source_target_pairs={{0,64},{64,128},{128,0},{1,65},{65,129},{129,1},{2,66},{66,130},{1... | collective-permute-start | bytes 196616 | tf_op jit(solution)/shard_map/ppermute | solution.py:188
  98.0 16.4 %collective-permute-start.9 = (f32[1,32,512]{2,1,0:T(8,128)S(1)}, f32[1,32,512]{2,1,0:T(8,128)S(1)}, u32[]{:S(2)}, u32[]{:S(2)}) collective-permute-start(f32[1,32,512]{2,1,0:T(8,128)S(1)} %bitcast.28), channel_id=1, source_target_pairs={{0,16},{16,32},{32,48},{48,0},{1,17},{17,33},{33,49},{49,1},{2,18}... | collective-permute-start | bytes 196616 | tf_op jit(solution)/shard_map/ppermute | solution.py:188
  104.0 13.7 %collective-permute-start.11 = (f32[1,32,512]{2,1,0:T(8,128)S(1)}, f32[1,32,512]{2,1,0:T(8,128)S(1)}, u32[]{:S(2)}, u32[]{:S(2)}) collective-permute-start(f32[1,32,512]{2,1,0:T(8,128)S(1)} %bitcast.29), channel_id=1, source_target_pairs={{0,48},{16,0},{32,16},{48,32},{1,49},{17,1},{33,17},{49,33},{2,50}... | collective-permute-start | bytes 196616 | tf_op jit(solution)/shard_map/ppermute | solution.py:188
  106.4 11.3 %collective-permute-start.10 = (f32[1,32,512]{2,1,0:T(8,128)S(1)}, f32[1,32,512]{2,1,0:T(8,128)S(1)}, u32[]{:S(2)}, u32[]{:S(2)}) collective-permute-start(f32[1,32,512]{2,1,0:T(8,128)S(1)} %bitcast.30), channel_id=1, source_target_pairs={{0,32},{16,48},{32,0},{48,16},{1,33},{17,49},{33,1},{49,17},{2,34}... | collective-permute-start | bytes 196616 | tf_op jit(solution)/shard_map/ppermute | solution.py:188
  129.2 33.1 %all-to-all-start.1 = ((f32[12,128,256]{2,1,0:T(8,128)}), f32[12,128,256]{2,1,0:T(8,128)}, u32[]{:S(2)}, u32[]{:S(2)}) async-start(f32[12,128,256]{2,1,0:T(8,128)} %fusion), calls=%async_computation.1 | async-start | bytes 3145728 | tf_op jit(solution)/shard_map/all_to_all | solution.py:253
  135.7 6.3 %collective-permute-start.12 = (f32[2,32,512]{2,1,0:T(8,128)S(1)}, f32[2,32,512]{2,1,0:T(8,128)S(1)}, u32[]{:S(2)}, u32[]{:S(2)}) collective-permute-start(f32[2,32,512]{2,1,0:T(8,128)S(1)} %constant_dynamic-slice_fusion.1), channel_id=1, source_target_pairs={{0,2},{2,0},{4,6},{6,4},{8,10},{10,8},{12,14},{14,12},{1,3},{3,1},... | collective-permute-start | bytes 393224 | tf_op jit(solution)/shard_map/ppermute | solution.py:152
  142.1 6.3 %collective-permute-start.13 = (f32[1,32,512]{2,1,0:T(8,128)S(1)}, f32[1,32,512]{2,1,0:T(8,128)S(1)}, u32[]{:S(2)}, u32[]{:S(2)}) collective-permute-start(f32[1,32,512]{2,1,0:T(8,128)S(1)} %constant_dynamic-slice_fusion), channel_id=1, source_target_pairs={{0,4},{2,6},{4,0},{6,2},{8,12},{10,14},{12,8},{14,10},{1,5},{3,7},... | collective-permute-start | bytes 196616 | tf_op jit(solution)/shard_map/ppermute | solution.py:152
  148.4 9.0 %collective-permute-start.14 = (f32[1,32,512]{2,1,0:T(8,128)S(1)}, f32[1,32,512]{2,1,0:T(8,128)S(1)}, u32[]{:S(2)}, u32[]{:S(2)}) collective-permute-start(f32[1,32,512]{2,1,0:T(8,128)S(1)} %dynamic-slice_add_fusion.2), channel_id=1, source_target_pairs={{0,8},{2,10},{4,12},{6,14},{8,0},{10,2},{12,4},{14,6},{1,9},{3,11}... | collective-permute-start | bytes 196616 | tf_op jit(solution)/shard_map/ppermute | solution.py:152
  164.1 1.2 copy-start.2
  165.3 44.4 %all-to-all-start.2 = ((f32[12,136,256]{2,1,0:T(8,128)}), f32[12,136,256]{2,1,0:T(8,128)}, u32[]{:S(2)}, u32[]{:S(2)}) async-start(f32[12,136,256]{2,1,0:T(8,128)} %copy-done.2), calls=%async_computation.2 | async-start | bytes 3342336 | tf_op jit(solution)/shard_map/all_to_all | solution.py:259
  169.7 5.9 %collective-permute-start.15 = (f32[1,32,512]{2,1,0:T(8,128)S(1)}, f32[1,32,512]{2,1,0:T(8,128)S(1)}, u32[]{:S(2)}, u32[]{:S(2)}) collective-permute-start(f32[1,32,512]{2,1,0:T(8,128)S(1)} %add.245), channel_id=1, source_target_pairs={{0,4},{2,6},{4,0},{6,2},{8,12},{10,14},{12,8},{14,10},{1,5},{3,7},... | collective-permute-start | bytes 196616 | tf_op jit(solution)/shard_map/ppermute | solution.py:152
  175.7 6.1 %collective-permute-start.16 = (f32[2,32,512]{2,1,0:T(8,128)S(1)}, f32[2,32,512]{2,1,0:T(8,128)S(1)}, u32[]{:S(2)}, u32[]{:S(2)}) collective-permute-start(f32[2,32,512]{2,1,0:T(8,128)S(1)} %pad_maximum_fusion.2), channel_id=1, source_target_pairs={{0,2},{2,0},{4,6},{6,4},{8,10},{10,8},{12,14},{14,12},{1,3},{3,1},... | collective-permute-start | bytes 393224 | tf_op jit(solution)/shard_map/ppermute | solution.py:152
  181.8 21.0 %collective-permute-start.17 = (f32[4,32,512]{2,1,0:T(8,128)S(1)}, f32[4,32,512]{2,1,0:T(8,128)S(1)}, u32[]{:S(2)}, u32[]{:S(2)}) collective-permute-start(f32[4,32,512]{2,1,0:T(8,128)S(1)} %pad_maximum_fusion.1), channel_id=1, source_target_pairs={{0,192},{192,384},{384,576},{576,0},{1,193},{193,385},{385,577},{5... | collective-permute-start | bytes 786440 | tf_op jit(solution)/shard_map/ppermute | solution.py:188
  185.4 24.2 %collective-permute-start.18 = (f32[4,32,512]{2,1,0:T(8,128)S(1)}, f32[4,32,512]{2,1,0:T(8,128)S(1)}, u32[]{:S(2)}, u32[]{:S(2)}) collective-permute-start(f32[4,32,512]{2,1,0:T(8,128)S(1)} %pad_maximum_fusion.1), channel_id=1, source_target_pairs={{0,384},{192,576},{384,0},{576,192},{1,385},{193,577},{385,1},{577... | collective-permute-start | bytes 786440 | tf_op jit(solution)/shard_map/ppermute | solution.py:188
  189.8 19.8 %collective-permute-start.19 = (f32[4,32,512]{2,1,0:T(8,128)S(1)}, f32[4,32,512]{2,1,0:T(8,128)S(1)}, u32[]{:S(2)}, u32[]{:S(2)}) collective-permute-start(f32[4,32,512]{2,1,0:T(8,128)S(1)} %pad_maximum_fusion.1), channel_id=1, source_target_pairs={{0,576},{192,0},{384,192},{576,384},{1,577},{193,1},{385,193},{577... | collective-permute-start | bytes 786440 | tf_op jit(solution)/shard_map/ppermute | solution.py:188
  213.9 5.0 %collective-permute-start.20 = (f32[4,128,512]{2,1,0:T(8,128)S(1)}, f32[4,128,512]{2,1,0:T(8,128)}, u32[]{:S(2)}, u32[]{:S(2)}) collective-permute-start(f32[4,128,512]{2,1,0:T(8,128)S(1)} %constant_dynamic-update-slice_fusion.1), channel_id=1, source_target_pairs={{0,1},{1,0},{2,3},{3,2},{4,5},{5,4},{6,7},{7,6},{8,9},{9,8},{10,11... | collective-permute-start | bytes 3145736 | tf_op jit(solution)/shard_map/ppermute | solution.py:188
  220.2 1.3 copy-start.7

commit v6 on v5

--- a/solution.py
+++ b/solution.py
@@ -198,17 +198,6 @@
     return jnp.concatenate([jnp.where(first, a, other), jnp.where(first, other, a)], axis=dim)
 
 
-def exchange_columns(a, axis, size):
-    me = lax.axis_index(axis)
-    n = a.shape[1] // size
-
-    def block(k):
-        return lax.dynamic_slice_in_dim(a, lax.rem(me + k, size) * n, n, 1)
-
-    got = [shift(block(k), axis, size, k) for k in range(1, size)]
-    return [block(0)] + got
-
-
 def sum_over_three(a):
     me = lax.axis_index("zl")
     got = [a] + [shift(a, "zl", NZL, k) for k in range(1, NZL)]
@@ -230,16 +219,16 @@
     cap = 2 * bag_slot.shape[0] // (NZH * here)
     first = (lax.axis_index("zh") * here).astype(i32).reshape(1)
     near = with_keys(layer_grad, bag_owner, bag_slot)
-    columns = exchange_columns(pooled, "zh", NZH)
+    columns = jnp.stack(jnp.split(pooled, NZH, axis=1))
+    columns = lax.all_to_all(columns, "zh", 0, 0, tiled=True)
     near = lax.all_gather(near, "zh", axis=0, tiled=False)
-    near, *columns = tie(near, *columns)
+    near, columns = tie(near, columns)
     rows = dispatch(first, near, dense_weight, width, here, cap)
-    rows, near, *columns = tie(rows, near, *columns)
+    rows, near, columns = tie(rows, near, columns)
     got = lax.all_to_all(rows, ("y", "c"), 0, 0, tiled=True)
-    level = lax.axis_index("zh")
-    lower = [lax.rem(level - k + NZH, NZH) for k in range(NZH)]
-    lg = [lax.dynamic_index_in_dim(near, at, 0, keepdims=False)[:, : layer_grad.shape[1]] for at in lower]
-    w = lax.dot_general(jnp.concatenate(columns, axis=0), jnp.concatenate(lg, axis=0), (((0,), (0,)), ((), ())), preferred_element_type=f32)
+    lg = near.reshape(-1, near.shape[2])[:, : layer_grad.shape[1]]
+    columns = columns.reshape(lg.shape[0], -1)
+    w = lax.dot_general(columns, lg, (((0,), (0,)), ((), ())), preferred_element_type=f32)
     w = halve(w, "c", NC, 1, 0)
     w = scatter_sum(w, "x", NX)
     w = gather(sum_over_three(w)[None], "zh", NZH)
@@ -262,8 +251,12 @@
     w = gather(w, "x", NX, 1)
     new_codes = payload[:, :part].reshape(touch, width)
     new_scale, lowest, new_accum = (payload[:, part + i, :part].reshape(touch) for i in range(3))
-    w, new_codes, new_scale, lowest, new_accum = tie(w, new_codes, new_scale, lowest, new_accum)
-    weight_grad = gather(w, "c", NC, 1).reshape(pooled.shape[1], layer_grad.shape[1])
+    other = swap(w, "c", NC, 1)
+    other, new_codes, new_scale, lowest, new_accum = tie(other, new_codes, new_scale, lowest, new_accum)
+    side = lax.axis_index("c") * w.shape[1]
+    weight_grad = jnp.concatenate([w, w], axis=1)
+    weight_grad = lax.dynamic_update_slice_in_dim(weight_grad, other, w.shape[1] - side, 1)
+    weight_grad = weight_grad.reshape(pooled.shape[1], layer_grad.shape[1])
     return (weight_grad, new_codes, new_scale, lowest, new_accum)
 
 

time: 223 us -> 219 us (0.982)
  starting transfers between devices: 110 us -> 97 us
  blocking collectives: 22.4 us -> 28.7 us
    ppermute x15 -> x11, starting transfers between devices: 70.6 us -> 41.6 us  [shift(): return lax.ppermute(a, axis, [(i, (i + k) % size) for i in range(size)])]
    all_to_all x0 -> x1, starting transfers between devices: none -> 15 us  [shards(): columns = lax.all_to_all(columns, 'zh', 0, 0, tiled=True)]
    all_gather x1, blocking collectives: 22.4 us -> 28.7 us  [shards(): near = lax.all_gather(near, 'zh', axis=0, tiled=False)]
    ppermute x6 -> x7, starting transfers between devices: 19.1 us -> 21.5 us  [swap(): return lax.ppermute(a, axis, [(i, i ^ bit) for i in range(size)])]
    ppermute x15 -> x11, waiting for transfers between devices: 25.2 us -> 24.1 us  [shift(): return lax.ppermute(a, axis, [(i, (i + k) % size) for i in range(size)])]
    ppermute x6 -> x7, waiting for transfers between devices: 16.9 us -> 17.1 us  [swap(): return lax.ppermute(a, axis, [(i, i ^ bit) for i in range(size)])]
    unnamed x18 -> x22, local copies, waits for them, and re-layouts: 5.25 us -> 5.37 us
  transfers between devices with their start and end apart: 24 -> 22, of which waited for: 14 -> 13; matrix products, arithmetic and copies ran while one was open for 4% -> 7% of each run, Pallas kernels for 0% -> 0%
where the time goes in v6:
time: 219 us; the launch traced here: 217 us
  starting transfers between devices  97 us (44%)
  waiting for transfers between devices  50 us (23%)
  blocking collectives  28.7 us (13%)
  local copies, waits for them, and re-layouts  17.4 us (8%)
  Pallas kernels  8.14 us (4%)
  matrix products  8.04 us (4%)
  other arithmetic  6.86 us (3%)
    ppermute x11, starting transfers between devices, shift(): return lax.ppermute(a, axis, [(i, (i + k) % size) for i in range(size)])  41.6 us
    all_gather x1, blocking collectives, shards(): near = lax.all_gather(near, 'zh', axis=0, tiled=False)  28.7 us
    ppermute x11, waiting for transfers between devices, shift(): return lax.ppermute(a, axis, [(i, (i + k) % size) for i in range(size)])  24.1 us
    ppermute x7, starting transfers between devices, swap(): return lax.ppermute(a, axis, [(i, i ^ bit) for i in range(size)])  21.5 us
    ppermute x7, waiting for transfers between devices, swap(): return lax.ppermute(a, axis, [(i, i ^ bit) for i in range(size)])  17.1 us
    all_to_all x1, starting transfers between devices, shards(): columns = lax.all_to_all(columns, 'zh', 0, 0, tiled=True)  15 us
    all_to_all x1, starting transfers between devices, shards(): got = lax.all_to_all(rows, ('y', 'c'), 0, 0, tiled=True)  9.23 us
    dot_general x1, matrix products, collect(): return jnp.dot(selector, got.reshape(-1, width), preferred_element_type=f32)  6.77 us
  transfers between devices with their start and end apart: 22, of which 13 were waited for; matrix products, arithmetic and copies ran while one was open for 7% of the time, Pallas kernels for 0%

profile of v6, /device:TPU:1, one launch (start us, length us, event | category | flops | bytes accessed | tf_op | source)
XLA Modules:
  0.0 217.5 jit_solution(13065016192672986071)
XLA Ops:
  2.5 15.0 %all-to-all-start = ((bf16[4,128,256]{2,1,0:T(8,128)(2,1)}), bf16[4,128,256]{2,1,0:T(8,128)(2,1)S(1)}, u32[]{:S(2)}, u32[]{:S(2)}) async-start(bf16[4,128,256]{2,1,0:T(8,128)(2,1)} %pad_maximum_fusion.1), calls=%async_computation | async-start | bytes 524288 | tf_op jit(solution)/shard_map/all_to_all | solution.py:223
  20.6 28.7 %all-gather = bf16[512,640]{1,0:T(8,128)(2,1)S(1)} all-gather(bf16[128,640]{1,0:T(8,128)(2,1)S(1)} %fusion.7), channel_id=2, replica_groups=mesh['x'=4,'zl'=3,'zh'=4,'y'=8,'c'=2] {'zh'}, dimensions={0}, use_global_device_ids=true | all-gather | bytes 819200 | tf_op jit(solution)/shard_map/all_gather | solution.py:224
  50.6 6.3 %dispatch.1 = bf16[16,272,256]{2,1,0:T(8,128)(2,1)S(1)} custom-call(s32[1]{0:T(128)} %bitcast.refs_0_, bf16[4,128,640]{2,1,0:T(8,128)(2,1)S(1)} %bitcast.27, bf16[1024,512]{1,0:T(8,128)(2,1)S(1)} %copy-done.3), custom_call_target="tpu_custom_call" | custom-call | tf_op jit(solution)/shard_map/dispatch/pallas_call | solution.py:96
  58.3 9.2 %all-to-all-start.1 = ((bf16[16,272,256]{2,1,0:T(8,128)(2,1)}), bf16[16,272,256]{2,1,0:T(8,128)(2,1)}, u32[]{:S(2)}, u32[]{:S(2)}) async-start(bf16[16,272,256]{2,1,0:T(8,128)(2,1)} %copy-done.1), calls=%async_computation.1 | async-start | bytes 4456448 | tf_op jit(solution)/shard_map/all_to_all | solution.py:228
  72.4 3.1 %collective-permute-start.1 = (f32[32,512]{1,0:T(8,128)S(1)}, f32[32,512]{1,0:T(8,128)S(1)}, u32[]{:S(2)}, u32[]{:S(2)}) collective-permute-start(f32[32,512]{1,0:T(8,128)S(1)} %get-tuple-element.42), channel_id=1, source_target_pairs={{0,192},{192,384},{384,576},{576,0},{1,193},{193,385},{385,577},{5... | collective-permute-start | bytes 196616 | tf_op jit(solution)/shard_map/ppermute | solution.py:188
  75.5 3.4 %collective-permute-start.3 = (f32[32,512]{1,0:T(8,128)S(1)}, f32[32,512]{1,0:T(8,128)S(1)}, u32[]{:S(2)}, u32[]{:S(2)}) collective-permute-start(f32[32,512]{1,0:T(8,128)S(1)} %get-tuple-element.43), channel_id=1, source_target_pairs={{0,576},{192,0},{384,192},{576,384},{1,577},{193,1},{385,193},{577... | collective-permute-start | bytes 196616 | tf_op jit(solution)/shard_map/ppermute | solution.py:188
  78.9 3.4 %collective-permute-start.2 = (f32[32,512]{1,0:T(8,128)S(1)}, f32[32,512]{1,0:T(8,128)S(1)}, u32[]{:S(2)}, u32[]{:S(2)}) collective-permute-start(f32[32,512]{1,0:T(8,128)S(1)} %get-tuple-element.44), channel_id=1, source_target_pairs={{0,384},{192,576},{384,0},{576,192},{1,385},{193,577},{385,1},{577... | collective-permute-start | bytes 196616 | tf_op jit(solution)/shard_map/ppermute | solution.py:188
  85.8 3.3 %collective-permute-start.5 = (f32[32,512]{1,0:T(8,128)S(1)}, f32[32,512]{1,0:T(8,128)S(1)}, u32[]{:S(2)}, u32[]{:S(2)}) collective-permute-start(f32[32,512]{1,0:T(8,128)S(1)} %add_add_fusion), channel_id=1, source_target_pairs={{0,128},{64,0},{128,64},{1,129},{65,1},{129,65},{2,130},{66,2},{13... | collective-permute-start | bytes 196616 | tf_op jit(solution)/shard_map/ppermute | solution.py:188
  92.5 2.9 %collective-permute-done.4 = f32[32,512]{1,0:T(8,128)S(1)} collective-permute-done((f32[32,512]{1,0:T(8,128)S(1)}, f32[32,512]{1,0:T(8,128)S(1)}, u32[]{:S(2)}, u32[]{:S(2)}) %collective-permute-start.4) | collective-permute-done | bytes 65568 | tf_op jit(solution)/shard_map/ppermute | solution.py:188
  95.4 6.6 %collective-permute-start.6 = (f32[1,32,512]{2,1,0:T(8,128)S(1)}, f32[1,32,512]{2,1,0:T(8,128)S(1)}, u32[]{:S(2)}, u32[]{:S(2)}) collective-permute-start(f32[1,32,512]{2,1,0:T(8,128)S(1)} %bitcast.31), channel_id=1, source_target_pairs={{0,16},{16,32},{32,48},{48,0},{1,17},{17,33},{33,49},{49,1},{2,18}... | collective-permute-start | bytes 196616 | tf_op jit(solution)/shard_map/ppermute | solution.py:188
  104.0 6.9 %collective-permute-start.7 = (f32[1,32,512]{2,1,0:T(8,128)S(1)}, f32[1,32,512]{2,1,0:T(8,128)S(1)}, u32[]{:S(2)}, u32[]{:S(2)}) collective-permute-start(f32[1,32,512]{2,1,0:T(8,128)S(1)} %bitcast.33), channel_id=1, source_target_pairs={{0,32},{16,48},{32,0},{48,16},{1,33},{17,49},{33,1},{49,17},{2,34}... | collective-permute-start | bytes 196616 | tf_op jit(solution)/shard_map/ppermute | solution.py:188
  110.9 4.4 %collective-permute-done.7 = f32[1,32,512]{2,1,0:T(8,128)S(1)} collective-permute-done((f32[1,32,512]{2,1,0:T(8,128)S(1)}, f32[1,32,512]{2,1,0:T(8,128)S(1)}, u32[]{:S(2)}, u32[]{:S(2)}) %collective-permute-start.7) | collective-permute-done | bytes 65568 | tf_op jit(solution)/shard_map/ppermute | solution.py:188
  115.3 3.9 %all-to-all-done.1 = bf16[16,272,256]{2,1,0:T(8,128)(2,1)} async-done(((bf16[16,272,256]{2,1,0:T(8,128)(2,1)}), bf16[16,272,256]{2,1,0:T(8,128)(2,1)}, u32[]{:S(2)}, u32[]{:S(2)}) %all-to-all-start.1) | async-done | bytes 2228256 | tf_op jit(solution)/shard_map/all_to_all | solution.py:228
  120.3 6.8 %fusion = f32[12,128,256]{2,1,0:T(8,128)} fusion(bf16[4352,256,1]{1,0,2:T(8,128)(2,1)} %bitcast.10, s32[4352]{0:T(1024)S(1)} %eq.69, s32[12,128]{1,0:T(8,128)S(1)} %multiply_add_fusion.1), kind=kOutput, calls=%fused_computation.4 | convolution fusion | flops 3429236736 | bytes 3824640 | tf_op jit(solution)/shard_map/dot_general | solution.py:113
  127.1 5.1 %all-to-all-start.2 = ((f32[12,128,256]{2,1,0:T(8,128)}), f32[12,128,256]{2,1,0:T(8,128)}, u32[]{:S(2)}, u32[]{:S(2)}) async-start(f32[12,128,256]{2,1,0:T(8,128)} %fusion), calls=%async_computation.2 | async-start | bytes 3145728 | tf_op jit(solution)/shard_map/all_to_all | solution.py:242
  134.3 4.3 %collective-permute-done.9 = f32[2,32,512]{2,1,0:T(8,128)S(1)} collective-permute-done((f32[2,32,512]{2,1,0:T(8,128)S(1)}, f32[2,32,512]{2,1,0:T(8,128)S(1)}, u32[]{:S(2)}, u32[]{:S(2)}) %collective-permute-start.9) | collective-permute-done | bytes 131104 | tf_op jit(solution)/shard_map/ppermute | solution.py:152
  138.6 4.2 %collective-permute-start.10 = (f32[1,32,512]{2,1,0:T(8,128)S(1)}, f32[1,32,512]{2,1,0:T(8,128)S(1)}, u32[]{:S(2)}, u32[]{:S(2)}) collective-permute-start(f32[1,32,512]{2,1,0:T(8,128)S(1)} %constant_dynamic-slice_fusion), channel_id=1, source_target_pairs={{0,4},{2,6},{4,0},{6,2},{8,12},{10,14},{12,8},{14,10},{1,5},{3,7},... | collective-permute-start | bytes 196616 | tf_op jit(solution)/shard_map/ppermute | solution.py:152
  144.9 4.5 %collective-permute-start.11 = (f32[1,32,512]{2,1,0:T(8,128)S(1)}, f32[1,32,512]{2,1,0:T(8,128)S(1)}, u32[]{:S(2)}, u32[]{:S(2)}) collective-permute-start(f32[1,32,512]{2,1,0:T(8,128)S(1)} %dynamic-slice_add_fusion.2), channel_id=1, source_target_pairs={{0,8},{2,10},{4,12},{6,14},{8,0},{10,2},{12,4},{14,6},{1,9},{3,11}... | collective-permute-start | bytes 196616 | tf_op jit(solution)/shard_map/ppermute | solution.py:152
  149.5 4.4 %collective-permute-done.11 = f32[1,32,512]{2,1,0:T(8,128)S(1)} collective-permute-done((f32[1,32,512]{2,1,0:T(8,128)S(1)}, f32[1,32,512]{2,1,0:T(8,128)S(1)}, u32[]{:S(2)}, u32[]{:S(2)}) %collective-permute-start.11) | collective-permute-done | bytes 65568 | tf_op jit(solution)/shard_map/ppermute | solution.py:152
  154.0 4.8 %all-to-all-done.2.sums_ref = f32[12,128,256]{2,1,0:T(8,128)} async-done(((f32[12,128,256]{2,1,0:T(8,128)}), f32[12,128,256]{2,1,0:T(8,128)}, u32[]{:S(2)}, u32[]{:S(2)}) %all-to-all-start.2) | async-done | bytes 1572896 | tf_op jit(solution)/shard_map/all_to_all | solution.py:242
  161.9 4.4 %all-to-all-start.3 = ((f32[12,136,256]{2,1,0:T(8,128)}), f32[12,136,256]{2,1,0:T(8,128)}, u32[]{:S(2)}, u32[]{:S(2)}) async-start(f32[12,136,256]{2,1,0:T(8,128)} %copy-done.2), calls=%async_computation.3 | async-start | bytes 3342336 | tf_op jit(solution)/shard_map/all_to_all | solution.py:248
  166.3 2.9 %collective-permute-start.12 = (f32[1,32,512]{2,1,0:T(8,128)S(1)}, f32[1,32,512]{2,1,0:T(8,128)S(1)}, u32[]{:S(2)}, u32[]{:S(2)}) collective-permute-start(f32[1,32,512]{2,1,0:T(8,128)S(1)} %add.206), channel_id=1, source_target_pairs={{0,4},{2,6},{4,0},{6,2},{8,12},{10,14},{12,8},{14,10},{1,5},{3,7},... | collective-permute-start | bytes 196616 | tf_op jit(solution)/shard_map/ppermute | solution.py:152
  169.2 3.0 %collective-permute-done.12 = f32[1,32,512]{2,1,0:T(8,128)S(1)} collective-permute-done((f32[1,32,512]{2,1,0:T(8,128)S(1)}, f32[1,32,512]{2,1,0:T(8,128)S(1)}, u32[]{:S(2)}, u32[]{:S(2)}) %collective-permute-start.12) | collective-permute-done | bytes 65568 | tf_op jit(solution)/shard_map/ppermute | solution.py:152
  172.2 3.4 %collective-permute-start.13 = (f32[2,32,512]{2,1,0:T(8,128)S(1)}, f32[2,32,512]{2,1,0:T(8,128)S(1)}, u32[]{:S(2)}, u32[]{:S(2)}) collective-permute-start(f32[2,32,512]{2,1,0:T(8,128)S(1)} %pad_maximum_fusion.3), channel_id=1, source_target_pairs={{0,2},{2,0},{4,6},{6,4},{8,10},{10,8},{12,14},{14,12},{1,3},{3,1},... | collective-permute-start | bytes 393224 | tf_op jit(solution)/shard_map/ppermute | solution.py:152
  175.6 2.7 %collective-permute-done.13 = f32[2,32,512]{2,1,0:T(8,128)S(1)} collective-permute-done((f32[2,32,512]{2,1,0:T(8,128)S(1)}, f32[2,32,512]{2,1,0:T(8,128)S(1)}, u32[]{:S(2)}, u32[]{:S(2)}) %collective-permute-start.13) | collective-permute-done | bytes 131104 | tf_op jit(solution)/shard_map/ppermute | solution.py:152
  178.4 3.6 %collective-permute-start.14 = (f32[4,32,512]{2,1,0:T(8,128)S(1)}, f32[4,32,512]{2,1,0:T(8,128)S(1)}, u32[]{:S(2)}, u32[]{:S(2)}) collective-permute-start(f32[4,32,512]{2,1,0:T(8,128)S(1)} %pad_maximum_fusion.2), channel_id=1, source_target_pairs={{0,192},{192,384},{384,576},{576,0},{1,193},{193,385},{385,577},{5... | collective-permute-start | bytes 786440 | tf_op jit(solution)/shard_map/ppermute | solution.py:188
  182.0 4.3 %collective-permute-start.15 = (f32[4,32,512]{2,1,0:T(8,128)S(1)}, f32[4,32,512]{2,1,0:T(8,128)S(1)}, u32[]{:S(2)}, u32[]{:S(2)}) collective-permute-start(f32[4,32,512]{2,1,0:T(8,128)S(1)} %pad_maximum_fusion.2), channel_id=1, source_target_pairs={{0,384},{192,576},{384,0},{576,192},{1,385},{193,577},{385,1},{577... | collective-permute-start | bytes 786440 | tf_op jit(solution)/shard_map/ppermute | solution.py:188
  186.3 3.1 %collective-permute-start.16 = (f32[4,32,512]{2,1,0:T(8,128)S(1)}, f32[4,32,512]{2,1,0:T(8,128)S(1)}, u32[]{:S(2)}, u32[]{:S(2)}) collective-permute-start(f32[4,32,512]{2,1,0:T(8,128)S(1)} %pad_maximum_fusion.2), channel_id=1, source_target_pairs={{0,576},{192,0},{384,192},{576,384},{1,577},{193,1},{385,193},{577... | collective-permute-start | bytes 786440 | tf_op jit(solution)/shard_map/ppermute | solution.py:188
  189.5 9.9 %collective-permute-done.14 = f32[4,32,512]{2,1,0:T(8,128)S(1)} collective-permute-done((f32[4,32,512]{2,1,0:T(8,128)S(1)}, f32[4,32,512]{2,1,0:T(8,128)S(1)}, u32[]{:S(2)}, u32[]{:S(2)}) %collective-permute-start.14) | collective-permute-done | bytes 262176 | tf_op jit(solution)/shard_map/ppermute | solution.py:188
  199.4 6.7 %collective-permute-done.15 = f32[4,32,512]{2,1,0:T(8,128)S(1)} collective-permute-done((f32[4,32,512]{2,1,0:T(8,128)S(1)}, f32[4,32,512]{2,1,0:T(8,128)S(1)}, u32[]{:S(2)}, u32[]{:S(2)}) %collective-permute-start.15) | collective-permute-done | bytes 262176 | tf_op jit(solution)/shard_map/ppermute | solution.py:188
  206.2 2.6 %collective-permute-start.17 = (f32[4,128,512]{2,1,0:T(8,128)S(1)}, f32[4,128,512]{2,1,0:T(8,128)}, u32[]{:S(2)}, u32[]{:S(2)}) collective-permute-start(f32[4,128,512]{2,1,0:T(8,128)S(1)} %constant_dynamic-update-slice_fusion.1), channel_id=1, source_target_pairs={{0,1},{1,0},{2,3},{3,2},{4,5},{5,4},{6,7},{7,6},{8,9},{9,8},{10,11... | collective-permute-start | bytes 3145736 | tf_op jit(solution)/shard_map/ppermute | solution.py:152
  210.4 2.8 %slice.37 = f32[12,128,256]{2,1,0:T(8,128)} slice(f32[12,136,256]{2,1,0:T(8,128)} %all-to-all-done.3), slice={[0:12], [0:128], [0:256]} | slice | bytes 3145728 | tf_op jit(solution)/shard_map/slice | solution.py:252
  (89 shorter events, 35.5 us)
Async XLA Ops:
  0.6 84.0 %copy-start = (bf16[4096,256]{1,0:T(8,128)(2,1)S(1)}, bf16[4096,256]{1,0:T(8,128)(2,1)}, u32[]{:S(2)}) copy-start(bf16[4096,256]{1,0:T(8,128)(2,1)} %param.16) | copy-start | bytes 6291460
  2.5 46.8 %all-to-all-start = ((bf16[4,128,256]{2,1,0:T(8,128)(2,1)}), bf16[4,128,256]{2,1,0:T(8,128)(2,1)S(1)}, u32[]{:S(2)}, u32[]{:S(2)}) async-start(bf16[4,128,256]{2,1,0:T(8,128)(2,1)} %pad_maximum_fusion.1), calls=%async_computation | async-start | bytes 524288 | tf_op jit(solution)/shard_map/all_to_all | solution.py:223
  49.3 9.0 %copy-start.9 = (bf16[4,128,256]{2,1,0:T(8,128)(2,1)}, bf16[4,128,256]{2,1,0:T(8,128)(2,1)S(1)}, u32[]{:S(2)}) copy-start(bf16[4,128,256]{2,1,0:T(8,128)(2,1)S(1)} %all-to-all-done) | copy-start | bytes 786436
  49.3 1.3 copy-start.3
  56.9 1.4 copy-start.1
  58.3 61.0 %all-to-all-start.1 = ((bf16[16,272,256]{2,1,0:T(8,128)(2,1)}), bf16[16,272,256]{2,1,0:T(8,128)(2,1)}, u32[]{:S(2)}, u32[]{:S(2)}) async-start(bf16[16,272,256]{2,1,0:T(8,128)(2,1)} %copy-done.1), calls=%async_computation.1 | async-start | bytes 4456448 | tf_op jit(solution)/shard_map/all_to_all | solution.py:228
  67.5 14.8 %copy-start.4 = (f32[4096]{0:T(1024)S(1)}, f32[4096]{0:T(1024)}, u32[]{:S(2)}) copy-start(f32[4096]{0:T(1024)} %param.18) | copy-start | bytes 49156
  67.5 16.0 %copy-start.5 = (f32[4096]{0:T(1024)S(1)}, f32[4096]{0:T(1024)}, u32[]{:S(2)}) copy-start(f32[4096]{0:T(1024)} %param.17) | copy-start | bytes 49156
  68.8 22.5 %copy-start.6 = (f32[4096]{0:T(1024)S(1)}, f32[4096]{0:T(1024)}, u32[]{:S(2)}) copy-start(f32[4096]{0:T(1024)} %param.19) | copy-start | bytes 49156
  68.9 3.4 %collective-permute-start = (f32[128,512]{1,0:T(8,128)S(1)}, f32[128,512]{1,0:T(8,128)S(1)}, u32[]{:S(2)}, u32[]{:S(2)}) collective-permute-start(f32[128,512]{1,0:T(8,128)S(1)} %constant_dynamic-slice_fusion.5), channel_id=1, source_target_pairs={{0,1},{1,0},{2,3},{3,2},{4,5},{5,4},{6,7},{7,6},{8,9},{9,8},{10,11... | collective-permute-start | bytes 786440 | tf_op jit(solution)/shard_map/ppermute | solution.py:152
  72.4 13.2 %collective-permute-start.1 = (f32[32,512]{1,0:T(8,128)S(1)}, f32[32,512]{1,0:T(8,128)S(1)}, u32[]{:S(2)}, u32[]{:S(2)}) collective-permute-start(f32[32,512]{1,0:T(8,128)S(1)} %get-tuple-element.42), channel_id=1, source_target_pairs={{0,192},{192,384},{384,576},{576,0},{1,193},{193,385},{385,577},{5... | collective-permute-start | bytes 196616 | tf_op jit(solution)/shard_map/ppermute | solution.py:188
  75.5 10.1 %collective-permute-start.3 = (f32[32,512]{1,0:T(8,128)S(1)}, f32[32,512]{1,0:T(8,128)S(1)}, u32[]{:S(2)}, u32[]{:S(2)}) collective-permute-start(f32[32,512]{1,0:T(8,128)S(1)} %get-tuple-element.43), channel_id=1, source_target_pairs={{0,576},{192,0},{384,192},{576,384},{1,577},{193,1},{385,193},{577... | collective-permute-start | bytes 196616 | tf_op jit(solution)/shard_map/ppermute | solution.py:188
  78.9 6.9 %collective-permute-start.2 = (f32[32,512]{1,0:T(8,128)S(1)}, f32[32,512]{1,0:T(8,128)S(1)}, u32[]{:S(2)}, u32[]{:S(2)}) collective-permute-start(f32[32,512]{1,0:T(8,128)S(1)} %get-tuple-element.44), channel_id=1, source_target_pairs={{0,384},{192,576},{384,0},{576,192},{1,385},{193,577},{385,1},{577... | collective-permute-start | bytes 196616 | tf_op jit(solution)/shard_map/ppermute | solution.py:188
  85.8 6.7 %collective-permute-start.5 = (f32[32,512]{1,0:T(8,128)S(1)}, f32[32,512]{1,0:T(8,128)S(1)}, u32[]{:S(2)}, u32[]{:S(2)}) collective-permute-start(f32[32,512]{1,0:T(8,128)S(1)} %add_add_fusion), channel_id=1, source_target_pairs={{0,128},{64,0},{128,64},{1,129},{65,1},{129,65},{2,130},{66,2},{13... | collective-permute-start | bytes 196616 | tf_op jit(solution)/shard_map/ppermute | solution.py:188
  89.1 6.3 %collective-permute-start.4 = (f32[32,512]{1,0:T(8,128)S(1)}, f32[32,512]{1,0:T(8,128)S(1)}, u32[]{:S(2)}, u32[]{:S(2)}) collective-permute-start(f32[32,512]{1,0:T(8,128)S(1)} %add_add_fusion), channel_id=1, source_target_pairs={{0,64},{64,128},{128,0},{1,65},{65,129},{129,1},{2,66},{66,130},{1... | collective-permute-start | bytes 196616 | tf_op jit(solution)/shard_map/ppermute | solution.py:188
  95.4 15.5 %collective-permute-start.6 = (f32[1,32,512]{2,1,0:T(8,128)S(1)}, f32[1,32,512]{2,1,0:T(8,128)S(1)}, u32[]{:S(2)}, u32[]{:S(2)}) collective-permute-start(f32[1,32,512]{2,1,0:T(8,128)S(1)} %bitcast.31), channel_id=1, source_target_pairs={{0,16},{16,32},{32,48},{48,0},{1,17},{17,33},{33,49},{49,1},{2,18}... | collective-permute-start | bytes 196616 | tf_op jit(solution)/shard_map/ppermute | solution.py:188
  102.0 13.3 %collective-permute-start.8 = (f32[1,32,512]{2,1,0:T(8,128)S(1)}, f32[1,32,512]{2,1,0:T(8,128)S(1)}, u32[]{:S(2)}, u32[]{:S(2)}) collective-permute-start(f32[1,32,512]{2,1,0:T(8,128)S(1)} %bitcast.32), channel_id=1, source_target_pairs={{0,48},{16,0},{32,16},{48,32},{1,49},{17,1},{33,17},{49,33},{2,50}... | collective-permute-start | bytes 196616 | tf_op jit(solution)/shard_map/ppermute | solution.py:188
  104.0 11.3 %collective-permute-start.7 = (f32[1,32,512]{2,1,0:T(8,128)S(1)}, f32[1,32,512]{2,1,0:T(8,128)S(1)}, u32[]{:S(2)}, u32[]{:S(2)}) collective-permute-start(f32[1,32,512]{2,1,0:T(8,128)S(1)} %bitcast.33), channel_id=1, source_target_pairs={{0,32},{16,48},{32,0},{48,16},{1,33},{17,49},{33,1},{49,17},{2,34}... | collective-permute-start | bytes 196616 | tf_op jit(solution)/shard_map/ppermute | solution.py:188
  127.1 31.7 %all-to-all-start.2 = ((f32[12,128,256]{2,1,0:T(8,128)}), f32[12,128,256]{2,1,0:T(8,128)}, u32[]{:S(2)}, u32[]{:S(2)}) async-start(f32[12,128,256]{2,1,0:T(8,128)} %fusion), calls=%async_computation.2 | async-start | bytes 3145728 | tf_op jit(solution)/shard_map/all_to_all | solution.py:242
  132.3 6.3 %collective-permute-start.9 = (f32[2,32,512]{2,1,0:T(8,128)S(1)}, f32[2,32,512]{2,1,0:T(8,128)S(1)}, u32[]{:S(2)}, u32[]{:S(2)}) collective-permute-start(f32[2,32,512]{2,1,0:T(8,128)S(1)} %constant_dynamic-slice_fusion.1), channel_id=1, source_target_pairs={{0,2},{2,0},{4,6},{6,4},{8,10},{10,8},{12,14},{14,12},{1,3},{3,1},... | collective-permute-start | bytes 393224 | tf_op jit(solution)/shard_map/ppermute | solution.py:152
  138.6 6.3 %collective-permute-start.10 = (f32[1,32,512]{2,1,0:T(8,128)S(1)}, f32[1,32,512]{2,1,0:T(8,128)S(1)}, u32[]{:S(2)}, u32[]{:S(2)}) collective-permute-start(f32[1,32,512]{2,1,0:T(8,128)S(1)} %constant_dynamic-slice_fusion), channel_id=1, source_target_pairs={{0,4},{2,6},{4,0},{6,2},{8,12},{10,14},{12,8},{14,10},{1,5},{3,7},... | collective-permute-start | bytes 196616 | tf_op jit(solution)/shard_map/ppermute | solution.py:152
  144.9 9.0 %collective-permute-start.11 = (f32[1,32,512]{2,1,0:T(8,128)S(1)}, f32[1,32,512]{2,1,0:T(8,128)S(1)}, u32[]{:S(2)}, u32[]{:S(2)}) collective-permute-start(f32[1,32,512]{2,1,0:T(8,128)S(1)} %dynamic-slice_add_fusion.2), channel_id=1, source_target_pairs={{0,8},{2,10},{4,12},{6,14},{8,0},{10,2},{12,4},{14,6},{1,9},{3,11}... | collective-permute-start | bytes 196616 | tf_op jit(solution)/shard_map/ppermute | solution.py:152
  160.7 1.2 copy-start.2
  161.9 48.5 %all-to-all-start.3 = ((f32[12,136,256]{2,1,0:T(8,128)}), f32[12,136,256]{2,1,0:T(8,128)}, u32[]{:S(2)}, u32[]{:S(2)}) async-start(f32[12,136,256]{2,1,0:T(8,128)} %copy-done.2), calls=%async_computation.3 | async-start | bytes 3342336 | tf_op jit(solution)/shard_map/all_to_all | solution.py:248
  166.3 5.9 %collective-permute-start.12 = (f32[1,32,512]{2,1,0:T(8,128)S(1)}, f32[1,32,512]{2,1,0:T(8,128)S(1)}, u32[]{:S(2)}, u32[]{:S(2)}) collective-permute-start(f32[1,32,512]{2,1,0:T(8,128)S(1)} %add.206), channel_id=1, source_target_pairs={{0,4},{2,6},{4,0},{6,2},{8,12},{10,14},{12,8},{14,10},{1,5},{3,7},... | collective-permute-start | bytes 196616 | tf_op jit(solution)/shard_map/ppermute | solution.py:152
  172.2 6.1 %collective-permute-start.13 = (f32[2,32,512]{2,1,0:T(8,128)S(1)}, f32[2,32,512]{2,1,0:T(8,128)S(1)}, u32[]{:S(2)}, u32[]{:S(2)}) collective-permute-start(f32[2,32,512]{2,1,0:T(8,128)S(1)} %pad_maximum_fusion.3), channel_id=1, source_target_pairs={{0,2},{2,0},{4,6},{6,4},{8,10},{10,8},{12,14},{14,12},{1,3},{3,1},... | collective-permute-start | bytes 393224 | tf_op jit(solution)/shard_map/ppermute | solution.py:152
  178.4 21.0 %collective-permute-start.14 = (f32[4,32,512]{2,1,0:T(8,128)S(1)}, f32[4,32,512]{2,1,0:T(8,128)S(1)}, u32[]{:S(2)}, u32[]{:S(2)}) collective-permute-start(f32[4,32,512]{2,1,0:T(8,128)S(1)} %pad_maximum_fusion.2), channel_id=1, source_target_pairs={{0,192},{192,384},{384,576},{576,0},{1,193},{193,385},{385,577},{5... | collective-permute-start | bytes 786440 | tf_op jit(solution)/shard_map/ppermute | solution.py:188
  182.0 24.2 %collective-permute-start.15 = (f32[4,32,512]{2,1,0:T(8,128)S(1)}, f32[4,32,512]{2,1,0:T(8,128)S(1)}, u32[]{:S(2)}, u32[]{:S(2)}) collective-permute-start(f32[4,32,512]{2,1,0:T(8,128)S(1)} %pad_maximum_fusion.2), channel_id=1, source_target_pairs={{0,384},{192,576},{384,0},{576,192},{1,385},{193,577},{385,1},{577... | collective-permute-start | bytes 786440 | tf_op jit(solution)/shard_map/ppermute | solution.py:188
  186.3 19.8 %collective-permute-start.16 = (f32[4,32,512]{2,1,0:T(8,128)S(1)}, f32[4,32,512]{2,1,0:T(8,128)S(1)}, u32[]{:S(2)}, u32[]{:S(2)}) collective-permute-start(f32[4,32,512]{2,1,0:T(8,128)S(1)} %pad_maximum_fusion.2), channel_id=1, source_target_pairs={{0,576},{192,0},{384,192},{576,384},{1,577},{193,1},{385,193},{577... | collective-permute-start | bytes 786440 | tf_op jit(solution)/shard_map/ppermute | solution.py:188
  206.2 8.6 %collective-permute-start.17 = (f32[4,128,512]{2,1,0:T(8,128)S(1)}, f32[4,128,512]{2,1,0:T(8,128)}, u32[]{:S(2)}, u32[]{:S(2)}) collective-permute-start(f32[4,128,512]{2,1,0:T(8,128)S(1)} %constant_dynamic-update-slice_fusion.1), channel_id=1, source_target_pairs={{0,1},{1,0},{2,3},{3,2},{4,5},{5,4},{6,7},{7,6},{8,9},{9,8},{10,11... | collective-permute-start | bytes 3145736 | tf_op jit(solution)/shard_map/ppermute | solution.py:152
  210.4 4.4 %copy-start.7 = (f32[4,256,512]{2,1,0:T(8,128)S(1)}, f32[4,256,512]{2,1,0:T(8,128)}, u32[]{:S(2)}) copy-start(f32[4,256,512]{2,1,0:T(8,128)} %pad_maximum_fusion) | copy-start | bytes 6291460
  216.1 1.3 copy-start.8

commit v7 on v6

--- a/solution.py
+++ b/solution.py
@@ -174,14 +174,17 @@
     return total
 
 
-def gather(a, axis, size, dim=0):
+def place(pieces, axis, size, dim):
     me = lax.axis_index(axis)
-    n = a.shape[dim]
-    got = [shift(a, axis, size, k) for k in range(1, size)]
-    out = jnp.concatenate([a] * size, axis=dim)
-    for k, piece in enumerate(got, 1):
+    n = pieces[0].shape[dim]
+    out = jnp.concatenate([pieces[0]] * size, axis=dim)
+    for k, piece in enumerate(pieces[1:], 1):
         out = lax.dynamic_update_slice_in_dim(out, piece, lax.rem(me - k + size, size) * n, dim)
     return out
+
+
+def gather(a, axis, size, dim=0):
+    return place([a] + [shift(a, axis, size, k) for k in range(1, size)], axis, size, dim)
 
 
 def shift(a, axis, size, k):
@@ -241,18 +244,18 @@
     sums = collect(got, touch).reshape(parts, part, width)
     sums = lax.all_to_all(sums, REP, 0, 0, tiled=True)
     w = halve(w, "y", NY, 1, 0)
-    w = halve(w, "y", NY, 2, 0)
+    w = w + swap(w, "y", NY, 2)
     w = w + swap(w, "y", NY, 4)
     sums, w = tie(sums, w)
 
     payload = lax.all_to_all(update(sums, old, old_accum), REP, 0, 0, tiled=True)
-    w = double(w, "y", NY, 2, 0)
     w = double(w, "y", NY, 1, 0)
-    w = gather(w, "x", NX, 1)
+    pieces = [w] + [shift(w, "x", NX, k) for k in range(1, NX)]
     new_codes = payload[:, :part].reshape(touch, width)
     new_scale, lowest, new_accum = (payload[:, part + i, :part].reshape(touch) for i in range(3))
+    pieces[-1], new_codes, new_scale, lowest, new_accum = tie(pieces[-1], new_codes, new_scale, lowest, new_accum)
+    w = place(pieces, "x", NX, 1)
     other = swap(w, "c", NC, 1)
-    other, new_codes, new_scale, lowest, new_accum = tie(other, new_codes, new_scale, lowest, new_accum)
     side = lax.axis_index("c") * w.shape[1]
     weight_grad = jnp.concatenate([w, w], axis=1)
     weight_grad = lax.dynamic_update_slice_in_dim(weight_grad, other, w.shape[1] - side, 1)

time: 219 us -> 218 us (level)
    ppermute x7 -> x6, waiting for transfers between devices: 17.1 us -> 23.5 us  [swap(): return lax.ppermute(a, axis, [(i, i ^ bit) for i in range(size)])]
    all_to_all x1, waiting for transfers between devices: 4.84 us -> 0.01 us  [shards(): sums = lax.all_to_all(sums, REP, 0, 0, tiled=True)]
    ppermute x7 -> x6, starting transfers between devices: 21.5 us -> 18.7 us  [swap(): return lax.ppermute(a, axis, [(i, i ^ bit) for i in range(size)])]
    unnamed x22 -> x20, local copies, waits for them, and re-layouts: 5.37 us -> 5.34 us
  transfers between devices with their start and end apart: 22 -> 21, of which waited for: 13 -> 12; matrix products, arithmetic and copies ran while one was open for 7% -> 7% of each run, Pallas kernels for 0% -> 0%
where the time goes in v7:
time: 218 us; the launch traced here: 216 us
  starting transfers between devices  95.1 us (44%)
  waiting for transfers between devices  51.2 us (23%)
  blocking collectives  28.7 us (13%)
  local copies, waits for them, and re-layouts  17.1 us (8%)
  Pallas kernels  8.15 us (4%)
  matrix products  8.04 us (4%)
  other arithmetic  6.24 us (3%)
    ppermute x11, starting transfers between devices, shift(): return lax.ppermute(a, axis, [(i, (i + k) % size) for i in range(size)])  41.3 us
    all_gather x1, blocking collectives, shards(): near = lax.all_gather(near, 'zh', axis=0, tiled=False)  28.7 us
    ppermute x11, waiting for transfers between devices, shift(): return lax.ppermute(a, axis, [(i, (i + k) % size) for i in range(size)])  23.7 us
    ppermute x6, waiting for transfers between devices, swap(): return lax.ppermute(a, axis, [(i, i ^ bit) for i in range(size)])  23.5 us
    ppermute x6, starting transfers between devices, swap(): return lax.ppermute(a, axis, [(i, i ^ bit) for i in range(size)])  18.7 us
    all_to_all x1, starting transfers between devices, shards(): columns = lax.all_to_all(columns, 'zh', 0, 0, tiled=True)  15 us
    all_to_all x1, starting transfers between devices, shards(): got = lax.all_to_all(rows, ('y', 'c'), 0, 0, tiled=True)  9.23 us
    dot_general x1, matrix products, collect(): return jnp.dot(selector, got.reshape(-1, width), preferred_element_type=f32)  6.78 us
  transfers between devices with their start and end apart: 21, of which 12 were waited for; matrix products, arithmetic and copies ran while one was open for 7% of the time, Pallas kernels for 0%

profile of v7, /device:TPU:1, one launch (start us, length us, event | category | flops | bytes accessed | tf_op | source)
XLA Modules:
  0.0 215.8 jit_solution(10344128476895177383)
XLA Ops:
  2.5 15.0 %all-to-all-start = ((bf16[4,128,256]{2,1,0:T(8,128)(2,1)}), bf16[4,128,256]{2,1,0:T(8,128)(2,1)S(1)}, u32[]{:S(2)}, u32[]{:S(2)}) async-start(bf16[4,128,256]{2,1,0:T(8,128)(2,1)} %pad_maximum_fusion.1), calls=%async_computation | async-start | bytes 524288 | tf_op jit(solution)/shard_map/all_to_all | solution.py:226
  20.6 28.7 %all-gather = bf16[512,640]{1,0:T(8,128)(2,1)S(1)} all-gather(bf16[128,640]{1,0:T(8,128)(2,1)S(1)} %fusion.7), channel_id=2, replica_groups=mesh['x'=4,'zl'=3,'zh'=4,'y'=8,'c'=2] {'zh'}, dimensions={0}, use_global_device_ids=true | all-gather | bytes 819200 | tf_op jit(solution)/shard_map/all_gather | solution.py:227
  50.6 6.3 %dispatch.1 = bf16[16,272,256]{2,1,0:T(8,128)(2,1)S(1)} custom-call(s32[1]{0:T(128)} %bitcast.refs_0_, bf16[4,128,640]{2,1,0:T(8,128)(2,1)S(1)} %bitcast.27, bf16[1024,512]{1,0:T(8,128)(2,1)S(1)} %copy-done.3), custom_call_target="tpu_custom_call" | custom-call | tf_op jit(solution)/shard_map/dispatch/pallas_call | solution.py:96
  58.3 9.2 %all-to-all-start.1 = ((bf16[16,272,256]{2,1,0:T(8,128)(2,1)}), bf16[16,272,256]{2,1,0:T(8,128)(2,1)}, u32[]{:S(2)}, u32[]{:S(2)}) async-start(bf16[16,272,256]{2,1,0:T(8,128)(2,1)} %copy-done.1), calls=%async_computation.1 | async-start | bytes 4456448 | tf_op jit(solution)/shard_map/all_to_all | solution.py:231
  68.9 2.1 collective-permute-start
  72.4 3.1 %collective-permute-start.1 = (f32[32,512]{1,0:T(8,128)S(1)}, f32[32,512]{1,0:T(8,128)S(1)}, u32[]{:S(2)}, u32[]{:S(2)}) collective-permute-start(f32[32,512]{1,0:T(8,128)S(1)} %get-tuple-element.42), channel_id=1, source_target_pairs={{0,192},{192,384},{384,576},{576,0},{1,193},{193,385},{385,577},{5... | collective-permute-start | bytes 196616 | tf_op jit(solution)/shard_map/ppermute | solution.py:191
  75.5 3.4 %collective-permute-start.3 = (f32[32,512]{1,0:T(8,128)S(1)}, f32[32,512]{1,0:T(8,128)S(1)}, u32[]{:S(2)}, u32[]{:S(2)}) collective-permute-start(f32[32,512]{1,0:T(8,128)S(1)} %get-tuple-element.43), channel_id=1, source_target_pairs={{0,576},{192,0},{384,192},{576,384},{1,577},{193,1},{385,193},{577... | collective-permute-start | bytes 196616 | tf_op jit(solution)/shard_map/ppermute | solution.py:191
  78.9 3.4 %collective-permute-start.2 = (f32[32,512]{1,0:T(8,128)S(1)}, f32[32,512]{1,0:T(8,128)S(1)}, u32[]{:S(2)}, u32[]{:S(2)}) collective-permute-start(f32[32,512]{1,0:T(8,128)S(1)} %get-tuple-element.44), channel_id=1, source_target_pairs={{0,384},{192,576},{384,0},{576,192},{1,385},{193,577},{385,1},{577... | collective-permute-start | bytes 196616 | tf_op jit(solution)/shard_map/ppermute | solution.py:191
  85.8 3.3 %collective-permute-start.5 = (f32[32,512]{1,0:T(8,128)S(1)}, f32[32,512]{1,0:T(8,128)S(1)}, u32[]{:S(2)}, u32[]{:S(2)}) collective-permute-start(f32[32,512]{1,0:T(8,128)S(1)} %add_add_fusion), channel_id=1, source_target_pairs={{0,128},{64,0},{128,64},{1,129},{65,1},{129,65},{2,130},{66,2},{13... | collective-permute-start | bytes 196616 | tf_op jit(solution)/shard_map/ppermute | solution.py:191
  89.1 2.0 collective-permute-start.4
  92.5 2.9 %collective-permute-done.4 = f32[32,512]{1,0:T(8,128)S(1)} collective-permute-done((f32[32,512]{1,0:T(8,128)S(1)}, f32[32,512]{1,0:T(8,128)S(1)}, u32[]{:S(2)}, u32[]{:S(2)}) %collective-permute-start.4) | collective-permute-done | bytes 65568 | tf_op jit(solution)/shard_map/ppermute | solution.py:191
  95.4 6.6 %collective-permute-start.6 = (f32[1,32,512]{2,1,0:T(8,128)S(1)}, f32[1,32,512]{2,1,0:T(8,128)S(1)}, u32[]{:S(2)}, u32[]{:S(2)}) collective-permute-start(f32[1,32,512]{2,1,0:T(8,128)S(1)} %bitcast.31), channel_id=1, source_target_pairs={{0,16},{16,32},{32,48},{48,0},{1,17},{17,33},{33,49},{49,1},{2,18}... | collective-permute-start | bytes 196616 | tf_op jit(solution)/shard_map/ppermute | solution.py:191
  104.0 6.9 %collective-permute-start.7 = (f32[1,32,512]{2,1,0:T(8,128)S(1)}, f32[1,32,512]{2,1,0:T(8,128)S(1)}, u32[]{:S(2)}, u32[]{:S(2)}) collective-permute-start(f32[1,32,512]{2,1,0:T(8,128)S(1)} %bitcast.33), channel_id=1, source_target_pairs={{0,32},{16,48},{32,0},{48,16},{1,33},{17,49},{33,1},{49,17},{2,34}... | collective-permute-start | bytes 196616 | tf_op jit(solution)/shard_map/ppermute | solution.py:191
  110.9 4.4 %collective-permute-done.7 = f32[1,32,512]{2,1,0:T(8,128)S(1)} collective-permute-done((f32[1,32,512]{2,1,0:T(8,128)S(1)}, f32[1,32,512]{2,1,0:T(8,128)S(1)}, u32[]{:S(2)}, u32[]{:S(2)}) %collective-permute-start.7) | collective-permute-done | bytes 65568 | tf_op jit(solution)/shard_map/ppermute | solution.py:191
  115.3 3.9 %all-to-all-done.1 = bf16[16,272,256]{2,1,0:T(8,128)(2,1)} async-done(((bf16[16,272,256]{2,1,0:T(8,128)(2,1)}), bf16[16,272,256]{2,1,0:T(8,128)(2,1)}, u32[]{:S(2)}, u32[]{:S(2)}) %all-to-all-start.1) | async-done | bytes 2228256 | tf_op jit(solution)/shard_map/all_to_all | solution.py:231
  120.3 6.8 %fusion = f32[12,128,256]{2,1,0:T(8,128)} fusion(bf16[4352,256,1]{1,0,2:T(8,128)(2,1)} %bitcast.10, s32[4352]{0:T(1024)S(1)} %eq.65, s32[12,128]{1,0:T(8,128)S(1)} %multiply_add_fusion.1), kind=kOutput, calls=%fused_computation.4 | convolution fusion | flops 3429236736 | bytes 3824640 | tf_op jit(solution)/shard_map/dot_general | solution.py:113
  127.1 5.1 %all-to-all-start.2 = ((f32[12,128,256]{2,1,0:T(8,128)}), f32[12,128,256]{2,1,0:T(8,128)}, u32[]{:S(2)}, u32[]{:S(2)}) async-start(f32[12,128,256]{2,1,0:T(8,128)} %fusion), calls=%async_computation.2 | async-start | bytes 3145728 | tf_op jit(solution)/shard_map/all_to_all | solution.py:245
  134.3 4.3 %collective-permute-done.9 = f32[2,32,512]{2,1,0:T(8,128)S(1)} collective-permute-done((f32[2,32,512]{2,1,0:T(8,128)S(1)}, f32[2,32,512]{2,1,0:T(8,128)S(1)}, u32[]{:S(2)}, u32[]{:S(2)}) %collective-permute-start.9) | collective-permute-done | bytes 131104 | tf_op jit(solution)/shard_map/ppermute | solution.py:152
  138.6 4.2 %collective-permute-start.10 = (f32[2,32,512]{2,1,0:T(8,128)S(1)}, f32[2,32,512]{2,1,0:T(8,128)S(1)}, u32[]{:S(2)}, u32[]{:S(2)}) collective-permute-start(f32[2,32,512]{2,1,0:T(8,128)S(1)} %dynamic-slice_add_fusion.1), channel_id=1, source_target_pairs={{0,4},{2,6},{4,0},{6,2},{8,12},{10,14},{12,8},{14,10},{1,5},{3,7},... | collective-permute-start | bytes 393224 | tf_op jit(solution)/shard_map/ppermute | solution.py:152
  142.8 6.0 %collective-permute-done.10 = f32[2,32,512]{2,1,0:T(8,128)S(1)} collective-permute-done((f32[2,32,512]{2,1,0:T(8,128)S(1)}, f32[2,32,512]{2,1,0:T(8,128)S(1)}, u32[]{:S(2)}, u32[]{:S(2)}) %collective-permute-start.10) | collective-permute-done | bytes 131104 | tf_op jit(solution)/shard_map/ppermute | solution.py:152
  148.8 2.7 %collective-permute-start.11 = (f32[2,32,512]{2,1,0:T(8,128)S(1)}, f32[2,32,512]{2,1,0:T(8,128)S(1)}, u32[]{:S(2)}, u32[]{:S(2)}) collective-permute-start(f32[2,32,512]{2,1,0:T(8,128)S(1)} %add.195), channel_id=1, source_target_pairs={{0,8},{2,10},{4,12},{6,14},{8,0},{10,2},{12,4},{14,6},{1,9},{3,11}... | collective-permute-start | bytes 393224 | tf_op jit(solution)/shard_map/ppermute | solution.py:152
  151.6 7.2 %collective-permute-done.11 = f32[2,32,512]{2,1,0:T(8,128)S(1)} collective-permute-done((f32[2,32,512]{2,1,0:T(8,128)S(1)}, f32[2,32,512]{2,1,0:T(8,128)S(1)}, u32[]{:S(2)}, u32[]{:S(2)}) %collective-permute-start.11) | collective-permute-done | bytes 131104 | tf_op jit(solution)/shard_map/ppermute | solution.py:152
  161.9 5.6 %all-to-all-start.3 = ((f32[12,136,256]{2,1,0:T(8,128)}), f32[12,136,256]{2,1,0:T(8,128)}, u32[]{:S(2)}, u32[]{:S(2)}) async-start(f32[12,136,256]{2,1,0:T(8,128)} %copy-done.2), calls=%async_computation.3 | async-start | bytes 3342336 | tf_op jit(solution)/shard_map/all_to_all | solution.py:251
  167.5 2.4 %collective-permute-start.12 = (f32[2,32,512]{2,1,0:T(8,128)S(1)}, f32[2,32,512]{2,1,0:T(8,128)S(1)}, u32[]{:S(2)}, u32[]{:S(2)}) collective-permute-start(f32[2,32,512]{2,1,0:T(8,128)S(1)} %add.196), channel_id=1, source_target_pairs={{0,2},{2,0},{4,6},{6,4},{8,10},{10,8},{12,14},{14,12},{1,3},{3,1},... | collective-permute-start | bytes 393224 | tf_op jit(solution)/shard_map/ppermute | solution.py:152
  169.9 3.3 %collective-permute-done.12 = f32[2,32,512]{2,1,0:T(8,128)S(1)} collective-permute-done((f32[2,32,512]{2,1,0:T(8,128)S(1)}, f32[2,32,512]{2,1,0:T(8,128)S(1)}, u32[]{:S(2)}, u32[]{:S(2)}) %collective-permute-start.12) | collective-permute-done | bytes 131104 | tf_op jit(solution)/shard_map/ppermute | solution.py:152
  174.0 3.7 %collective-permute-start.13 = (f32[4,32,512]{2,1,0:T(8,128)}, f32[4,32,512]{2,1,0:T(8,128)S(1)}, u32[]{:S(2)}, u32[]{:S(2)}) collective-permute-start(f32[4,32,512]{2,1,0:T(8,128)} %pad_maximum_fusion.2), channel_id=1, source_target_pairs={{0,192},{192,384},{384,576},{576,0},{1,193},{193,385},{385,577},{5... | collective-permute-start | bytes 786440 | tf_op jit(solution)/shard_map/ppermute | solution.py:191
  177.7 4.3 %collective-permute-start.14 = (f32[4,32,512]{2,1,0:T(8,128)}, f32[4,32,512]{2,1,0:T(8,128)S(1)}, u32[]{:S(2)}, u32[]{:S(2)}) collective-permute-start(f32[4,32,512]{2,1,0:T(8,128)} %pad_maximum_fusion.2), channel_id=1, source_target_pairs={{0,384},{192,576},{384,0},{576,192},{1,385},{193,577},{385,1},{577... | collective-permute-start | bytes 786440 | tf_op jit(solution)/shard_map/ppermute | solution.py:191
  182.0 2.7 %collective-permute-start.15 = (f32[4,32,512]{2,1,0:T(8,128)}, f32[4,32,512]{2,1,0:T(8,128)S(1)}, u32[]{:S(2)}, u32[]{:S(2)}) collective-permute-start(f32[4,32,512]{2,1,0:T(8,128)} %pad_maximum_fusion.2), channel_id=1, source_target_pairs={{0,576},{192,0},{384,192},{576,384},{1,577},{193,1},{385,193},{577... | collective-permute-start | bytes 786440 | tf_op jit(solution)/shard_map/ppermute | solution.py:191
  186.3 14.7 %collective-permute-done.14 = f32[4,32,512]{2,1,0:T(8,128)S(1)} collective-permute-done((f32[4,32,512]{2,1,0:T(8,128)}, f32[4,32,512]{2,1,0:T(8,128)S(1)}, u32[]{:S(2)}, u32[]{:S(2)}) %collective-permute-start.14) | collective-permute-done | bytes 262176 | tf_op jit(solution)/shard_map/ppermute | solution.py:191
  201.1 2.7 %slice.37 = f32[12,128,256]{2,1,0:T(8,128)} slice(f32[12,136,256]{2,1,0:T(8,128)} %all-to-all-done.3), slice={[0:12], [0:128], [0:256]} | slice | bytes 3145728 | tf_op jit(solution)/shard_map/slice | solution.py:254
  205.3 5.5 %collective-permute-start.16 = (f32[4,128,512]{2,1,0:T(8,128)S(1)}, f32[4,128,512]{2,1,0:T(8,128)}, u32[]{:S(2)}, u32[]{:S(2)}) collective-permute-start(f32[4,128,512]{2,1,0:T(8,128)S(1)} %constant_dynamic-update-slice_fusion.1), channel_id=1, source_target_pairs={{0,1},{1,0},{2,3},{3,2},{4,5},{5,4},{6,7},{7,6},{8,9},{9,8},{10,11... | collective-permute-start | bytes 3145736 | tf_op jit(solution)/shard_map/ppermute | solution.py:152
  211.0 2.1 collective-permute-done.16
  (82 shorter events, 30.0 us)
Async XLA Ops:
  0.6 84.0 %copy-start = (bf16[4096,256]{1,0:T(8,128)(2,1)S(1)}, bf16[4096,256]{1,0:T(8,128)(2,1)}, u32[]{:S(2)}) copy-start(bf16[4096,256]{1,0:T(8,128)(2,1)} %param.16) | copy-start | bytes 6291460
  2.5 46.8 %all-to-all-start = ((bf16[4,128,256]{2,1,0:T(8,128)(2,1)}), bf16[4,128,256]{2,1,0:T(8,128)(2,1)S(1)}, u32[]{:S(2)}, u32[]{:S(2)}) async-start(bf16[4,128,256]{2,1,0:T(8,128)(2,1)} %pad_maximum_fusion.1), calls=%async_computation | async-start | bytes 524288 | tf_op jit(solution)/shard_map/all_to_all | solution.py:226
  49.3 9.0 %copy-start.8 = (bf16[4,128,256]{2,1,0:T(8,128)(2,1)}, bf16[4,128,256]{2,1,0:T(8,128)(2,1)S(1)}, u32[]{:S(2)}) copy-start(bf16[4,128,256]{2,1,0:T(8,128)(2,1)S(1)} %all-to-all-done) | copy-start | bytes 786436
  49.3 1.3 copy-start.3
  56.9 1.4 copy-start.1
  58.3 61.0 %all-to-all-start.1 = ((bf16[16,272,256]{2,1,0:T(8,128)(2,1)}), bf16[16,272,256]{2,1,0:T(8,128)(2,1)}, u32[]{:S(2)}, u32[]{:S(2)}) async-start(bf16[16,272,256]{2,1,0:T(8,128)(2,1)} %copy-done.1), calls=%async_computation.1 | async-start | bytes 4456448 | tf_op jit(solution)/shard_map/all_to_all | solution.py:231
  67.5 14.8 %copy-start.4 = (f32[4096]{0:T(1024)S(1)}, f32[4096]{0:T(1024)}, u32[]{:S(2)}) copy-start(f32[4096]{0:T(1024)} %param.18) | copy-start | bytes 49156
  67.5 16.0 %copy-start.5 = (f32[4096]{0:T(1024)S(1)}, f32[4096]{0:T(1024)}, u32[]{:S(2)}) copy-start(f32[4096]{0:T(1024)} %param.17) | copy-start | bytes 49156
  68.8 22.5 %copy-start.6 = (f32[4096]{0:T(1024)S(1)}, f32[4096]{0:T(1024)}, u32[]{:S(2)}) copy-start(f32[4096]{0:T(1024)} %param.19) | copy-start | bytes 49156
  68.9 3.4 %collective-permute-start = (f32[128,512]{1,0:T(8,128)S(1)}, f32[128,512]{1,0:T(8,128)S(1)}, u32[]{:S(2)}, u32[]{:S(2)}) collective-permute-start(f32[128,512]{1,0:T(8,128)S(1)} %constant_dynamic-slice_fusion.4), channel_id=1, source_target_pairs={{0,1},{1,0},{2,3},{3,2},{4,5},{5,4},{6,7},{7,6},{8,9},{9,8},{10,11... | collective-permute-start | bytes 786440 | tf_op jit(solution)/shard_map/ppermute | solution.py:152
  72.4 13.2 %collective-permute-start.1 = (f32[32,512]{1,0:T(8,128)S(1)}, f32[32,512]{1,0:T(8,128)S(1)}, u32[]{:S(2)}, u32[]{:S(2)}) collective-permute-start(f32[32,512]{1,0:T(8,128)S(1)} %get-tuple-element.42), channel_id=1, source_target_pairs={{0,192},{192,384},{384,576},{576,0},{1,193},{193,385},{385,577},{5... | collective-permute-start | bytes 196616 | tf_op jit(solution)/shard_map/ppermute | solution.py:191
  75.5 10.1 %collective-permute-start.3 = (f32[32,512]{1,0:T(8,128)S(1)}, f32[32,512]{1,0:T(8,128)S(1)}, u32[]{:S(2)}, u32[]{:S(2)}) collective-permute-start(f32[32,512]{1,0:T(8,128)S(1)} %get-tuple-element.43), channel_id=1, source_target_pairs={{0,576},{192,0},{384,192},{576,384},{1,577},{193,1},{385,193},{577... | collective-permute-start | bytes 196616 | tf_op jit(solution)/shard_map/ppermute | solution.py:191
  78.9 6.9 %collective-permute-start.2 = (f32[32,512]{1,0:T(8,128)S(1)}, f32[32,512]{1,0:T(8,128)S(1)}, u32[]{:S(2)}, u32[]{:S(2)}) collective-permute-start(f32[32,512]{1,0:T(8,128)S(1)} %get-tuple-element.44), channel_id=1, source_target_pairs={{0,384},{192,576},{384,0},{576,192},{1,385},{193,577},{385,1},{577... | collective-permute-start | bytes 196616 | tf_op jit(solution)/shard_map/ppermute | solution.py:191
  85.8 6.7 %collective-permute-start.5 = (f32[32,512]{1,0:T(8,128)S(1)}, f32[32,512]{1,0:T(8,128)S(1)}, u32[]{:S(2)}, u32[]{:S(2)}) collective-permute-start(f32[32,512]{1,0:T(8,128)S(1)} %add_add_fusion), channel_id=1, source_target_pairs={{0,128},{64,0},{128,64},{1,129},{65,1},{129,65},{2,130},{66,2},{13... | collective-permute-start | bytes 196616 | tf_op jit(solution)/shard_map/ppermute | solution.py:191
  89.1 6.3 %collective-permute-start.4 = (f32[32,512]{1,0:T(8,128)S(1)}, f32[32,512]{1,0:T(8,128)S(1)}, u32[]{:S(2)}, u32[]{:S(2)}) collective-permute-start(f32[32,512]{1,0:T(8,128)S(1)} %add_add_fusion), channel_id=1, source_target_pairs={{0,64},{64,128},{128,0},{1,65},{65,129},{129,1},{2,66},{66,130},{1... | collective-permute-start | bytes 196616 | tf_op jit(solution)/shard_map/ppermute | solution.py:191
  95.4 15.5 %collective-permute-start.6 = (f32[1,32,512]{2,1,0:T(8,128)S(1)}, f32[1,32,512]{2,1,0:T(8,128)S(1)}, u32[]{:S(2)}, u32[]{:S(2)}) collective-permute-start(f32[1,32,512]{2,1,0:T(8,128)S(1)} %bitcast.31), channel_id=1, source_target_pairs={{0,16},{16,32},{32,48},{48,0},{1,17},{17,33},{33,49},{49,1},{2,18}... | collective-permute-start | bytes 196616 | tf_op jit(solution)/shard_map/ppermute | solution.py:191
  102.0 13.3 %collective-permute-start.8 = (f32[1,32,512]{2,1,0:T(8,128)S(1)}, f32[1,32,512]{2,1,0:T(8,128)S(1)}, u32[]{:S(2)}, u32[]{:S(2)}) collective-permute-start(f32[1,32,512]{2,1,0:T(8,128)S(1)} %bitcast.32), channel_id=1, source_target_pairs={{0,48},{16,0},{32,16},{48,32},{1,49},{17,1},{33,17},{49,33},{2,50}... | collective-permute-start | bytes 196616 | tf_op jit(solution)/shard_map/ppermute | solution.py:191
  104.0 11.3 %collective-permute-start.7 = (f32[1,32,512]{2,1,0:T(8,128)S(1)}, f32[1,32,512]{2,1,0:T(8,128)S(1)}, u32[]{:S(2)}, u32[]{:S(2)}) collective-permute-start(f32[1,32,512]{2,1,0:T(8,128)S(1)} %bitcast.33), channel_id=1, source_target_pairs={{0,32},{16,48},{32,0},{48,16},{1,33},{17,49},{33,1},{49,17},{2,34}... | collective-permute-start | bytes 196616 | tf_op jit(solution)/shard_map/ppermute | solution.py:191
  127.1 31.7 %all-to-all-start.2 = ((f32[12,128,256]{2,1,0:T(8,128)}), f32[12,128,256]{2,1,0:T(8,128)}, u32[]{:S(2)}, u32[]{:S(2)}) async-start(f32[12,128,256]{2,1,0:T(8,128)} %fusion), calls=%async_computation.2 | async-start | bytes 3145728 | tf_op jit(solution)/shard_map/all_to_all | solution.py:245
  132.3 6.3 %collective-permute-start.9 = (f32[2,32,512]{2,1,0:T(8,128)S(1)}, f32[2,32,512]{2,1,0:T(8,128)S(1)}, u32[]{:S(2)}, u32[]{:S(2)}) collective-permute-start(f32[2,32,512]{2,1,0:T(8,128)S(1)} %constant_dynamic-slice_fusion), channel_id=1, source_target_pairs={{0,2},{2,0},{4,6},{6,4},{8,10},{10,8},{12,14},{14,12},{1,3},{3,1},... | collective-permute-start | bytes 393224 | tf_op jit(solution)/shard_map/ppermute | solution.py:152
  138.6 10.2 %collective-permute-start.10 = (f32[2,32,512]{2,1,0:T(8,128)S(1)}, f32[2,32,512]{2,1,0:T(8,128)S(1)}, u32[]{:S(2)}, u32[]{:S(2)}) collective-permute-start(f32[2,32,512]{2,1,0:T(8,128)S(1)} %dynamic-slice_add_fusion.1), channel_id=1, source_target_pairs={{0,4},{2,6},{4,0},{6,2},{8,12},{10,14},{12,8},{14,10},{1,5},{3,7},... | collective-permute-start | bytes 393224 | tf_op jit(solution)/shard_map/ppermute | solution.py:152
  148.8 10.0 %collective-permute-start.11 = (f32[2,32,512]{2,1,0:T(8,128)S(1)}, f32[2,32,512]{2,1,0:T(8,128)S(1)}, u32[]{:S(2)}, u32[]{:S(2)}) collective-permute-start(f32[2,32,512]{2,1,0:T(8,128)S(1)} %add.195), channel_id=1, source_target_pairs={{0,8},{2,10},{4,12},{6,14},{8,0},{10,2},{12,4},{14,6},{1,9},{3,11}... | collective-permute-start | bytes 393224 | tf_op jit(solution)/shard_map/ppermute | solution.py:152
  160.7 1.2 copy-start.2
  161.9 39.2 %all-to-all-start.3 = ((f32[12,136,256]{2,1,0:T(8,128)}), f32[12,136,256]{2,1,0:T(8,128)}, u32[]{:S(2)}, u32[]{:S(2)}) async-start(f32[12,136,256]{2,1,0:T(8,128)} %copy-done.2), calls=%async_computation.3 | async-start | bytes 3342336 | tf_op jit(solution)/shard_map/all_to_all | solution.py:251
  167.5 5.7 %collective-permute-start.12 = (f32[2,32,512]{2,1,0:T(8,128)S(1)}, f32[2,32,512]{2,1,0:T(8,128)S(1)}, u32[]{:S(2)}, u32[]{:S(2)}) collective-permute-start(f32[2,32,512]{2,1,0:T(8,128)S(1)} %add.196), channel_id=1, source_target_pairs={{0,2},{2,0},{4,6},{6,4},{8,10},{10,8},{12,14},{14,12},{1,3},{3,1},... | collective-permute-start | bytes 393224 | tf_op jit(solution)/shard_map/ppermute | solution.py:152
  174.0 12.3 %collective-permute-start.13 = (f32[4,32,512]{2,1,0:T(8,128)}, f32[4,32,512]{2,1,0:T(8,128)S(1)}, u32[]{:S(2)}, u32[]{:S(2)}) collective-permute-start(f32[4,32,512]{2,1,0:T(8,128)} %pad_maximum_fusion.2), channel_id=1, source_target_pairs={{0,192},{192,384},{384,576},{576,0},{1,193},{193,385},{385,577},{5... | collective-permute-start | bytes 786440 | tf_op jit(solution)/shard_map/ppermute | solution.py:191
  177.7 23.4 %collective-permute-start.14 = (f32[4,32,512]{2,1,0:T(8,128)}, f32[4,32,512]{2,1,0:T(8,128)S(1)}, u32[]{:S(2)}, u32[]{:S(2)}) collective-permute-start(f32[4,32,512]{2,1,0:T(8,128)} %pad_maximum_fusion.2), channel_id=1, source_target_pairs={{0,384},{192,576},{384,0},{576,192},{1,385},{193,577},{385,1},{577... | collective-permute-start | bytes 786440 | tf_op jit(solution)/shard_map/ppermute | solution.py:191
  182.0 23.3 %collective-permute-start.15 = (f32[4,32,512]{2,1,0:T(8,128)}, f32[4,32,512]{2,1,0:T(8,128)S(1)}, u32[]{:S(2)}, u32[]{:S(2)}) collective-permute-start(f32[4,32,512]{2,1,0:T(8,128)} %pad_maximum_fusion.2), channel_id=1, source_target_pairs={{0,576},{192,0},{384,192},{576,384},{1,577},{193,1},{385,193},{577... | collective-permute-start | bytes 786440 | tf_op jit(solution)/shard_map/ppermute | solution.py:191
  205.3 7.9 %collective-permute-start.16 = (f32[4,128,512]{2,1,0:T(8,128)S(1)}, f32[4,128,512]{2,1,0:T(8,128)}, u32[]{:S(2)}, u32[]{:S(2)}) collective-permute-start(f32[4,128,512]{2,1,0:T(8,128)S(1)} %constant_dynamic-update-slice_fusion.1), channel_id=1, source_target_pairs={{0,1},{1,0},{2,3},{3,2},{4,5},{5,4},{6,7},{7,6},{8,9},{9,8},{10,11... | collective-permute-start | bytes 3145736 | tf_op jit(solution)/shard_map/ppermute | solution.py:152
  214.5 1.3 copy-start.7

commit v8 on v7

--- a/solution.py
+++ b/solution.py
@@ -250,12 +250,13 @@
 
     payload = lax.all_to_all(update(sums, old, old_accum), REP, 0, 0, tiled=True)
     w = double(w, "y", NY, 1, 0)
-    pieces = [w] + [shift(w, "x", NX, k) for k in range(1, NX)]
+    after = shift(w, "x", NX, NX - 1)
+    pieces = [w, shift(w, "x", NX, 1), shift(after, "x", NX, NX - 1), after]
     new_codes = payload[:, :part].reshape(touch, width)
     new_scale, lowest, new_accum = (payload[:, part + i, :part].reshape(touch) for i in range(3))
-    pieces[-1], new_codes, new_scale, lowest, new_accum = tie(pieces[-1], new_codes, new_scale, lowest, new_accum)
     w = place(pieces, "x", NX, 1)
     other = swap(w, "c", NC, 1)
+    other, new_codes, new_scale, lowest, new_accum = tie(other, new_codes, new_scale, lowest, new_accum)
     side = lax.axis_index("c") * w.shape[1]
     weight_grad = jnp.concatenate([w, w], axis=1)
     weight_grad = lax.dynamic_update_slice_in_dim(weight_grad, other, w.shape[1] - side, 1)

time: 218 us -> 215 us (0.986)
  starting transfers between devices: 95.1 us -> 91.2 us
    unnamed x20 -> x22, local copies, waits for them, and re-layouts: 5.34 us -> 5.34 us
  transfers between devices with their start and end apart: 21 -> 21, of which waited for: 12 -> 11; matrix products, arithmetic and copies ran while one was open for 7% -> 8% of each run, Pallas kernels for 0% -> 0%
where the time goes in v8:
time: 215 us; the launch traced here: 212 us
  starting transfers between devices  91.2 us (42%)
  waiting for transfers between devices  50.2 us (23%)
  blocking collectives  28.7 us (13%)
  local copies, waits for them, and re-layouts  17.3 us (8%)
  Pallas kernels  8.15 us (4%)
  matrix products  8.04 us (4%)
  other arithmetic  6.85 us (3%)
    ppermute x11, starting transfers between devices, shift(): return lax.ppermute(a, axis, [(i, (i + k) % size) for i in range(size)])  39.4 us
    all_gather x1, blocking collectives, shards(): near = lax.all_gather(near, 'zh', axis=0, tiled=False)  28.7 us
    ppermute x11, waiting for transfers between devices, shift(): return lax.ppermute(a, axis, [(i, (i + k) % size) for i in range(size)])  24.9 us
    ppermute x6, waiting for transfers between devices, swap(): return lax.ppermute(a, axis, [(i, i ^ bit) for i in range(size)])  21.4 us
    ppermute x6, starting transfers between devices, swap(): return lax.ppermute(a, axis, [(i, i ^ bit) for i in range(size)])  16.8 us
    all_to_all x1, starting transfers between devices, shards(): columns = lax.all_to_all(columns, 'zh', 0, 0, tiled=True)  15 us
    all_to_all x1, starting transfers between devices, shards(): got = lax.all_to_all(rows, ('y', 'c'), 0, 0, tiled=True)  9.23 us
    dot_general x1, matrix products, collect(): return jnp.dot(selector, got.reshape(-1, width), preferred_element_type=f32)  6.77 us
  transfers between devices with their start and end apart: 21, of which 11 were waited for; matrix products, arithmetic and copies ran while one was open for 8% of the time, Pallas kernels for 0%

profile of v8, /device:TPU:1, one launch (start us, length us, event | category | flops | bytes accessed | tf_op | source)
XLA Modules:
  0.0 211.8 jit_solution(12587155195656016594)
XLA Ops:
  2.5 15.0 %all-to-all-start = ((bf16[4,128,256]{2,1,0:T(8,128)(2,1)}), bf16[4,128,256]{2,1,0:T(8,128)(2,1)S(1)}, u32[]{:S(2)}, u32[]{:S(2)}) async-start(bf16[4,128,256]{2,1,0:T(8,128)(2,1)} %pad_maximum_fusion.1), calls=%async_computation | async-start | bytes 524288 | tf_op jit(solution)/shard_map/all_to_all | solution.py:226
  20.6 28.7 %all-gather = bf16[512,640]{1,0:T(8,128)(2,1)S(1)} all-gather(bf16[128,640]{1,0:T(8,128)(2,1)S(1)} %fusion.7), channel_id=2, replica_groups=mesh['x'=4,'zl'=3,'zh'=4,'y'=8,'c'=2] {'zh'}, dimensions={0}, use_global_device_ids=true | all-gather | bytes 819200 | tf_op jit(solution)/shard_map/all_gather | solution.py:227
  50.6 6.3 %dispatch.1 = bf16[16,272,256]{2,1,0:T(8,128)(2,1)S(1)} custom-call(s32[1]{0:T(128)} %bitcast.refs_0_, bf16[4,128,640]{2,1,0:T(8,128)(2,1)S(1)} %bitcast.27, bf16[1024,512]{1,0:T(8,128)(2,1)S(1)} %copy-done.3), custom_call_target="tpu_custom_call" | custom-call | tf_op jit(solution)/shard_map/dispatch/pallas_call | solution.py:96
  58.3 9.2 %all-to-all-start.1 = ((bf16[16,272,256]{2,1,0:T(8,128)(2,1)}), bf16[16,272,256]{2,1,0:T(8,128)(2,1)}, u32[]{:S(2)}, u32[]{:S(2)}) async-start(bf16[16,272,256]{2,1,0:T(8,128)(2,1)} %copy-done.1), calls=%async_computation.1 | async-start | bytes 4456448 | tf_op jit(solution)/shard_map/all_to_all | solution.py:231
  68.8 2.1 collective-permute-start
  72.4 3.1 %collective-permute-start.1 = (f32[32,512]{1,0:T(8,128)S(1)}, f32[32,512]{1,0:T(8,128)S(1)}, u32[]{:S(2)}, u32[]{:S(2)}) collective-permute-start(f32[32,512]{1,0:T(8,128)S(1)} %get-tuple-element.42), channel_id=1, source_target_pairs={{0,192},{192,384},{384,576},{576,0},{1,193},{193,385},{385,577},{5... | collective-permute-start | bytes 196616 | tf_op jit(solution)/shard_map/ppermute | solution.py:191
  75.5 3.4 %collective-permute-start.3 = (f32[32,512]{1,0:T(8,128)S(1)}, f32[32,512]{1,0:T(8,128)S(1)}, u32[]{:S(2)}, u32[]{:S(2)}) collective-permute-start(f32[32,512]{1,0:T(8,128)S(1)} %get-tuple-element.43), channel_id=1, source_target_pairs={{0,576},{192,0},{384,192},{576,384},{1,577},{193,1},{385,193},{577... | collective-permute-start | bytes 196616 | tf_op jit(solution)/shard_map/ppermute | solution.py:191
  78.9 3.4 %collective-permute-start.2 = (f32[32,512]{1,0:T(8,128)S(1)}, f32[32,512]{1,0:T(8,128)S(1)}, u32[]{:S(2)}, u32[]{:S(2)}) collective-permute-start(f32[32,512]{1,0:T(8,128)S(1)} %get-tuple-element.44), channel_id=1, source_target_pairs={{0,384},{192,576},{384,0},{576,192},{1,385},{193,577},{385,1},{577... | collective-permute-start | bytes 196616 | tf_op jit(solution)/shard_map/ppermute | solution.py:191
  85.8 3.3 %collective-permute-start.5 = (f32[32,512]{1,0:T(8,128)S(1)}, f32[32,512]{1,0:T(8,128)S(1)}, u32[]{:S(2)}, u32[]{:S(2)}) collective-permute-start(f32[32,512]{1,0:T(8,128)S(1)} %add_add_fusion), channel_id=1, source_target_pairs={{0,128},{64,0},{128,64},{1,129},{65,1},{129,65},{2,130},{66,2},{13... | collective-permute-start | bytes 196616 | tf_op jit(solution)/shard_map/ppermute | solution.py:191
  89.1 2.0 collective-permute-start.4
  92.5 2.9 %collective-permute-done.4 = f32[32,512]{1,0:T(8,128)S(1)} collective-permute-done((f32[32,512]{1,0:T(8,128)S(1)}, f32[32,512]{1,0:T(8,128)S(1)}, u32[]{:S(2)}, u32[]{:S(2)}) %collective-permute-start.4) | collective-permute-done | bytes 65568 | tf_op jit(solution)/shard_map/ppermute | solution.py:191
  95.4 6.6 %collective-permute-start.6 = (f32[1,32,512]{2,1,0:T(8,128)S(1)}, f32[1,32,512]{2,1,0:T(8,128)S(1)}, u32[]{:S(2)}, u32[]{:S(2)}) collective-permute-start(f32[1,32,512]{2,1,0:T(8,128)S(1)} %bitcast.31), channel_id=1, source_target_pairs={{0,16},{16,32},{32,48},{48,0},{1,17},{17,33},{33,49},{49,1},{2,18}... | collective-permute-start | bytes 196616 | tf_op jit(solution)/shard_map/ppermute | solution.py:191
  104.0 6.9 %collective-permute-start.7 = (f32[1,32,512]{2,1,0:T(8,128)S(1)}, f32[1,32,512]{2,1,0:T(8,128)S(1)}, u32[]{:S(2)}, u32[]{:S(2)}) collective-permute-start(f32[1,32,512]{2,1,0:T(8,128)S(1)} %bitcast.33), channel_id=1, source_target_pairs={{0,32},{16,48},{32,0},{48,16},{1,33},{17,49},{33,1},{49,17},{2,34}... | collective-permute-start | bytes 196616 | tf_op jit(solution)/shard_map/ppermute | solution.py:191
  110.9 4.4 %collective-permute-done.7 = f32[1,32,512]{2,1,0:T(8,128)S(1)} collective-permute-done((f32[1,32,512]{2,1,0:T(8,128)S(1)}, f32[1,32,512]{2,1,0:T(8,128)S(1)}, u32[]{:S(2)}, u32[]{:S(2)}) %collective-permute-start.7) | collective-permute-done | bytes 65568 | tf_op jit(solution)/shard_map/ppermute | solution.py:191
  115.3 3.9 %all-to-all-done.1 = bf16[16,272,256]{2,1,0:T(8,128)(2,1)} async-done(((bf16[16,272,256]{2,1,0:T(8,128)(2,1)}), bf16[16,272,256]{2,1,0:T(8,128)(2,1)}, u32[]{:S(2)}, u32[]{:S(2)}) %all-to-all-start.1) | async-done | bytes 2228256 | tf_op jit(solution)/shard_map/all_to_all | solution.py:231
  120.3 6.8 %fusion = f32[12,128,256]{2,1,0:T(8,128)} fusion(bf16[4352,256,1]{1,0,2:T(8,128)(2,1)} %bitcast.10, s32[4352]{0:T(1024)S(1)} %eq.65, s32[12,128]{1,0:T(8,128)S(1)} %multiply_add_fusion.1), kind=kOutput, calls=%fused_computation.4 | convolution fusion | flops 3429236736 | bytes 3824640 | tf_op jit(solution)/shard_map/dot_general | solution.py:113
  127.1 5.1 %all-to-all-start.2 = ((f32[12,128,256]{2,1,0:T(8,128)}), f32[12,128,256]{2,1,0:T(8,128)}, u32[]{:S(2)}, u32[]{:S(2)}) async-start(f32[12,128,256]{2,1,0:T(8,128)} %fusion), calls=%async_computation.2 | async-start | bytes 3145728 | tf_op jit(solution)/shard_map/all_to_all | solution.py:245
  132.3 2.0 collective-permute-start.9
  134.3 4.3 %collective-permute-done.9 = f32[2,32,512]{2,1,0:T(8,128)S(1)} collective-permute-done((f32[2,32,512]{2,1,0:T(8,128)S(1)}, f32[2,32,512]{2,1,0:T(8,128)S(1)}, u32[]{:S(2)}, u32[]{:S(2)}) %collective-permute-start.9) | collective-permute-done | bytes 131104 | tf_op jit(solution)/shard_map/ppermute | solution.py:152
  138.6 4.2 %collective-permute-start.10 = (f32[2,32,512]{2,1,0:T(8,128)S(1)}, f32[2,32,512]{2,1,0:T(8,128)S(1)}, u32[]{:S(2)}, u32[]{:S(2)}) collective-permute-start(f32[2,32,512]{2,1,0:T(8,128)S(1)} %dynamic-slice_add_fusion.1), channel_id=1, source_target_pairs={{0,4},{2,6},{4,0},{6,2},{8,12},{10,14},{12,8},{14,10},{1,5},{3,7},... | collective-permute-start | bytes 393224 | tf_op jit(solution)/shard_map/ppermute | solution.py:152
  142.7 6.0 %collective-permute-done.10 = f32[2,32,512]{2,1,0:T(8,128)S(1)} collective-permute-done((f32[2,32,512]{2,1,0:T(8,128)S(1)}, f32[2,32,512]{2,1,0:T(8,128)S(1)}, u32[]{:S(2)}, u32[]{:S(2)}) %collective-permute-start.10) | collective-permute-done | bytes 131104 | tf_op jit(solution)/shard_map/ppermute | solution.py:152
  148.8 2.7 %collective-permute-start.11 = (f32[2,32,512]{2,1,0:T(8,128)S(1)}, f32[2,32,512]{2,1,0:T(8,128)S(1)}, u32[]{:S(2)}, u32[]{:S(2)}) collective-permute-start(f32[2,32,512]{2,1,0:T(8,128)S(1)} %add.195), channel_id=1, source_target_pairs={{0,8},{2,10},{4,12},{6,14},{8,0},{10,2},{12,4},{14,6},{1,9},{3,11}... | collective-permute-start | bytes 393224 | tf_op jit(solution)/shard_map/ppermute | solution.py:152
  151.6 7.2 %collective-permute-done.11 = f32[2,32,512]{2,1,0:T(8,128)S(1)} collective-permute-done((f32[2,32,512]{2,1,0:T(8,128)S(1)}, f32[2,32,512]{2,1,0:T(8,128)S(1)}, u32[]{:S(2)}, u32[]{:S(2)}) %collective-permute-start.11) | collective-permute-done | bytes 131104 | tf_op jit(solution)/shard_map/ppermute | solution.py:152
  161.9 5.6 %all-to-all-start.3 = ((f32[12,136,256]{2,1,0:T(8,128)}), f32[12,136,256]{2,1,0:T(8,128)}, u32[]{:S(2)}, u32[]{:S(2)}) async-start(f32[12,136,256]{2,1,0:T(8,128)} %copy-done.2), calls=%async_computation.3 | async-start | bytes 3342336 | tf_op jit(solution)/shard_map/all_to_all | solution.py:251
  167.5 2.4 %collective-permute-start.12 = (f32[2,32,512]{2,1,0:T(8,128)S(1)}, f32[2,32,512]{2,1,0:T(8,128)S(1)}, u32[]{:S(2)}, u32[]{:S(2)}) collective-permute-start(f32[2,32,512]{2,1,0:T(8,128)S(1)} %add.196), channel_id=1, source_target_pairs={{0,2},{2,0},{4,6},{6,4},{8,10},{10,8},{12,14},{14,12},{1,3},{3,1},... | collective-permute-start | bytes 393224 | tf_op jit(solution)/shard_map/ppermute | solution.py:152
  169.9 3.3 %collective-permute-done.12 = f32[2,32,512]{2,1,0:T(8,128)S(1)} collective-permute-done((f32[2,32,512]{2,1,0:T(8,128)S(1)}, f32[2,32,512]{2,1,0:T(8,128)S(1)}, u32[]{:S(2)}, u32[]{:S(2)}) %collective-permute-start.12) | collective-permute-done | bytes 131104 | tf_op jit(solution)/shard_map/ppermute | solution.py:152
  173.2 4.9 %collective-permute-start.14 = (f32[4,32,512]{2,1,0:T(8,128)S(1)}, f32[4,32,512]{2,1,0:T(8,128)S(1)}, u32[]{:S(2)}, u32[]{:S(2)}) collective-permute-start(f32[4,32,512]{2,1,0:T(8,128)S(1)} %pad_maximum_fusion.2), channel_id=1, source_target_pairs={{0,576},{192,0},{384,192},{576,384},{1,577},{193,1},{385,193},{577... | collective-permute-start | bytes 786440 | tf_op jit(solution)/shard_map/ppermute | solution.py:191
  178.2 1.9 collective-permute-start.13
  180.1 8.8 %collective-permute-done.14 = f32[4,32,512]{2,1,0:T(8,128)S(1)} collective-permute-done((f32[4,32,512]{2,1,0:T(8,128)S(1)}, f32[4,32,512]{2,1,0:T(8,128)S(1)}, u32[]{:S(2)}, u32[]{:S(2)}) %collective-permute-start.14) | collective-permute-done | bytes 262176 | tf_op jit(solution)/shard_map/ppermute | solution.py:191
  191.0 8.5 %collective-permute-done.15 = f32[4,32,512]{2,1,0:T(8,128)S(1)} collective-permute-done((f32[4,32,512]{2,1,0:T(8,128)S(1)}, f32[4,32,512]{2,1,0:T(8,128)S(1)}, u32[]{:S(2)}, u32[]{:S(2)}) %collective-permute-start.15) | collective-permute-done | bytes 262176 | tf_op jit(solution)/shard_map/ppermute | solution.py:191
  199.6 3.5 %collective-permute-start.16 = (f32[4,128,512]{2,1,0:T(8,128)S(1)}, f32[4,128,512]{2,1,0:T(8,128)}, u32[]{:S(2)}, u32[]{:S(2)}) collective-permute-start(f32[4,128,512]{2,1,0:T(8,128)S(1)} %constant_dynamic-update-slice_fusion.1), channel_id=1, source_target_pairs={{0,1},{1,0},{2,3},{3,2},{4,5},{5,4},{6,7},{7,6},{8,9},{9,8},{10,11... | collective-permute-start | bytes 3145736 | tf_op jit(solution)/shard_map/ppermute | solution.py:152
  204.7 2.8 %slice.37 = f32[12,128,256]{2,1,0:T(8,128)} slice(f32[12,136,256]{2,1,0:T(8,128)} %all-to-all-done.3), slice={[0:12], [0:128], [0:256]} | slice | bytes 3145728 | tf_op jit(solution)/shard_map/slice | solution.py:255
  (84 shorter events, 29.1 us)
Async XLA Ops:
  0.6 84.0 %copy-start = (bf16[4096,256]{1,0:T(8,128)(2,1)S(1)}, bf16[4096,256]{1,0:T(8,128)(2,1)}, u32[]{:S(2)}) copy-start(bf16[4096,256]{1,0:T(8,128)(2,1)} %param.16) | copy-start | bytes 6291460
  2.5 46.8 %all-to-all-start = ((bf16[4,128,256]{2,1,0:T(8,128)(2,1)}), bf16[4,128,256]{2,1,0:T(8,128)(2,1)S(1)}, u32[]{:S(2)}, u32[]{:S(2)}) async-start(bf16[4,128,256]{2,1,0:T(8,128)(2,1)} %pad_maximum_fusion.1), calls=%async_computation | async-start | bytes 524288 | tf_op jit(solution)/shard_map/all_to_all | solution.py:226
  49.3 9.0 %copy-start.9 = (bf16[4,128,256]{2,1,0:T(8,128)(2,1)}, bf16[4,128,256]{2,1,0:T(8,128)(2,1)S(1)}, u32[]{:S(2)}) copy-start(bf16[4,128,256]{2,1,0:T(8,128)(2,1)S(1)} %all-to-all-done) | copy-start | bytes 786436
  49.3 1.3 copy-start.3
  56.9 1.4 copy-start.1
  58.3 61.0 %all-to-all-start.1 = ((bf16[16,272,256]{2,1,0:T(8,128)(2,1)}), bf16[16,272,256]{2,1,0:T(8,128)(2,1)}, u32[]{:S(2)}, u32[]{:S(2)}) async-start(bf16[16,272,256]{2,1,0:T(8,128)(2,1)} %copy-done.1), calls=%async_computation.1 | async-start | bytes 4456448 | tf_op jit(solution)/shard_map/all_to_all | solution.py:231
  67.5 14.8 %copy-start.4 = (f32[4096]{0:T(1024)S(1)}, f32[4096]{0:T(1024)}, u32[]{:S(2)}) copy-start(f32[4096]{0:T(1024)} %param.18) | copy-start | bytes 49156
  67.5 16.0 %copy-start.5 = (f32[4096]{0:T(1024)S(1)}, f32[4096]{0:T(1024)}, u32[]{:S(2)}) copy-start(f32[4096]{0:T(1024)} %param.17) | copy-start | bytes 49156
  68.8 22.5 %copy-start.6 = (f32[4096]{0:T(1024)S(1)}, f32[4096]{0:T(1024)}, u32[]{:S(2)}) copy-start(f32[4096]{0:T(1024)} %param.19) | copy-start | bytes 49156
  68.8 3.4 %collective-permute-start = (f32[128,512]{1,0:T(8,128)S(1)}, f32[128,512]{1,0:T(8,128)S(1)}, u32[]{:S(2)}, u32[]{:S(2)}) collective-permute-start(f32[128,512]{1,0:T(8,128)S(1)} %constant_dynamic-slice_fusion.4), channel_id=1, source_target_pairs={{0,1},{1,0},{2,3},{3,2},{4,5},{5,4},{6,7},{7,6},{8,9},{9,8},{10,11... | collective-permute-start | bytes 786440 | tf_op jit(solution)/shard_map/ppermute | solution.py:152
  72.4 13.2 %collective-permute-start.1 = (f32[32,512]{1,0:T(8,128)S(1)}, f32[32,512]{1,0:T(8,128)S(1)}, u32[]{:S(2)}, u32[]{:S(2)}) collective-permute-start(f32[32,512]{1,0:T(8,128)S(1)} %get-tuple-element.42), channel_id=1, source_target_pairs={{0,192},{192,384},{384,576},{576,0},{1,193},{193,385},{385,577},{5... | collective-permute-start | bytes 196616 | tf_op jit(solution)/shard_map/ppermute | solution.py:191
  75.5 10.1 %collective-permute-start.3 = (f32[32,512]{1,0:T(8,128)S(1)}, f32[32,512]{1,0:T(8,128)S(1)}, u32[]{:S(2)}, u32[]{:S(2)}) collective-permute-start(f32[32,512]{1,0:T(8,128)S(1)} %get-tuple-element.43), channel_id=1, source_target_pairs={{0,576},{192,0},{384,192},{576,384},{1,577},{193,1},{385,193},{577... | collective-permute-start | bytes 196616 | tf_op jit(solution)/shard_map/ppermute | solution.py:191
  78.9 6.9 %collective-permute-start.2 = (f32[32,512]{1,0:T(8,128)S(1)}, f32[32,512]{1,0:T(8,128)S(1)}, u32[]{:S(2)}, u32[]{:S(2)}) collective-permute-start(f32[32,512]{1,0:T(8,128)S(1)} %get-tuple-element.44), channel_id=1, source_target_pairs={{0,384},{192,576},{384,0},{576,192},{1,385},{193,577},{385,1},{577... | collective-permute-start | bytes 196616 | tf_op jit(solution)/shard_map/ppermute | solution.py:191
  85.8 6.7 %collective-permute-start.5 = (f32[32,512]{1,0:T(8,128)S(1)}, f32[32,512]{1,0:T(8,128)S(1)}, u32[]{:S(2)}, u32[]{:S(2)}) collective-permute-start(f32[32,512]{1,0:T(8,128)S(1)} %add_add_fusion), channel_id=1, source_target_pairs={{0,128},{64,0},{128,64},{1,129},{65,1},{129,65},{2,130},{66,2},{13... | collective-permute-start | bytes 196616 | tf_op jit(solution)/shard_map/ppermute | solution.py:191
  89.1 6.3 %collective-permute-start.4 = (f32[32,512]{1,0:T(8,128)S(1)}, f32[32,512]{1,0:T(8,128)S(1)}, u32[]{:S(2)}, u32[]{:S(2)}) collective-permute-start(f32[32,512]{1,0:T(8,128)S(1)} %add_add_fusion), channel_id=1, source_target_pairs={{0,64},{64,128},{128,0},{1,65},{65,129},{129,1},{2,66},{66,130},{1... | collective-permute-start | bytes 196616 | tf_op jit(solution)/shard_map/ppermute | solution.py:191
  95.4 15.5 %collective-permute-start.6 = (f32[1,32,512]{2,1,0:T(8,128)S(1)}, f32[1,32,512]{2,1,0:T(8,128)S(1)}, u32[]{:S(2)}, u32[]{:S(2)}) collective-permute-start(f32[1,32,512]{2,1,0:T(8,128)S(1)} %bitcast.31), channel_id=1, source_target_pairs={{0,16},{16,32},{32,48},{48,0},{1,17},{17,33},{33,49},{49,1},{2,18}... | collective-permute-start | bytes 196616 | tf_op jit(solution)/shard_map/ppermute | solution.py:191
  102.0 13.3 %collective-permute-start.8 = (f32[1,32,512]{2,1,0:T(8,128)S(1)}, f32[1,32,512]{2,1,0:T(8,128)S(1)}, u32[]{:S(2)}, u32[]{:S(2)}) collective-permute-start(f32[1,32,512]{2,1,0:T(8,128)S(1)} %bitcast.32), channel_id=1, source_target_pairs={{0,48},{16,0},{32,16},{48,32},{1,49},{17,1},{33,17},{49,33},{2,50}... | collective-permute-start | bytes 196616 | tf_op jit(solution)/shard_map/ppermute | solution.py:191
  104.0 11.3 %collective-permute-start.7 = (f32[1,32,512]{2,1,0:T(8,128)S(1)}, f32[1,32,512]{2,1,0:T(8,128)S(1)}, u32[]{:S(2)}, u32[]{:S(2)}) collective-permute-start(f32[1,32,512]{2,1,0:T(8,128)S(1)} %bitcast.33), channel_id=1, source_target_pairs={{0,32},{16,48},{32,0},{48,16},{1,33},{17,49},{33,1},{49,17},{2,34}... | collective-permute-start | bytes 196616 | tf_op jit(solution)/shard_map/ppermute | solution.py:191
  127.1 31.7 %all-to-all-start.2 = ((f32[12,128,256]{2,1,0:T(8,128)}), f32[12,128,256]{2,1,0:T(8,128)}, u32[]{:S(2)}, u32[]{:S(2)}) async-start(f32[12,128,256]{2,1,0:T(8,128)} %fusion), calls=%async_computation.2 | async-start | bytes 3145728 | tf_op jit(solution)/shard_map/all_to_all | solution.py:245
  132.3 6.3 %collective-permute-start.9 = (f32[2,32,512]{2,1,0:T(8,128)S(1)}, f32[2,32,512]{2,1,0:T(8,128)S(1)}, u32[]{:S(2)}, u32[]{:S(2)}) collective-permute-start(f32[2,32,512]{2,1,0:T(8,128)S(1)} %constant_dynamic-slice_fusion), channel_id=1, source_target_pairs={{0,2},{2,0},{4,6},{6,4},{8,10},{10,8},{12,14},{14,12},{1,3},{3,1},... | collective-permute-start | bytes 393224 | tf_op jit(solution)/shard_map/ppermute | solution.py:152
  138.6 10.2 %collective-permute-start.10 = (f32[2,32,512]{2,1,0:T(8,128)S(1)}, f32[2,32,512]{2,1,0:T(8,128)S(1)}, u32[]{:S(2)}, u32[]{:S(2)}) collective-permute-start(f32[2,32,512]{2,1,0:T(8,128)S(1)} %dynamic-slice_add_fusion.1), channel_id=1, source_target_pairs={{0,4},{2,6},{4,0},{6,2},{8,12},{10,14},{12,8},{14,10},{1,5},{3,7},... | collective-permute-start | bytes 393224 | tf_op jit(solution)/shard_map/ppermute | solution.py:152
  148.8 10.0 %collective-permute-start.11 = (f32[2,32,512]{2,1,0:T(8,128)S(1)}, f32[2,32,512]{2,1,0:T(8,128)S(1)}, u32[]{:S(2)}, u32[]{:S(2)}) collective-permute-start(f32[2,32,512]{2,1,0:T(8,128)S(1)} %add.195), channel_id=1, source_target_pairs={{0,8},{2,10},{4,12},{6,14},{8,0},{10,2},{12,4},{14,6},{1,9},{3,11}... | collective-permute-start | bytes 393224 | tf_op jit(solution)/shard_map/ppermute | solution.py:152
  160.7 1.2 copy-start.2
  161.9 42.9 %all-to-all-start.3 = ((f32[12,136,256]{2,1,0:T(8,128)}), f32[12,136,256]{2,1,0:T(8,128)}, u32[]{:S(2)}, u32[]{:S(2)}) async-start(f32[12,136,256]{2,1,0:T(8,128)} %copy-done.2), calls=%async_computation.3 | async-start | bytes 3342336 | tf_op jit(solution)/shard_map/all_to_all | solution.py:251
  167.5 5.7 %collective-permute-start.12 = (f32[2,32,512]{2,1,0:T(8,128)S(1)}, f32[2,32,512]{2,1,0:T(8,128)S(1)}, u32[]{:S(2)}, u32[]{:S(2)}) collective-permute-start(f32[2,32,512]{2,1,0:T(8,128)S(1)} %add.196), channel_id=1, source_target_pairs={{0,2},{2,0},{4,6},{6,4},{8,10},{10,8},{12,14},{14,12},{1,3},{3,1},... | collective-permute-start | bytes 393224 | tf_op jit(solution)/shard_map/ppermute | solution.py:152
  173.2 15.7 %collective-permute-start.14 = (f32[4,32,512]{2,1,0:T(8,128)S(1)}, f32[4,32,512]{2,1,0:T(8,128)S(1)}, u32[]{:S(2)}, u32[]{:S(2)}) collective-permute-start(f32[4,32,512]{2,1,0:T(8,128)S(1)} %pad_maximum_fusion.2), channel_id=1, source_target_pairs={{0,576},{192,0},{384,192},{576,384},{1,577},{193,1},{385,193},{577... | collective-permute-start | bytes 786440 | tf_op jit(solution)/shard_map/ppermute | solution.py:191
  178.2 12.8 %collective-permute-start.13 = (f32[4,32,512]{2,1,0:T(8,128)S(1)}, f32[4,32,512]{2,1,0:T(8,128)S(1)}, u32[]{:S(2)}, u32[]{:S(2)}) collective-permute-start(f32[4,32,512]{2,1,0:T(8,128)S(1)} %pad_maximum_fusion.2), channel_id=1, source_target_pairs={{0,192},{192,384},{384,576},{576,0},{1,193},{193,385},{385,577},{5... | collective-permute-start | bytes 786440 | tf_op jit(solution)/shard_map/ppermute | solution.py:191
  188.9 10.6 %collective-permute-start.15 = (f32[4,32,512]{2,1,0:T(8,128)S(1)}, f32[4,32,512]{2,1,0:T(8,128)S(1)}, u32[]{:S(2)}, u32[]{:S(2)}) collective-permute-start(f32[4,32,512]{2,1,0:T(8,128)S(1)} %collective-permute-done.14), channel_id=1, source_target_pairs={{0,576},{192,0},{384,192},{576,384},{1,577},{193,1},{385,193},{577... | collective-permute-start | bytes 786440 | tf_op jit(solution)/shard_map/ppermute | solution.py:191
  199.6 9.6 %collective-permute-start.16 = (f32[4,128,512]{2,1,0:T(8,128)S(1)}, f32[4,128,512]{2,1,0:T(8,128)}, u32[]{:S(2)}, u32[]{:S(2)}) collective-permute-start(f32[4,128,512]{2,1,0:T(8,128)S(1)} %constant_dynamic-update-slice_fusion.1), channel_id=1, source_target_pairs={{0,1},{1,0},{2,3},{3,2},{4,5},{5,4},{6,7},{7,6},{8,9},{9,8},{10,11... | collective-permute-start | bytes 3145736 | tf_op jit(solution)/shard_map/ppermute | solution.py:152
  204.7 4.4 %copy-start.7 = (f32[4,256,512]{2,1,0:T(8,128)S(1)}, f32[4,256,512]{2,1,0:T(8,128)}, u32[]{:S(2)}) copy-start(f32[4,256,512]{2,1,0:T(8,128)} %pad_maximum_fusion) | copy-start | bytes 6291460
  210.5 1.3 copy-start.8

commit v9 on v8

--- a/solution.py
+++ b/solution.py
@@ -148,6 +148,27 @@
     )(sums, old, old_accum[:, None])
 
 
+def side_kernel(side_ref, own_ref, other_ref, out_ref):
+    n = own_ref.shape[1]
+    first = side_ref[0] == 0
+    own, other = own_ref[...], other_ref[...]
+    out_ref[:, :n, :] = jnp.where(first, own, other)
+    out_ref[:, n:, :] = jnp.where(first, other, own)
+
+
+def side_by_side(side, own, other):
+    count, n, columns = own.shape
+    half = pl.BlockSpec((1, n, columns), lambda i: (i, 0, 0))
+    return pl.pallas_call(
+        side_kernel,
+        grid=(count,),
+        out_shape=jax.ShapeDtypeStruct((count, 2 * n, columns), f32),
+        in_specs=[pl.BlockSpec(memory_space=pltpu.SMEM), half, half],
+        out_specs=pl.BlockSpec((1, 2 * n, columns), lambda i: (i, 0, 0)),
+        name="side_by_side",
+    )(side, own, other)
+
+
 def swap(a, axis, size, bit):
     return lax.ppermute(a, axis, [(i, i ^ bit) for i in range(size)])
 
@@ -222,10 +243,10 @@
     cap = 2 * bag_slot.shape[0] // (NZH * here)
     first = (lax.axis_index("zh") * here).astype(i32).reshape(1)
     near = with_keys(layer_grad, bag_owner, bag_slot)
+    near = lax.all_gather(near, "zh", axis=0, tiled=False)
     columns = jnp.stack(jnp.split(pooled, NZH, axis=1))
+    near, columns = tie(near, columns)
     columns = lax.all_to_all(columns, "zh", 0, 0, tiled=True)
-    near = lax.all_gather(near, "zh", axis=0, tiled=False)
-    near, columns = tie(near, columns)
     rows = dispatch(first, near, dense_weight, width, here, cap)
     rows, near, columns = tie(rows, near, columns)
     got = lax.all_to_all(rows, ("y", "c"), 0, 0, tiled=True)
@@ -257,9 +278,7 @@
     w = place(pieces, "x", NX, 1)
     other = swap(w, "c", NC, 1)
     other, new_codes, new_scale, lowest, new_accum = tie(other, new_codes, new_scale, lowest, new_accum)
-    side = lax.axis_index("c") * w.shape[1]
-    weight_grad = jnp.concatenate([w, w], axis=1)
-    weight_grad = lax.dynamic_update_slice_in_dim(weight_grad, other, w.shape[1] - side, 1)
+    weight_grad = side_by_side(lax.axis_index("c").astype(i32).reshape(1), w, other)
     weight_grad = weight_grad.reshape(pooled.shape[1], layer_grad.shape[1])
     return (weight_grad, new_codes, new_scale, lowest, new_accum)
 

time: 215 us -> 215 us (level)
  starting transfers between devices: 91.2 us -> 83.3 us
  blocking collectives: 28.7 us -> 33.5 us
  Pallas kernels: 8.15 us -> 11.9 us
  waiting for transfers between devices: 50.2 us -> 52.9 us
  local copies, waits for them, and re-layouts: 17.3 us -> 15 us
    all_to_all x1, starting transfers between devices: 15 us -> 3.41 us  [shards(): columns = lax.all_to_all(columns, 'zh', 0, 0, tiled=True)]
    all_gather x1, blocking collectives: 28.7 us -> 33.5 us  [shards(): near = lax.all_gather(near, 'zh', axis=0, tiled=False)]
    pallas_call x0 -> x1, Pallas kernels: none -> 3.77 us  [side_by_side(): pl.pallas_call(side_kernel, grid=(count,), out_shape=jax.ShapeDtypeStruct...]
    all_to_all x1, starting transfers between devices: 9.23 us -> 12.5 us  [shards(): got = lax.all_to_all(rows, ('y', 'c'), 0, 0, tiled=True)]
    all_to_all x1, waiting for transfers between devices: 0.01 us -> 3.23 us  [shards(): columns = lax.all_to_all(columns, 'zh', 0, 0, tiled=True)]
    unnamed x22 -> x20, local copies, waits for them, and re-layouts: 5.34 us -> 4.64 us
  transfers between devices with their start and end apart: 21 -> 21, of which waited for: 11 -> 12; matrix products, arithmetic and copies ran while one was open for 8% -> 5% of each run, Pallas kernels for 0% -> 3%
where the time goes in v9:
time: 215 us; the launch traced here: 211 us
  starting transfers between devices  83.3 us (39%)
  waiting for transfers between devices  52.9 us (25%)
  blocking collectives  33.5 us (16%)
  local copies, waits for them, and re-layouts  15 us (7%)
  Pallas kernels  11.9 us (6%)
  matrix products  8.04 us (4%)
  other arithmetic  5.37 us (2%)
    ppermute x11, starting transfers between devices, shift(): return lax.ppermute(a, axis, [(i, (i + k) % size) for i in range(size)])  39.9 us
    all_gather x1, blocking collectives, shards(): near = lax.all_gather(near, 'zh', axis=0, tiled=False)  33.5 us
    ppermute x11, waiting for transfers between devices, shift(): return lax.ppermute(a, axis, [(i, (i + k) % size) for i in range(size)])  24.1 us
    ppermute x6, waiting for transfers between devices, swap(): return lax.ppermute(a, axis, [(i, i ^ bit) for i in range(size)])  21.4 us
    ppermute x6, starting transfers between devices, swap(): return lax.ppermute(a, axis, [(i, i ^ bit) for i in range(size)])  16.8 us
    all_to_all x1, starting transfers between devices, shards(): got = lax.all_to_all(rows, ('y', 'c'), 0, 0, tiled=True)  12.5 us
    dot_general x1, matrix products, collect(): return jnp.dot(selector, got.reshape(-1, width), preferred_element_type=f32)  6.78 us
    pallas_call x1, Pallas kernels, dispatch(): pl.pallas_call(lambda *refs: dispatch_kernel(here, cap, *refs), out_shape...  6.31 us
  transfers between devices with their start and end apart: 21, of which 12 were waited for; matrix products, arithmetic and copies ran while one was open for 5% of the time, Pallas kernels for 3%

profile of v9, /device:TPU:1, one launch (start us, length us, event | category | flops | bytes accessed | tf_op | source)
XLA Modules:
  0.0 211.4 jit_solution(16551199016760120103)
XLA Ops:
  4.8 33.5 %all-gather = bf16[512,640]{1,0:T(8,128)(2,1)S(1)} all-gather(bf16[128,640]{1,0:T(8,128)(2,1)S(1)} %fusion.7), channel_id=2, replica_groups=mesh['x'=4,'zl'=3,'zh'=4,'y'=8,'c'=2] {'zh'}, dimensions={0}, use_global_device_ids=true | all-gather | bytes 819200 | tf_op jit(solution)/shard_map/all_gather | solution.py:246
  39.0 3.4 %all-to-all-start = ((bf16[4,128,256]{2,1,0:T(8,128)(2,1)}), bf16[4,128,256]{2,1,0:T(8,128)(2,1)S(1)}, u32[]{:S(2)}, u32[]{:S(2)}) async-start(bf16[4,128,256]{2,1,0:T(8,128)(2,1)} %pad_maximum_fusion), calls=%async_computation | async-start | bytes 524288 | tf_op jit(solution)/shard_map/all_to_all | solution.py:249
  43.7 6.3 %dispatch.1 = bf16[16,272,256]{2,1,0:T(8,128)(2,1)S(1)} custom-call(s32[1]{0:T(128)} %bitcast.1.refs_0_, bf16[4,128,640]{2,1,0:T(8,128)(2,1)S(1)} %bitcast.28, bf16[1024,512]{1,0:T(8,128)(2,1)S(1)} %copy-done.3), custom_call_target="tpu_custom_call" | custom-call | tf_op jit(solution)/shard_map/dispatch/pallas_call | solution.py:96
  51.4 3.2 %all-to-all-done = bf16[4,128,256]{2,1,0:T(8,128)(2,1)S(1)} async-done(((bf16[4,128,256]{2,1,0:T(8,128)(2,1)}), bf16[4,128,256]{2,1,0:T(8,128)(2,1)S(1)}, u32[]{:S(2)}, u32[]{:S(2)}) %all-to-all-start) | async-done | bytes 262176 | tf_op jit(solution)/shard_map/all_to_all | solution.py:249
  55.3 12.5 %all-to-all-start.1 = ((bf16[16,272,256]{2,1,0:T(8,128)(2,1)}), bf16[16,272,256]{2,1,0:T(8,128)(2,1)}, u32[]{:S(2)}, u32[]{:S(2)}) async-start(bf16[16,272,256]{2,1,0:T(8,128)(2,1)} %copy-done.1), calls=%async_computation.1 | async-start | bytes 4456448 | tf_op jit(solution)/shard_map/all_to_all | solution.py:252
  72.7 3.1 %collective-permute-start.1 = (f32[32,512]{1,0:T(8,128)S(1)}, f32[32,512]{1,0:T(8,128)S(1)}, u32[]{:S(2)}, u32[]{:S(2)}) collective-permute-start(f32[32,512]{1,0:T(8,128)S(1)} %get-tuple-element.42), channel_id=1, source_target_pairs={{0,192},{192,384},{384,576},{576,0},{1,193},{193,385},{385,577},{5... | collective-permute-start | bytes 196616 | tf_op jit(solution)/shard_map/ppermute | solution.py:212
  75.8 3.4 %collective-permute-start.3 = (f32[32,512]{1,0:T(8,128)S(1)}, f32[32,512]{1,0:T(8,128)S(1)}, u32[]{:S(2)}, u32[]{:S(2)}) collective-permute-start(f32[32,512]{1,0:T(8,128)S(1)} %get-tuple-element.43), channel_id=1, source_target_pairs={{0,576},{192,0},{384,192},{576,384},{1,577},{193,1},{385,193},{577... | collective-permute-start | bytes 196616 | tf_op jit(solution)/shard_map/ppermute | solution.py:212
  79.2 3.4 %collective-permute-start.2 = (f32[32,512]{1,0:T(8,128)S(1)}, f32[32,512]{1,0:T(8,128)S(1)}, u32[]{:S(2)}, u32[]{:S(2)}) collective-permute-start(f32[32,512]{1,0:T(8,128)S(1)} %get-tuple-element.44), channel_id=1, source_target_pairs={{0,384},{192,576},{384,0},{576,192},{1,385},{193,577},{385,1},{577... | collective-permute-start | bytes 196616 | tf_op jit(solution)/shard_map/ppermute | solution.py:212
  86.1 3.2 %collective-permute-start.5 = (f32[32,512]{1,0:T(8,128)S(1)}, f32[32,512]{1,0:T(8,128)S(1)}, u32[]{:S(2)}, u32[]{:S(2)}) collective-permute-start(f32[32,512]{1,0:T(8,128)S(1)} %add_add_fusion), channel_id=1, source_target_pairs={{0,128},{64,0},{128,64},{1,129},{65,1},{129,65},{2,130},{66,2},{13... | collective-permute-start | bytes 196616 | tf_op jit(solution)/shard_map/ppermute | solution.py:212
  89.3 2.1 collective-permute-start.4
  92.8 2.8 %collective-permute-done.4 = f32[32,512]{1,0:T(8,128)S(1)} collective-permute-done((f32[32,512]{1,0:T(8,128)S(1)}, f32[32,512]{1,0:T(8,128)S(1)}, u32[]{:S(2)}, u32[]{:S(2)}) %collective-permute-start.4) | collective-permute-done | bytes 65568 | tf_op jit(solution)/shard_map/ppermute | solution.py:212
  95.7 4.5 %collective-permute-start.6 = (f32[1,32,512]{2,1,0:T(8,128)S(1)}, f32[1,32,512]{2,1,0:T(8,128)S(1)}, u32[]{:S(2)}, u32[]{:S(2)}) collective-permute-start(f32[1,32,512]{2,1,0:T(8,128)S(1)} %bitcast.32), channel_id=1, source_target_pairs={{0,16},{16,32},{32,48},{48,0},{1,17},{17,33},{33,49},{49,1},{2,18}... | collective-permute-start | bytes 196616 | tf_op jit(solution)/shard_map/ppermute | solution.py:212
  100.2 3.8 %collective-permute-start.8 = (f32[1,32,512]{2,1,0:T(8,128)S(1)}, f32[1,32,512]{2,1,0:T(8,128)S(1)}, u32[]{:S(2)}, u32[]{:S(2)}) collective-permute-start(f32[1,32,512]{2,1,0:T(8,128)S(1)} %bitcast.33), channel_id=1, source_target_pairs={{0,48},{16,0},{32,16},{48,32},{1,49},{17,1},{33,17},{49,33},{2,50}... | collective-permute-start | bytes 196616 | tf_op jit(solution)/shard_map/ppermute | solution.py:212
  104.0 7.7 %collective-permute-start.7 = (f32[1,32,512]{2,1,0:T(8,128)S(1)}, f32[1,32,512]{2,1,0:T(8,128)S(1)}, u32[]{:S(2)}, u32[]{:S(2)}) collective-permute-start(f32[1,32,512]{2,1,0:T(8,128)S(1)} %bitcast.34), channel_id=1, source_target_pairs={{0,32},{16,48},{32,0},{48,16},{1,33},{17,49},{33,1},{49,17},{2,34}... | collective-permute-start | bytes 196616 | tf_op jit(solution)/shard_map/ppermute | solution.py:212
  111.7 3.6 %collective-permute-done.7 = f32[1,32,512]{2,1,0:T(8,128)S(1)} collective-permute-done((f32[1,32,512]{2,1,0:T(8,128)S(1)}, f32[1,32,512]{2,1,0:T(8,128)S(1)}, u32[]{:S(2)}, u32[]{:S(2)}) %collective-permute-start.7) | collective-permute-done | bytes 65568 | tf_op jit(solution)/shard_map/ppermute | solution.py:212
  115.4 4.2 %all-to-all-done.1 = bf16[16,272,256]{2,1,0:T(8,128)(2,1)} async-done(((bf16[16,272,256]{2,1,0:T(8,128)(2,1)}), bf16[16,272,256]{2,1,0:T(8,128)(2,1)}, u32[]{:S(2)}, u32[]{:S(2)}) %all-to-all-start.1) | async-done | bytes 2228256 | tf_op jit(solution)/shard_map/all_to_all | solution.py:252
  120.7 6.8 %fusion = f32[12,128,256]{2,1,0:T(8,128)} fusion(bf16[4352,256,1]{1,0,2:T(8,128)(2,1)} %bitcast.11, s32[4352]{0:T(1024)S(1)} %eq.65, s32[12,128]{1,0:T(8,128)S(1)} %multiply_add_fusion.1), kind=kOutput, calls=%fused_computation.4 | convolution fusion | flops 3429236736 | bytes 3824640 | tf_op jit(solution)/shard_map/dot_general | solution.py:113
  127.4 5.1 %all-to-all-start.2 = ((f32[12,128,256]{2,1,0:T(8,128)}), f32[12,128,256]{2,1,0:T(8,128)}, u32[]{:S(2)}, u32[]{:S(2)}) async-start(f32[12,128,256]{2,1,0:T(8,128)} %fusion), calls=%async_computation.2 | async-start | bytes 3145728 | tf_op jit(solution)/shard_map/all_to_all | solution.py:266
  134.5 4.3 %collective-permute-done.9 = f32[2,32,512]{2,1,0:T(8,128)S(1)} collective-permute-done((f32[2,32,512]{2,1,0:T(8,128)S(1)}, f32[2,32,512]{2,1,0:T(8,128)S(1)}, u32[]{:S(2)}, u32[]{:S(2)}) %collective-permute-start.9) | collective-permute-done | bytes 131104 | tf_op jit(solution)/shard_map/ppermute | solution.py:173
  138.8 4.2 %collective-permute-start.10 = (f32[2,32,512]{2,1,0:T(8,128)S(1)}, f32[2,32,512]{2,1,0:T(8,128)S(1)}, u32[]{:S(2)}, u32[]{:S(2)}) collective-permute-start(f32[2,32,512]{2,1,0:T(8,128)S(1)} %dynamic-slice_add_fusion.1), channel_id=1, source_target_pairs={{0,4},{2,6},{4,0},{6,2},{8,12},{10,14},{12,8},{14,10},{1,5},{3,7},... | collective-permute-start | bytes 393224 | tf_op jit(solution)/shard_map/ppermute | solution.py:173
  143.0 6.0 %collective-permute-done.10 = f32[2,32,512]{2,1,0:T(8,128)S(1)} collective-permute-done((f32[2,32,512]{2,1,0:T(8,128)S(1)}, f32[2,32,512]{2,1,0:T(8,128)S(1)}, u32[]{:S(2)}, u32[]{:S(2)}) %collective-permute-start.10) | collective-permute-done | bytes 131104 | tf_op jit(solution)/shard_map/ppermute | solution.py:173
  149.1 2.7 %collective-permute-start.11 = (f32[2,32,512]{2,1,0:T(8,128)S(1)}, f32[2,32,512]{2,1,0:T(8,128)S(1)}, u32[]{:S(2)}, u32[]{:S(2)}) collective-permute-start(f32[2,32,512]{2,1,0:T(8,128)S(1)} %add.191), channel_id=1, source_target_pairs={{0,8},{2,10},{4,12},{6,14},{8,0},{10,2},{12,4},{14,6},{1,9},{3,11}... | collective-permute-start | bytes 393224 | tf_op jit(solution)/shard_map/ppermute | solution.py:173
  151.9 7.2 %collective-permute-done.11 = f32[2,32,512]{2,1,0:T(8,128)S(1)} collective-permute-done((f32[2,32,512]{2,1,0:T(8,128)S(1)}, f32[2,32,512]{2,1,0:T(8,128)S(1)}, u32[]{:S(2)}, u32[]{:S(2)}) %collective-permute-start.11) | collective-permute-done | bytes 131104 | tf_op jit(solution)/shard_map/ppermute | solution.py:173
  162.2 5.6 %all-to-all-start.3 = ((f32[12,136,256]{2,1,0:T(8,128)}), f32[12,136,256]{2,1,0:T(8,128)}, u32[]{:S(2)}, u32[]{:S(2)}) async-start(f32[12,136,256]{2,1,0:T(8,128)} %copy-done.2), calls=%async_computation.3 | async-start | bytes 3342336 | tf_op jit(solution)/shard_map/all_to_all | solution.py:272
  167.7 2.4 %collective-permute-start.12 = (f32[2,32,512]{2,1,0:T(8,128)S(1)}, f32[2,32,512]{2,1,0:T(8,128)S(1)}, u32[]{:S(2)}, u32[]{:S(2)}) collective-permute-start(f32[2,32,512]{2,1,0:T(8,128)S(1)} %add.192), channel_id=1, source_target_pairs={{0,2},{2,0},{4,6},{6,4},{8,10},{10,8},{12,14},{14,12},{1,3},{3,1},... | collective-permute-start | bytes 393224 | tf_op jit(solution)/shard_map/ppermute | solution.py:173
  170.2 3.3 %collective-permute-done.12 = f32[2,32,512]{2,1,0:T(8,128)S(1)} collective-permute-done((f32[2,32,512]{2,1,0:T(8,128)S(1)}, f32[2,32,512]{2,1,0:T(8,128)S(1)}, u32[]{:S(2)}, u32[]{:S(2)}) %collective-permute-start.12) | collective-permute-done | bytes 131104 | tf_op jit(solution)/shard_map/ppermute | solution.py:173
  173.5 4.9 %collective-permute-start.14 = (f32[4,32,512]{2,1,0:T(8,128)S(1)}, f32[4,32,512]{2,1,0:T(8,128)S(1)}, u32[]{:S(2)}, u32[]{:S(2)}) collective-permute-start(f32[4,32,512]{2,1,0:T(8,128)S(1)} %pad_maximum_fusion.1), channel_id=1, source_target_pairs={{0,576},{192,0},{384,192},{576,384},{1,577},{193,1},{385,193},{577... | collective-permute-start | bytes 786440 | tf_op jit(solution)/shard_map/ppermute | solution.py:212
  180.3 8.8 %collective-permute-done.14 = f32[4,32,512]{2,1,0:T(8,128)S(1)} collective-permute-done((f32[4,32,512]{2,1,0:T(8,128)S(1)}, f32[4,32,512]{2,1,0:T(8,128)S(1)}, u32[]{:S(2)}, u32[]{:S(2)}) %collective-permute-start.14) | collective-permute-done | bytes 262176 | tf_op jit(solution)/shard_map/ppermute | solution.py:212
  191.3 8.5 %collective-permute-done.15 = f32[4,32,512]{2,1,0:T(8,128)S(1)} collective-permute-done((f32[4,32,512]{2,1,0:T(8,128)S(1)}, f32[4,32,512]{2,1,0:T(8,128)S(1)}, u32[]{:S(2)}, u32[]{:S(2)}) %collective-permute-start.15) | collective-permute-done | bytes 262176 | tf_op jit(solution)/shard_map/ppermute | solution.py:212
  199.9 3.5 %collective-permute-start.16 = (f32[4,128,512]{2,1,0:T(8,128)S(1)}, f32[4,128,512]{2,1,0:T(8,128)}, u32[]{:S(2)}, u32[]{:S(2)}) collective-permute-start(f32[4,128,512]{2,1,0:T(8,128)S(1)} %constant_dynamic-update-slice_fusion.own_ref), channel_id=1, source_target_pairs={{0,1},{1,0},{2,3},{3,2},{4,5},{5,4},{6,7},{7,6},{8,9},{9,8},{10,11... | collective-permute-start | bytes 3145736 | tf_op jit(solution)/shard_map/ppermute | solution.py:173
  203.4 2.7 %slice.37 = f32[12,128,256]{2,1,0:T(8,128)} slice(f32[12,136,256]{2,1,0:T(8,128)} %all-to-all-done.3), slice={[0:12], [0:128], [0:256]} | slice | bytes 3145728 | tf_op jit(solution)/shard_map/slice | solution.py:276
  207.6 3.8 %side_by_side.1 = f32[4,256,512]{2,1,0:T(8,128)} custom-call(s32[1]{0:T(128)} %bitcast.side_ref, f32[4,128,512]{2,1,0:T(8,128)} %copy-done.7, f32[4,128,512]{2,1,0:T(8,128)} %collective-permute-done.16.other_ref), custom_call_target="tpu_custom_call" | custom-call | tf_op jit(solution)/shard_map/side_by_side/pallas_call | solution.py:162
  (81 shorter events, 29.5 us)
Async XLA Ops:
  0.6 84.4 %copy-start = (bf16[4096,256]{1,0:T(8,128)(2,1)S(1)}, bf16[4096,256]{1,0:T(8,128)(2,1)}, u32[]{:S(2)}) copy-start(bf16[4096,256]{1,0:T(8,128)(2,1)} %param.16) | copy-start | bytes 6291460
  39.0 15.6 %all-to-all-start = ((bf16[4,128,256]{2,1,0:T(8,128)(2,1)}), bf16[4,128,256]{2,1,0:T(8,128)(2,1)S(1)}, u32[]{:S(2)}, u32[]{:S(2)}) async-start(bf16[4,128,256]{2,1,0:T(8,128)(2,1)} %pad_maximum_fusion), calls=%async_computation | async-start | bytes 524288 | tf_op jit(solution)/shard_map/all_to_all | solution.py:249
  42.4 1.2 copy-start.3
  50.0 1.4 copy-start.1
  54.6 0.7 copy-start.8
  55.3 64.3 %all-to-all-start.1 = ((bf16[16,272,256]{2,1,0:T(8,128)(2,1)}), bf16[16,272,256]{2,1,0:T(8,128)(2,1)}, u32[]{:S(2)}, u32[]{:S(2)}) async-start(bf16[16,272,256]{2,1,0:T(8,128)(2,1)} %copy-done.1), calls=%async_computation.1 | async-start | bytes 4456448 | tf_op jit(solution)/shard_map/all_to_all | solution.py:252
  67.8 14.8 %copy-start.4 = (f32[4096]{0:T(1024)S(1)}, f32[4096]{0:T(1024)}, u32[]{:S(2)}) copy-start(f32[4096]{0:T(1024)} %param.18) | copy-start | bytes 49156
  67.8 16.0 %copy-start.5 = (f32[4096]{0:T(1024)S(1)}, f32[4096]{0:T(1024)}, u32[]{:S(2)}) copy-start(f32[4096]{0:T(1024)} %param.17) | copy-start | bytes 49156
  69.1 22.5 %copy-start.6 = (f32[4096]{0:T(1024)S(1)}, f32[4096]{0:T(1024)}, u32[]{:S(2)}) copy-start(f32[4096]{0:T(1024)} %param.19) | copy-start | bytes 49156
  69.2 3.4 %collective-permute-start = (f32[128,512]{1,0:T(8,128)S(1)}, f32[128,512]{1,0:T(8,128)S(1)}, u32[]{:S(2)}, u32[]{:S(2)}) collective-permute-start(f32[128,512]{1,0:T(8,128)S(1)} %constant_dynamic-slice_fusion.4), channel_id=1, source_target_pairs={{0,1},{1,0},{2,3},{3,2},{4,5},{5,4},{6,7},{7,6},{8,9},{9,8},{10,11... | collective-permute-start | bytes 786440 | tf_op jit(solution)/shard_map/ppermute | solution.py:173
  72.7 13.2 %collective-permute-start.1 = (f32[32,512]{1,0:T(8,128)S(1)}, f32[32,512]{1,0:T(8,128)S(1)}, u32[]{:S(2)}, u32[]{:S(2)}) collective-permute-start(f32[32,512]{1,0:T(8,128)S(1)} %get-tuple-element.42), channel_id=1, source_target_pairs={{0,192},{192,384},{384,576},{576,0},{1,193},{193,385},{385,577},{5... | collective-permute-start | bytes 196616 | tf_op jit(solution)/shard_map/ppermute | solution.py:212
  75.8 10.1 %collective-permute-start.3 = (f32[32,512]{1,0:T(8,128)S(1)}, f32[32,512]{1,0:T(8,128)S(1)}, u32[]{:S(2)}, u32[]{:S(2)}) collective-permute-start(f32[32,512]{1,0:T(8,128)S(1)} %get-tuple-element.43), channel_id=1, source_target_pairs={{0,576},{192,0},{384,192},{576,384},{1,577},{193,1},{385,193},{577... | collective-permute-start | bytes 196616 | tf_op jit(solution)/shard_map/ppermute | solution.py:212
  79.2 6.9 %collective-permute-start.2 = (f32[32,512]{1,0:T(8,128)S(1)}, f32[32,512]{1,0:T(8,128)S(1)}, u32[]{:S(2)}, u32[]{:S(2)}) collective-permute-start(f32[32,512]{1,0:T(8,128)S(1)} %get-tuple-element.44), channel_id=1, source_target_pairs={{0,384},{192,576},{384,0},{576,192},{1,385},{193,577},{385,1},{577... | collective-permute-start | bytes 196616 | tf_op jit(solution)/shard_map/ppermute | solution.py:212
  86.1 6.7 %collective-permute-start.5 = (f32[32,512]{1,0:T(8,128)S(1)}, f32[32,512]{1,0:T(8,128)S(1)}, u32[]{:S(2)}, u32[]{:S(2)}) collective-permute-start(f32[32,512]{1,0:T(8,128)S(1)} %add_add_fusion), channel_id=1, source_target_pairs={{0,128},{64,0},{128,64},{1,129},{65,1},{129,65},{2,130},{66,2},{13... | collective-permute-start | bytes 196616 | tf_op jit(solution)/shard_map/ppermute | solution.py:212
  89.3 6.3 %collective-permute-start.4 = (f32[32,512]{1,0:T(8,128)S(1)}, f32[32,512]{1,0:T(8,128)S(1)}, u32[]{:S(2)}, u32[]{:S(2)}) collective-permute-start(f32[32,512]{1,0:T(8,128)S(1)} %add_add_fusion), channel_id=1, source_target_pairs={{0,64},{64,128},{128,0},{1,65},{65,129},{129,1},{2,66},{66,130},{1... | collective-permute-start | bytes 196616 | tf_op jit(solution)/shard_map/ppermute | solution.py:212
  95.7 16.0 %collective-permute-start.6 = (f32[1,32,512]{2,1,0:T(8,128)S(1)}, f32[1,32,512]{2,1,0:T(8,128)S(1)}, u32[]{:S(2)}, u32[]{:S(2)}) collective-permute-start(f32[1,32,512]{2,1,0:T(8,128)S(1)} %bitcast.32), channel_id=1, source_target_pairs={{0,16},{16,32},{32,48},{48,0},{1,17},{17,33},{33,49},{49,1},{2,18}... | collective-permute-start | bytes 196616 | tf_op jit(solution)/shard_map/ppermute | solution.py:212
  100.2 15.1 %collective-permute-start.8 = (f32[1,32,512]{2,1,0:T(8,128)S(1)}, f32[1,32,512]{2,1,0:T(8,128)S(1)}, u32[]{:S(2)}, u32[]{:S(2)}) collective-permute-start(f32[1,32,512]{2,1,0:T(8,128)S(1)} %bitcast.33), channel_id=1, source_target_pairs={{0,48},{16,0},{32,16},{48,32},{1,49},{17,1},{33,17},{49,33},{2,50}... | collective-permute-start | bytes 196616 | tf_op jit(solution)/shard_map/ppermute | solution.py:212
  104.0 11.4 %collective-permute-start.7 = (f32[1,32,512]{2,1,0:T(8,128)S(1)}, f32[1,32,512]{2,1,0:T(8,128)S(1)}, u32[]{:S(2)}, u32[]{:S(2)}) collective-permute-start(f32[1,32,512]{2,1,0:T(8,128)S(1)} %bitcast.34), channel_id=1, source_target_pairs={{0,32},{16,48},{32,0},{48,16},{1,33},{17,49},{33,1},{49,17},{2,34}... | collective-permute-start | bytes 196616 | tf_op jit(solution)/shard_map/ppermute | solution.py:212
  127.4 31.7 %all-to-all-start.2 = ((f32[12,128,256]{2,1,0:T(8,128)}), f32[12,128,256]{2,1,0:T(8,128)}, u32[]{:S(2)}, u32[]{:S(2)}) async-start(f32[12,128,256]{2,1,0:T(8,128)} %fusion), calls=%async_computation.2 | async-start | bytes 3145728 | tf_op jit(solution)/shard_map/all_to_all | solution.py:266
  132.5 6.3 %collective-permute-start.9 = (f32[2,32,512]{2,1,0:T(8,128)S(1)}, f32[2,32,512]{2,1,0:T(8,128)S(1)}, u32[]{:S(2)}, u32[]{:S(2)}) collective-permute-start(f32[2,32,512]{2,1,0:T(8,128)S(1)} %constant_dynamic-slice_fusion), channel_id=1, source_target_pairs={{0,2},{2,0},{4,6},{6,4},{8,10},{10,8},{12,14},{14,12},{1,3},{3,1},... | collective-permute-start | bytes 393224 | tf_op jit(solution)/shard_map/ppermute | solution.py:173
  138.8 10.2 %collective-permute-start.10 = (f32[2,32,512]{2,1,0:T(8,128)S(1)}, f32[2,32,512]{2,1,0:T(8,128)S(1)}, u32[]{:S(2)}, u32[]{:S(2)}) collective-permute-start(f32[2,32,512]{2,1,0:T(8,128)S(1)} %dynamic-slice_add_fusion.1), channel_id=1, source_target_pairs={{0,4},{2,6},{4,0},{6,2},{8,12},{10,14},{12,8},{14,10},{1,5},{3,7},... | collective-permute-start | bytes 393224 | tf_op jit(solution)/shard_map/ppermute | solution.py:173
  149.1 10.0 %collective-permute-start.11 = (f32[2,32,512]{2,1,0:T(8,128)S(1)}, f32[2,32,512]{2,1,0:T(8,128)S(1)}, u32[]{:S(2)}, u32[]{:S(2)}) collective-permute-start(f32[2,32,512]{2,1,0:T(8,128)S(1)} %add.191), channel_id=1, source_target_pairs={{0,8},{2,10},{4,12},{6,14},{8,0},{10,2},{12,4},{14,6},{1,9},{3,11}... | collective-permute-start | bytes 393224 | tf_op jit(solution)/shard_map/ppermute | solution.py:173
  161.0 1.2 copy-start.2
  162.2 41.3 %all-to-all-start.3 = ((f32[12,136,256]{2,1,0:T(8,128)}), f32[12,136,256]{2,1,0:T(8,128)}, u32[]{:S(2)}, u32[]{:S(2)}) async-start(f32[12,136,256]{2,1,0:T(8,128)} %copy-done.2), calls=%async_computation.3 | async-start | bytes 3342336 | tf_op jit(solution)/shard_map/all_to_all | solution.py:272
  167.7 5.7 %collective-permute-start.12 = (f32[2,32,512]{2,1,0:T(8,128)S(1)}, f32[2,32,512]{2,1,0:T(8,128)S(1)}, u32[]{:S(2)}, u32[]{:S(2)}) collective-permute-start(f32[2,32,512]{2,1,0:T(8,128)S(1)} %add.192), channel_id=1, source_target_pairs={{0,2},{2,0},{4,6},{6,4},{8,10},{10,8},{12,14},{14,12},{1,3},{3,1},... | collective-permute-start | bytes 393224 | tf_op jit(solution)/shard_map/ppermute | solution.py:173
  173.5 15.7 %collective-permute-start.14 = (f32[4,32,512]{2,1,0:T(8,128)S(1)}, f32[4,32,512]{2,1,0:T(8,128)S(1)}, u32[]{:S(2)}, u32[]{:S(2)}) collective-permute-start(f32[4,32,512]{2,1,0:T(8,128)S(1)} %pad_maximum_fusion.1), channel_id=1, source_target_pairs={{0,576},{192,0},{384,192},{576,384},{1,577},{193,1},{385,193},{577... | collective-permute-start | bytes 786440 | tf_op jit(solution)/shard_map/ppermute | solution.py:212
  178.4 12.8 %collective-permute-start.13 = (f32[4,32,512]{2,1,0:T(8,128)S(1)}, f32[4,32,512]{2,1,0:T(8,128)S(1)}, u32[]{:S(2)}, u32[]{:S(2)}) collective-permute-start(f32[4,32,512]{2,1,0:T(8,128)S(1)} %pad_maximum_fusion.1), channel_id=1, source_target_pairs={{0,192},{192,384},{384,576},{576,0},{1,193},{193,385},{385,577},{5... | collective-permute-start | bytes 786440 | tf_op jit(solution)/shard_map/ppermute | solution.py:212
  189.2 10.6 %collective-permute-start.15 = (f32[4,32,512]{2,1,0:T(8,128)S(1)}, f32[4,32,512]{2,1,0:T(8,128)S(1)}, u32[]{:S(2)}, u32[]{:S(2)}) collective-permute-start(f32[4,32,512]{2,1,0:T(8,128)S(1)} %collective-permute-done.14), channel_id=1, source_target_pairs={{0,576},{192,0},{384,192},{576,384},{1,577},{193,1},{385,193},{577... | collective-permute-start | bytes 786440 | tf_op jit(solution)/shard_map/ppermute | solution.py:212
  199.8 7.8 %copy-start.7 = (f32[4,128,512]{2,1,0:T(8,128)}, f32[4,128,512]{2,1,0:T(8,128)S(1)}, u32[]{:S(2)}) copy-start(f32[4,128,512]{2,1,0:T(8,128)S(1)} %constant_dynamic-update-slice_fusion.own_ref) | copy-start | bytes 3145732
  199.9 7.8 %collective-permute-start.16 = (f32[4,128,512]{2,1,0:T(8,128)S(1)}, f32[4,128,512]{2,1,0:T(8,128)}, u32[]{:S(2)}, u32[]{:S(2)}) collective-permute-start(f32[4,128,512]{2,1,0:T(8,128)S(1)} %constant_dynamic-update-slice_fusion.own_ref), channel_id=1, source_target_pairs={{0,1},{1,0},{2,3},{3,2},{4,5},{5,4},{6,7},{7,6},{8,9},{9,8},{10,11... | collective-permute-start | bytes 3145736 | tf_op jit(solution)/shard_map/ppermute | solution.py:173

commit v10 on v9

--- a/solution.py
+++ b/solution.py
@@ -248,7 +248,7 @@
     near, columns = tie(near, columns)
     columns = lax.all_to_all(columns, "zh", 0, 0, tiled=True)
     rows = dispatch(first, near, dense_weight, width, here, cap)
-    rows, near, columns = tie(rows, near, columns)
+    rows, near = tie(rows, near)
     got = lax.all_to_all(rows, ("y", "c"), 0, 0, tiled=True)
     lg = near.reshape(-1, near.shape[2])[:, : layer_grad.shape[1]]
     columns = columns.reshape(lg.shape[0], -1)

time: 215 us -> 215 us (level)
  no operation moved by 1% of the time
where the time goes in v10:
time: 215 us; the launch traced here: 211 us
  starting transfers between devices  83.3 us (39%)
  waiting for transfers between devices  52.9 us (25%)
  blocking collectives  33.5 us (16%)
  local copies, waits for them, and re-layouts  15 us (7%)
  Pallas kernels  11.9 us (6%)
  matrix products  8.04 us (4%)
  other arithmetic  5.37 us (2%)
    ppermute x11, starting transfers between devices, shift(): return lax.ppermute(a, axis, [(i, (i + k) % size) for i in range(size)])  39.9 us
    all_gather x1, blocking collectives, shards(): near = lax.all_gather(near, 'zh', axis=0, tiled=False)  33.5 us
    ppermute x11, waiting for transfers between devices, shift(): return lax.ppermute(a, axis, [(i, (i + k) % size) for i in range(size)])  24.1 us
    ppermute x6, waiting for transfers between devices, swap(): return lax.ppermute(a, axis, [(i, i ^ bit) for i in range(size)])  21.4 us
    ppermute x6, starting transfers between devices, swap(): return lax.ppermute(a, axis, [(i, i ^ bit) for i in range(size)])  16.8 us
    all_to_all x1, starting transfers between devices, shards(): got = lax.all_to_all(rows, ('y', 'c'), 0, 0, tiled=True)  12.5 us
    dot_general x1, matrix products, collect(): return jnp.dot(selector, got.reshape(-1, width), preferred_element_type=f32)  6.78 us
    pallas_call x1, Pallas kernels, dispatch(): pl.pallas_call(lambda *refs: dispatch_kernel(here, cap, *refs), out_shape...  6.31 us
  transfers between devices with their start and end apart: 21, of which 12 were waited for; matrix products, arithmetic and copies ran while one was open for 5% of the time, Pallas kernels for 3%

profile of v10, /device:TPU:1, one launch (start us, length us, event | category | flops | bytes accessed | tf_op | source)
XLA Modules:
  0.0 211.4 jit_solution(16551199016760120103)
XLA Ops:
  4.8 33.5 %all-gather = bf16[512,640]{1,0:T(8,128)(2,1)S(1)} all-gather(bf16[128,640]{1,0:T(8,128)(2,1)S(1)} %fusion.7), channel_id=2, replica_groups=mesh['x'=4,'zl'=3,'zh'=4,'y'=8,'c'=2] {'zh'}, dimensions={0}, use_global_device_ids=true | all-gather | bytes 819200 | tf_op jit(solution)/shard_map/all_gather | solution.py:246
  39.0 3.4 %all-to-all-start.1 = ((bf16[4,128,256]{2,1,0:T(8,128)(2,1)}), bf16[4,128,256]{2,1,0:T(8,128)(2,1)S(1)}, u32[]{:S(2)}, u32[]{:S(2)}) async-start(bf16[4,128,256]{2,1,0:T(8,128)(2,1)} %pad_maximum_fusion), calls=%async_computation.1 | async-start | bytes 524288 | tf_op jit(solution)/shard_map/all_to_all | solution.py:249
  43.7 6.3 %dispatch.1 = bf16[16,272,256]{2,1,0:T(8,128)(2,1)S(1)} custom-call(s32[1]{0:T(128)} %bitcast.1.refs_0_, bf16[4,128,640]{2,1,0:T(8,128)(2,1)S(1)} %bitcast.28, bf16[1024,512]{1,0:T(8,128)(2,1)S(1)} %copy-done.3), custom_call_target="tpu_custom_call" | custom-call | tf_op jit(solution)/shard_map/dispatch/pallas_call | solution.py:96
  51.4 3.2 %all-to-all-done.1 = bf16[4,128,256]{2,1,0:T(8,128)(2,1)S(1)} async-done(((bf16[4,128,256]{2,1,0:T(8,128)(2,1)}), bf16[4,128,256]{2,1,0:T(8,128)(2,1)S(1)}, u32[]{:S(2)}, u32[]{:S(2)}) %all-to-all-start.1) | async-done | bytes 262176 | tf_op jit(solution)/shard_map/all_to_all | solution.py:249
  55.3 12.5 %all-to-all-start = ((bf16[16,272,256]{2,1,0:T(8,128)(2,1)}), bf16[16,272,256]{2,1,0:T(8,128)(2,1)}, u32[]{:S(2)}, u32[]{:S(2)}) async-start(bf16[16,272,256]{2,1,0:T(8,128)(2,1)} %copy-done.1), calls=%async_computation | async-start | bytes 4456448 | tf_op jit(solution)/shard_map/all_to_all | solution.py:252
  72.7 3.1 %collective-permute-start.1 = (f32[32,512]{1,0:T(8,128)S(1)}, f32[32,512]{1,0:T(8,128)S(1)}, u32[]{:S(2)}, u32[]{:S(2)}) collective-permute-start(f32[32,512]{1,0:T(8,128)S(1)} %get-tuple-element.40), channel_id=1, source_target_pairs={{0,192},{192,384},{384,576},{576,0},{1,193},{193,385},{385,577},{5... | collective-permute-start | bytes 196616 | tf_op jit(solution)/shard_map/ppermute | solution.py:212
  75.8 3.4 %collective-permute-start.3 = (f32[32,512]{1,0:T(8,128)S(1)}, f32[32,512]{1,0:T(8,128)S(1)}, u32[]{:S(2)}, u32[]{:S(2)}) collective-permute-start(f32[32,512]{1,0:T(8,128)S(1)} %get-tuple-element.41), channel_id=1, source_target_pairs={{0,576},{192,0},{384,192},{576,384},{1,577},{193,1},{385,193},{577... | collective-permute-start | bytes 196616 | tf_op jit(solution)/shard_map/ppermute | solution.py:212
  79.2 3.4 %collective-permute-start.2 = (f32[32,512]{1,0:T(8,128)S(1)}, f32[32,512]{1,0:T(8,128)S(1)}, u32[]{:S(2)}, u32[]{:S(2)}) collective-permute-start(f32[32,512]{1,0:T(8,128)S(1)} %get-tuple-element.42), channel_id=1, source_target_pairs={{0,384},{192,576},{384,0},{576,192},{1,385},{193,577},{385,1},{577... | collective-permute-start | bytes 196616 | tf_op jit(solution)/shard_map/ppermute | solution.py:212
  86.1 3.2 %collective-permute-start.5 = (f32[32,512]{1,0:T(8,128)S(1)}, f32[32,512]{1,0:T(8,128)S(1)}, u32[]{:S(2)}, u32[]{:S(2)}) collective-permute-start(f32[32,512]{1,0:T(8,128)S(1)} %add_add_fusion), channel_id=1, source_target_pairs={{0,128},{64,0},{128,64},{1,129},{65,1},{129,65},{2,130},{66,2},{13... | collective-permute-start | bytes 196616 | tf_op jit(solution)/shard_map/ppermute | solution.py:212
  89.3 2.1 collective-permute-start.4
  92.8 2.8 %collective-permute-done.4 = f32[32,512]{1,0:T(8,128)S(1)} collective-permute-done((f32[32,512]{1,0:T(8,128)S(1)}, f32[32,512]{1,0:T(8,128)S(1)}, u32[]{:S(2)}, u32[]{:S(2)}) %collective-permute-start.4) | collective-permute-done | bytes 65568 | tf_op jit(solution)/shard_map/ppermute | solution.py:212
  95.7 4.5 %collective-permute-start.6 = (f32[1,32,512]{2,1,0:T(8,128)S(1)}, f32[1,32,512]{2,1,0:T(8,128)S(1)}, u32[]{:S(2)}, u32[]{:S(2)}) collective-permute-start(f32[1,32,512]{2,1,0:T(8,128)S(1)} %bitcast.32), channel_id=1, source_target_pairs={{0,16},{16,32},{32,48},{48,0},{1,17},{17,33},{33,49},{49,1},{2,18}... | collective-permute-start | bytes 196616 | tf_op jit(solution)/shard_map/ppermute | solution.py:212
  100.2 3.8 %collective-permute-start.8 = (f32[1,32,512]{2,1,0:T(8,128)S(1)}, f32[1,32,512]{2,1,0:T(8,128)S(1)}, u32[]{:S(2)}, u32[]{:S(2)}) collective-permute-start(f32[1,32,512]{2,1,0:T(8,128)S(1)} %bitcast.33), channel_id=1, source_target_pairs={{0,48},{16,0},{32,16},{48,32},{1,49},{17,1},{33,17},{49,33},{2,50}... | collective-permute-start | bytes 196616 | tf_op jit(solution)/shard_map/ppermute | solution.py:212
  104.0 7.7 %collective-permute-start.7 = (f32[1,32,512]{2,1,0:T(8,128)S(1)}, f32[1,32,512]{2,1,0:T(8,128)S(1)}, u32[]{:S(2)}, u32[]{:S(2)}) collective-permute-start(f32[1,32,512]{2,1,0:T(8,128)S(1)} %bitcast.34), channel_id=1, source_target_pairs={{0,32},{16,48},{32,0},{48,16},{1,33},{17,49},{33,1},{49,17},{2,34}... | collective-permute-start | bytes 196616 | tf_op jit(solution)/shard_map/ppermute | solution.py:212
  111.7 3.6 %collective-permute-done.7 = f32[1,32,512]{2,1,0:T(8,128)S(1)} collective-permute-done((f32[1,32,512]{2,1,0:T(8,128)S(1)}, f32[1,32,512]{2,1,0:T(8,128)S(1)}, u32[]{:S(2)}, u32[]{:S(2)}) %collective-permute-start.7) | collective-permute-done | bytes 65568 | tf_op jit(solution)/shard_map/ppermute | solution.py:212
  115.4 4.2 %all-to-all-done = bf16[16,272,256]{2,1,0:T(8,128)(2,1)} async-done(((bf16[16,272,256]{2,1,0:T(8,128)(2,1)}), bf16[16,272,256]{2,1,0:T(8,128)(2,1)}, u32[]{:S(2)}, u32[]{:S(2)}) %all-to-all-start) | async-done | bytes 2228256 | tf_op jit(solution)/shard_map/all_to_all | solution.py:252
  120.7 6.8 %fusion = f32[12,128,256]{2,1,0:T(8,128)} fusion(bf16[4352,256,1]{1,0,2:T(8,128)(2,1)} %bitcast.11, s32[4352]{0:T(1024)S(1)} %eq.65, s32[12,128]{1,0:T(8,128)S(1)} %multiply_add_fusion.1), kind=kOutput, calls=%fused_computation.4 | convolution fusion | flops 3429236736 | bytes 3824640 | tf_op jit(solution)/shard_map/dot_general | solution.py:113
  127.4 5.1 %all-to-all-start.2 = ((f32[12,128,256]{2,1,0:T(8,128)}), f32[12,128,256]{2,1,0:T(8,128)}, u32[]{:S(2)}, u32[]{:S(2)}) async-start(f32[12,128,256]{2,1,0:T(8,128)} %fusion), calls=%async_computation.2 | async-start | bytes 3145728 | tf_op jit(solution)/shard_map/all_to_all | solution.py:266
  134.5 4.3 %collective-permute-done.9 = f32[2,32,512]{2,1,0:T(8,128)S(1)} collective-permute-done((f32[2,32,512]{2,1,0:T(8,128)S(1)}, f32[2,32,512]{2,1,0:T(8,128)S(1)}, u32[]{:S(2)}, u32[]{:S(2)}) %collective-permute-start.9) | collective-permute-done | bytes 131104 | tf_op jit(solution)/shard_map/ppermute | solution.py:173
  138.8 4.2 %collective-permute-start.10 = (f32[2,32,512]{2,1,0:T(8,128)S(1)}, f32[2,32,512]{2,1,0:T(8,128)S(1)}, u32[]{:S(2)}, u32[]{:S(2)}) collective-permute-start(f32[2,32,512]{2,1,0:T(8,128)S(1)} %dynamic-slice_add_fusion.1), channel_id=1, source_target_pairs={{0,4},{2,6},{4,0},{6,2},{8,12},{10,14},{12,8},{14,10},{1,5},{3,7},... | collective-permute-start | bytes 393224 | tf_op jit(solution)/shard_map/ppermute | solution.py:173
  143.0 6.0 %collective-permute-done.10 = f32[2,32,512]{2,1,0:T(8,128)S(1)} collective-permute-done((f32[2,32,512]{2,1,0:T(8,128)S(1)}, f32[2,32,512]{2,1,0:T(8,128)S(1)}, u32[]{:S(2)}, u32[]{:S(2)}) %collective-permute-start.10) | collective-permute-done | bytes 131104 | tf_op jit(solution)/shard_map/ppermute | solution.py:173
  149.1 2.7 %collective-permute-start.11 = (f32[2,32,512]{2,1,0:T(8,128)S(1)}, f32[2,32,512]{2,1,0:T(8,128)S(1)}, u32[]{:S(2)}, u32[]{:S(2)}) collective-permute-start(f32[2,32,512]{2,1,0:T(8,128)S(1)} %add.191), channel_id=1, source_target_pairs={{0,8},{2,10},{4,12},{6,14},{8,0},{10,2},{12,4},{14,6},{1,9},{3,11}... | collective-permute-start | bytes 393224 | tf_op jit(solution)/shard_map/ppermute | solution.py:173
  151.9 7.2 %collective-permute-done.11 = f32[2,32,512]{2,1,0:T(8,128)S(1)} collective-permute-done((f32[2,32,512]{2,1,0:T(8,128)S(1)}, f32[2,32,512]{2,1,0:T(8,128)S(1)}, u32[]{:S(2)}, u32[]{:S(2)}) %collective-permute-start.11) | collective-permute-done | bytes 131104 | tf_op jit(solution)/shard_map/ppermute | solution.py:173
  162.2 5.6 %all-to-all-start.3 = ((f32[12,136,256]{2,1,0:T(8,128)}), f32[12,136,256]{2,1,0:T(8,128)}, u32[]{:S(2)}, u32[]{:S(2)}) async-start(f32[12,136,256]{2,1,0:T(8,128)} %copy-done.2), calls=%async_computation.3 | async-start | bytes 3342336 | tf_op jit(solution)/shard_map/all_to_all | solution.py:272
  167.7 2.4 %collective-permute-start.12 = (f32[2,32,512]{2,1,0:T(8,128)S(1)}, f32[2,32,512]{2,1,0:T(8,128)S(1)}, u32[]{:S(2)}, u32[]{:S(2)}) collective-permute-start(f32[2,32,512]{2,1,0:T(8,128)S(1)} %add.192), channel_id=1, source_target_pairs={{0,2},{2,0},{4,6},{6,4},{8,10},{10,8},{12,14},{14,12},{1,3},{3,1},... | collective-permute-start | bytes 393224 | tf_op jit(solution)/shard_map/ppermute | solution.py:173
  170.2 3.3 %collective-permute-done.12 = f32[2,32,512]{2,1,0:T(8,128)S(1)} collective-permute-done((f32[2,32,512]{2,1,0:T(8,128)S(1)}, f32[2,32,512]{2,1,0:T(8,128)S(1)}, u32[]{:S(2)}, u32[]{:S(2)}) %collective-permute-start.12) | collective-permute-done | bytes 131104 | tf_op jit(solution)/shard_map/ppermute | solution.py:173
  173.5 4.9 %collective-permute-start.14 = (f32[4,32,512]{2,1,0:T(8,128)S(1)}, f32[4,32,512]{2,1,0:T(8,128)S(1)}, u32[]{:S(2)}, u32[]{:S(2)}) collective-permute-start(f32[4,32,512]{2,1,0:T(8,128)S(1)} %pad_maximum_fusion.1), channel_id=1, source_target_pairs={{0,576},{192,0},{384,192},{576,384},{1,577},{193,1},{385,193},{577... | collective-permute-start | bytes 786440 | tf_op jit(solution)/shard_map/ppermute | solution.py:212
  180.3 8.8 %collective-permute-done.14 = f32[4,32,512]{2,1,0:T(8,128)S(1)} collective-permute-done((f32[4,32,512]{2,1,0:T(8,128)S(1)}, f32[4,32,512]{2,1,0:T(8,128)S(1)}, u32[]{:S(2)}, u32[]{:S(2)}) %collective-permute-start.14) | collective-permute-done | bytes 262176 | tf_op jit(solution)/shard_map/ppermute | solution.py:212
  191.3 8.5 %collective-permute-done.15 = f32[4,32,512]{2,1,0:T(8,128)S(1)} collective-permute-done((f32[4,32,512]{2,1,0:T(8,128)S(1)}, f32[4,32,512]{2,1,0:T(8,128)S(1)}, u32[]{:S(2)}, u32[]{:S(2)}) %collective-permute-start.15) | collective-permute-done | bytes 262176 | tf_op jit(solution)/shard_map/ppermute | solution.py:212
  199.9 3.5 %collective-permute-start.16 = (f32[4,128,512]{2,1,0:T(8,128)S(1)}, f32[4,128,512]{2,1,0:T(8,128)}, u32[]{:S(2)}, u32[]{:S(2)}) collective-permute-start(f32[4,128,512]{2,1,0:T(8,128)S(1)} %constant_dynamic-update-slice_fusion.own_ref), channel_id=1, source_target_pairs={{0,1},{1,0},{2,3},{3,2},{4,5},{5,4},{6,7},{7,6},{8,9},{9,8},{10,11... | collective-permute-start | bytes 3145736 | tf_op jit(solution)/shard_map/ppermute | solution.py:173
  203.4 2.7 %slice.37 = f32[12,128,256]{2,1,0:T(8,128)} slice(f32[12,136,256]{2,1,0:T(8,128)} %all-to-all-done.3), slice={[0:12], [0:128], [0:256]} | slice | bytes 3145728 | tf_op jit(solution)/shard_map/slice | solution.py:276
  207.6 3.8 %side_by_side.1 = f32[4,256,512]{2,1,0:T(8,128)} custom-call(s32[1]{0:T(128)} %bitcast.side_ref, f32[4,128,512]{2,1,0:T(8,128)} %copy-done.7, f32[4,128,512]{2,1,0:T(8,128)} %collective-permute-done.16.other_ref), custom_call_target="tpu_custom_call" | custom-call | tf_op jit(solution)/shard_map/side_by_side/pallas_call | solution.py:162
  (81 shorter events, 29.5 us)
Async XLA Ops:
  0.6 84.4 %copy-start = (bf16[4096,256]{1,0:T(8,128)(2,1)S(1)}, bf16[4096,256]{1,0:T(8,128)(2,1)}, u32[]{:S(2)}) copy-start(bf16[4096,256]{1,0:T(8,128)(2,1)} %param.16) | copy-start | bytes 6291460
  39.0 15.6 %all-to-all-start.1 = ((bf16[4,128,256]{2,1,0:T(8,128)(2,1)}), bf16[4,128,256]{2,1,0:T(8,128)(2,1)S(1)}, u32[]{:S(2)}, u32[]{:S(2)}) async-start(bf16[4,128,256]{2,1,0:T(8,128)(2,1)} %pad_maximum_fusion), calls=%async_computation.1 | async-start | bytes 524288 | tf_op jit(solution)/shard_map/all_to_all | solution.py:249
  42.4 1.2 copy-start.3
  50.0 1.4 copy-start.1
  54.6 0.7 copy-start.8
  55.3 64.3 %all-to-all-start = ((bf16[16,272,256]{2,1,0:T(8,128)(2,1)}), bf16[16,272,256]{2,1,0:T(8,128)(2,1)}, u32[]{:S(2)}, u32[]{:S(2)}) async-start(bf16[16,272,256]{2,1,0:T(8,128)(2,1)} %copy-done.1), calls=%async_computation | async-start | bytes 4456448 | tf_op jit(solution)/shard_map/all_to_all | solution.py:252
  67.8 14.8 %copy-start.4 = (f32[4096]{0:T(1024)S(1)}, f32[4096]{0:T(1024)}, u32[]{:S(2)}) copy-start(f32[4096]{0:T(1024)} %param.18) | copy-start | bytes 49156
  67.8 16.0 %copy-start.5 = (f32[4096]{0:T(1024)S(1)}, f32[4096]{0:T(1024)}, u32[]{:S(2)}) copy-start(f32[4096]{0:T(1024)} %param.17) | copy-start | bytes 49156
  69.1 22.5 %copy-start.6 = (f32[4096]{0:T(1024)S(1)}, f32[4096]{0:T(1024)}, u32[]{:S(2)}) copy-start(f32[4096]{0:T(1024)} %param.19) | copy-start | bytes 49156
  69.2 3.4 %collective-permute-start = (f32[128,512]{1,0:T(8,128)S(1)}, f32[128,512]{1,0:T(8,128)S(1)}, u32[]{:S(2)}, u32[]{:S(2)}) collective-permute-start(f32[128,512]{1,0:T(8,128)S(1)} %constant_dynamic-slice_fusion.4), channel_id=1, source_target_pairs={{0,1},{1,0},{2,3},{3,2},{4,5},{5,4},{6,7},{7,6},{8,9},{9,8},{10,11... | collective-permute-start | bytes 786440 | tf_op jit(solution)/shard_map/ppermute | solution.py:173
  72.7 13.2 %collective-permute-start.1 = (f32[32,512]{1,0:T(8,128)S(1)}, f32[32,512]{1,0:T(8,128)S(1)}, u32[]{:S(2)}, u32[]{:S(2)}) collective-permute-start(f32[32,512]{1,0:T(8,128)S(1)} %get-tuple-element.40), channel_id=1, source_target_pairs={{0,192},{192,384},{384,576},{576,0},{1,193},{193,385},{385,577},{5... | collective-permute-start | bytes 196616 | tf_op jit(solution)/shard_map/ppermute | solution.py:212
  75.8 10.1 %collective-permute-start.3 = (f32[32,512]{1,0:T(8,128)S(1)}, f32[32,512]{1,0:T(8,128)S(1)}, u32[]{:S(2)}, u32[]{:S(2)}) collective-permute-start(f32[32,512]{1,0:T(8,128)S(1)} %get-tuple-element.41), channel_id=1, source_target_pairs={{0,576},{192,0},{384,192},{576,384},{1,577},{193,1},{385,193},{577... | collective-permute-start | bytes 196616 | tf_op jit(solution)/shard_map/ppermute | solution.py:212
  79.2 6.9 %collective-permute-start.2 = (f32[32,512]{1,0:T(8,128)S(1)}, f32[32,512]{1,0:T(8,128)S(1)}, u32[]{:S(2)}, u32[]{:S(2)}) collective-permute-start(f32[32,512]{1,0:T(8,128)S(1)} %get-tuple-element.42), channel_id=1, source_target_pairs={{0,384},{192,576},{384,0},{576,192},{1,385},{193,577},{385,1},{577... | collective-permute-start | bytes 196616 | tf_op jit(solution)/shard_map/ppermute | solution.py:212
  86.1 6.7 %collective-permute-start.5 = (f32[32,512]{1,0:T(8,128)S(1)}, f32[32,512]{1,0:T(8,128)S(1)}, u32[]{:S(2)}, u32[]{:S(2)}) collective-permute-start(f32[32,512]{1,0:T(8,128)S(1)} %add_add_fusion), channel_id=1, source_target_pairs={{0,128},{64,0},{128,64},{1,129},{65,1},{129,65},{2,130},{66,2},{13... | collective-permute-start | bytes 196616 | tf_op jit(solution)/shard_map/ppermute | solution.py:212
  89.3 6.3 %collective-permute-start.4 = (f32[32,512]{1,0:T(8,128)S(1)}, f32[32,512]{1,0:T(8,128)S(1)}, u32[]{:S(2)}, u32[]{:S(2)}) collective-permute-start(f32[32,512]{1,0:T(8,128)S(1)} %add_add_fusion), channel_id=1, source_target_pairs={{0,64},{64,128},{128,0},{1,65},{65,129},{129,1},{2,66},{66,130},{1... | collective-permute-start | bytes 196616 | tf_op jit(solution)/shard_map/ppermute | solution.py:212
  95.7 16.0 %collective-permute-start.6 = (f32[1,32,512]{2,1,0:T(8,128)S(1)}, f32[1,32,512]{2,1,0:T(8,128)S(1)}, u32[]{:S(2)}, u32[]{:S(2)}) collective-permute-start(f32[1,32,512]{2,1,0:T(8,128)S(1)} %bitcast.32), channel_id=1, source_target_pairs={{0,16},{16,32},{32,48},{48,0},{1,17},{17,33},{33,49},{49,1},{2,18}... | collective-permute-start | bytes 196616 | tf_op jit(solution)/shard_map/ppermute | solution.py:212
  100.2 15.1 %collective-permute-start.8 = (f32[1,32,512]{2,1,0:T(8,128)S(1)}, f32[1,32,512]{2,1,0:T(8,128)S(1)}, u32[]{:S(2)}, u32[]{:S(2)}) collective-permute-start(f32[1,32,512]{2,1,0:T(8,128)S(1)} %bitcast.33), channel_id=1, source_target_pairs={{0,48},{16,0},{32,16},{48,32},{1,49},{17,1},{33,17},{49,33},{2,50}... | collective-permute-start | bytes 196616 | tf_op jit(solution)/shard_map/ppermute | solution.py:212
  104.0 11.4 %collective-permute-start.7 = (f32[1,32,512]{2,1,0:T(8,128)S(1)}, f32[1,32,512]{2,1,0:T(8,128)S(1)}, u32[]{:S(2)}, u32[]{:S(2)}) collective-permute-start(f32[1,32,512]{2,1,0:T(8,128)S(1)} %bitcast.34), channel_id=1, source_target_pairs={{0,32},{16,48},{32,0},{48,16},{1,33},{17,49},{33,1},{49,17},{2,34}... | collective-permute-start | bytes 196616 | tf_op jit(solution)/shard_map/ppermute | solution.py:212
  127.4 31.7 %all-to-all-start.2 = ((f32[12,128,256]{2,1,0:T(8,128)}), f32[12,128,256]{2,1,0:T(8,128)}, u32[]{:S(2)}, u32[]{:S(2)}) async-start(f32[12,128,256]{2,1,0:T(8,128)} %fusion), calls=%async_computation.2 | async-start | bytes 3145728 | tf_op jit(solution)/shard_map/all_to_all | solution.py:266
  132.5 6.3 %collective-permute-start.9 = (f32[2,32,512]{2,1,0:T(8,128)S(1)}, f32[2,32,512]{2,1,0:T(8,128)S(1)}, u32[]{:S(2)}, u32[]{:S(2)}) collective-permute-start(f32[2,32,512]{2,1,0:T(8,128)S(1)} %constant_dynamic-slice_fusion), channel_id=1, source_target_pairs={{0,2},{2,0},{4,6},{6,4},{8,10},{10,8},{12,14},{14,12},{1,3},{3,1},... | collective-permute-start | bytes 393224 | tf_op jit(solution)/shard_map/ppermute | solution.py:173
  138.8 10.2 %collective-permute-start.10 = (f32[2,32,512]{2,1,0:T(8,128)S(1)}, f32[2,32,512]{2,1,0:T(8,128)S(1)}, u32[]{:S(2)}, u32[]{:S(2)}) collective-permute-start(f32[2,32,512]{2,1,0:T(8,128)S(1)} %dynamic-slice_add_fusion.1), channel_id=1, source_target_pairs={{0,4},{2,6},{4,0},{6,2},{8,12},{10,14},{12,8},{14,10},{1,5},{3,7},... | collective-permute-start | bytes 393224 | tf_op jit(solution)/shard_map/ppermute | solution.py:173
  149.1 10.0 %collective-permute-start.11 = (f32[2,32,512]{2,1,0:T(8,128)S(1)}, f32[2,32,512]{2,1,0:T(8,128)S(1)}, u32[]{:S(2)}, u32[]{:S(2)}) collective-permute-start(f32[2,32,512]{2,1,0:T(8,128)S(1)} %add.191), channel_id=1, source_target_pairs={{0,8},{2,10},{4,12},{6,14},{8,0},{10,2},{12,4},{14,6},{1,9},{3,11}... | collective-permute-start | bytes 393224 | tf_op jit(solution)/shard_map/ppermute | solution.py:173
  161.0 1.2 copy-start.2
  162.2 41.3 %all-to-all-start.3 = ((f32[12,136,256]{2,1,0:T(8,128)}), f32[12,136,256]{2,1,0:T(8,128)}, u32[]{:S(2)}, u32[]{:S(2)}) async-start(f32[12,136,256]{2,1,0:T(8,128)} %copy-done.2), calls=%async_computation.3 | async-start | bytes 3342336 | tf_op jit(solution)/shard_map/all_to_all | solution.py:272
  167.7 5.7 %collective-permute-start.12 = (f32[2,32,512]{2,1,0:T(8,128)S(1)}, f32[2,32,512]{2,1,0:T(8,128)S(1)}, u32[]{:S(2)}, u32[]{:S(2)}) collective-permute-start(f32[2,32,512]{2,1,0:T(8,128)S(1)} %add.192), channel_id=1, source_target_pairs={{0,2},{2,0},{4,6},{6,4},{8,10},{10,8},{12,14},{14,12},{1,3},{3,1},... | collective-permute-start | bytes 393224 | tf_op jit(solution)/shard_map/ppermute | solution.py:173
  173.5 15.7 %collective-permute-start.14 = (f32[4,32,512]{2,1,0:T(8,128)S(1)}, f32[4,32,512]{2,1,0:T(8,128)S(1)}, u32[]{:S(2)}, u32[]{:S(2)}) collective-permute-start(f32[4,32,512]{2,1,0:T(8,128)S(1)} %pad_maximum_fusion.1), channel_id=1, source_target_pairs={{0,576},{192,0},{384,192},{576,384},{1,577},{193,1},{385,193},{577... | collective-permute-start | bytes 786440 | tf_op jit(solution)/shard_map/ppermute | solution.py:212
  178.4 12.8 %collective-permute-start.13 = (f32[4,32,512]{2,1,0:T(8,128)S(1)}, f32[4,32,512]{2,1,0:T(8,128)S(1)}, u32[]{:S(2)}, u32[]{:S(2)}) collective-permute-start(f32[4,32,512]{2,1,0:T(8,128)S(1)} %pad_maximum_fusion.1), channel_id=1, source_target_pairs={{0,192},{192,384},{384,576},{576,0},{1,193},{193,385},{385,577},{5... | collective-permute-start | bytes 786440 | tf_op jit(solution)/shard_map/ppermute | solution.py:212
  189.2 10.6 %collective-permute-start.15 = (f32[4,32,512]{2,1,0:T(8,128)S(1)}, f32[4,32,512]{2,1,0:T(8,128)S(1)}, u32[]{:S(2)}, u32[]{:S(2)}) collective-permute-start(f32[4,32,512]{2,1,0:T(8,128)S(1)} %collective-permute-done.14), channel_id=1, source_target_pairs={{0,576},{192,0},{384,192},{576,384},{1,577},{193,1},{385,193},{577... | collective-permute-start | bytes 786440 | tf_op jit(solution)/shard_map/ppermute | solution.py:212
  199.8 7.8 %copy-start.7 = (f32[4,128,512]{2,1,0:T(8,128)}, f32[4,128,512]{2,1,0:T(8,128)S(1)}, u32[]{:S(2)}) copy-start(f32[4,128,512]{2,1,0:T(8,128)S(1)} %constant_dynamic-update-slice_fusion.own_ref) | copy-start | bytes 3145732
  199.9 7.8 %collective-permute-start.16 = (f32[4,128,512]{2,1,0:T(8,128)S(1)}, f32[4,128,512]{2,1,0:T(8,128)}, u32[]{:S(2)}, u32[]{:S(2)}) collective-permute-start(f32[4,128,512]{2,1,0:T(8,128)S(1)} %constant_dynamic-update-slice_fusion.own_ref), channel_id=1, source_target_pairs={{0,1},{1,0},{2,3},{3,2},{4,5},{5,4},{6,7},{7,6},{8,9},{9,8},{10,11... | collective-permute-start | bytes 3145736 | tf_op jit(solution)/shard_map/ppermute | solution.py:173
